TPU v7x, 32 devices: a whole 2x2x4 slice. The times are simulated.
32 devices in a mesh: dp: 8 (over y, x, core), fsdp: 4 (over z).
Axes of the slice: x: 2, y: 2, z: 4, core: 2. Of those that a mesh axis runs over, the one named last changes fastest.
Arguments:
- frames: bfloat16 [49152, 512], P(('dp', 'fsdp'))
- seq_lengths: int32 [32, 3], P(('dp', 'fsdp')), may hold values from 512 to 1536, as said below
- seq_offsets: int32 [32, 3], P(('dp', 'fsdp')), may hold values from 0 to 1024, as said below
- seq_counts: int32 [32], P(('dp', 'fsdp')), may hold values from 1 to 3, as said below
- ffn_up: bfloat16 [2, 512, 2048], P(None, ('dp', 'fsdp')), may hold values from -0.25 to 0.25
- ffn_down: bfloat16 [2, 2048, 512], P(None, ('dp', 'fsdp')), may hold values from -0.125 to 0.125
- ffn_bias_up: bfloat16 [2, 2048], P(None, ('dp', 'fsdp')), may hold values from -3 to 3
- mix_in: bfloat16 [512, 1024], P(('dp', 'fsdp')), may hold values from -0.25 to 0.25
- mix_out: bfloat16 [512, 512], P(('dp', 'fsdp')), may hold values from -0.25 to 0.25
- conv_in: bfloat16 [512, 1024], P(('dp', 'fsdp')), may hold values from -0.25 to 0.25
- conv_out: bfloat16 [512, 512], P(('dp', 'fsdp')), may hold values from -0.25 to 0.25
- conv_out_bias: bfloat16 [512], P(('dp', 'fsdp')), may hold values from -3 to 3
- ssm_rate: bfloat16 [32, 512], P(None, ('dp', 'fsdp')), may hold values from -8 to -3
- ssm_map: bfloat16 [2, 32, 512], P(None, None, ('dp', 'fsdp')), may hold values from -4 to 4
- conv_kernel: bfloat16 [15, 512], P(None, ('dp', 'fsdp')), may hold values from -1.5 to 1.5
- gains: bfloat16 [6, 512], P(None, ('dp', 'fsdp')), may hold values from 0.099609375 to 1.8984375
- shifts: bfloat16 [12, 512], P(None, ('dp', 'fsdp')), may hold values from -3 to 3
- cotangent: bfloat16 [49152, 512], P(('dp', 'fsdp')), may hold values from -6 to 6
Outputs:
- output: bfloat16 [49152, 512], P(('dp', 'fsdp'))
- frames_grad: float32 [49152, 512], P(('dp', 'fsdp'))
- ffn_up_grad: float32 [2, 512, 2048], P(None, ('dp', 'fsdp'))
- ffn_down_grad: float32 [2, 2048, 512], P(None, ('dp', 'fsdp'))
- ffn_bias_up_grad: float32 [2, 2048], P(None, ('dp', 'fsdp'))
- mix_in_grad: float32 [512, 1024], P(('dp', 'fsdp'))
- mix_out_grad: float32 [512, 512], P(('dp', 'fsdp'))
- conv_in_grad: float32 [512, 1024], P(('dp', 'fsdp'))
- conv_out_grad: float32 [512, 512], P(('dp', 'fsdp'))
- conv_out_bias_grad: float32 [512], P(('dp', 'fsdp'))
- ssm_rate_grad: float32 [32, 512], P(None, ('dp', 'fsdp'))
- ssm_map_grad: float32 [2, 32, 512], P(None, None, ('dp', 'fsdp'))
- conv_kernel_grad: float32 [15, 512], P(None, ('dp', 'fsdp'))
- gains_grad: float32 [6, 512], P(None, ('dp', 'fsdp'))
- shifts_grad: float32 [12, 512], P(None, ('dp', 'fsdp'))
Inputs may be any that keep to these rules, and one draw needn't show every extreme that they name: `seq_lengths`: each device's lengths are multiples of 512, and those of its first seq_counts slots sum to 1536; slots at or past seq_counts repeat the last used slot. Some device holds one sequence of 1536 frames and some device three sequences. `seq_offsets`: each used slot's offset is the sum of the lengths of the device's earlier slots; slots at or past seq_counts repeat the last used slot. `seq_counts`: the number of used slots of each device.
All inputs are finite; a program needn't handle non-finite values.
Results may differ from a plain program's by a relative error of at most 0.013.
Values may be sent and summed in bfloat16 or wider, within the bound.
A program may use at most 320 MiB of HBM per device.

v0:
```python
import itertools
from functools import partial

import jax
import jax.numpy as jnp
from jax import lax
from jax.experimental import pallas as pl
from jax.experimental.pallas import tpu as pltpu
from jax.sharding import PartitionSpec as P

MESH = pl.DeviceIdType.MESH
BF16 = jnp.bfloat16
F32 = jnp.float32


def flip(index, bit):
    return index + bit * (1 - 2 * lax.rem(lax.div(index, bit), 2))


def flip_all(index, bits):
    for bit in bits:
        index = flip(index, bit)
    return index


def combos(bits):
    found = [()]
    for bit in bits:
        found = found + [entry + (bit,) for entry in found]
    return found


def plan_bits(n_dp):
    bits, bit = [], 2
    while bit < n_dp:
        bits.append(bit)
        bit *= 2
    return tuple(bits)


def greet(dp, fs, n_dp, n_fs):
    barrier = pltpu.get_barrier_semaphore()
    bits = (1,) + plan_bits(n_dp)
    for bit in bits:
        pl.semaphore_signal(barrier, inc=1, device_id=(flip(dp, bit), fs), device_id_type=MESH)
    for step in range(1, n_fs):
        pl.semaphore_signal(
            barrier, inc=1, device_id=(dp, lax.rem(fs + step, n_fs)), device_id_type=MESH
        )
    pl.semaphore_wait(barrier, len(bits) + n_fs - 1)


def gather_kernel(n_dp, n_fs, layers, *refs):
    n_in = len(layers)
    n_out = sum(layers)
    ins, outs = refs[:n_in], refs[n_in : n_in + n_out]
    send_sem, recv_sem, local_sem = refs[n_in + n_out :]
    sources = []
    for ref, count in zip(ins, layers):
        sources += [ref.at[layer] for layer in range(count)]
    dp, fs = lax.axis_index("dp"), lax.axis_index("fsdp")
    bits = plan_bits(n_dp)
    orders = (bits, bits[::-1])
    half = n_fs // 2
    greet(dp, fs, n_dp, n_fs)
    sends = []

    def remote(chunk, slot, src, dst, device):
        return pltpu.make_async_remote_copy(
            src_ref=src,
            dst_ref=dst,
            send_sem=send_sem.at[chunk, slot],
            recv_sem=recv_sem.at[chunk, slot],
            device_id=device,
            device_id_type=MESH,
        )

    def stages(chunk):
        src, out = sources[chunk], outs[chunk]
        mine = dp * n_fs + fs
        slots = itertools.count()

        def zone(where, part):
            if part is None:
                return out.at[pl.ds(where * n_fs, n_fs)]
            return out.at[pl.ds(where * n_fs + part * half, half)]

        steps = []
        z_slots = [next(slots) for _ in range(1, n_fs)]
        local = pltpu.make_async_copy(src, out.at[mine], local_sem.at[chunk])

        def start():
            local.start()
            for step in range(1, n_fs):
                to = (dp, lax.rem(fs + step, n_fs))
                copy = remote(chunk, z_slots[step - 1], src, out.at[mine], to)
                copy.start()
                sends.append(copy)

        steps.append(start)

        def wait_z():
            local.wait()
            for step in range(1, n_fs):
                origin = dp * n_fs + lax.rem(fs + n_fs - step, n_fs)
                remote(chunk, z_slots[step - 1], src, out.at[origin], (dp, fs)).wait_recv()

        waits = [wait_z]
        for depth in range(len(bits)):
            plan = []
            for part, order in enumerate(orders):
                for entry in combos(order[:depth]):
                    plan.append((next(slots), part, order[depth], entry))

            def go(plan=plan, before=tuple(waits)):
                for wait in before:
                    wait()
                for slot, part, bit, entry in plan:
                    view = zone(flip_all(dp, entry), part)
                    copy = remote(chunk, slot, view, view, (flip(dp, bit), fs))
                    copy.start()
                    sends.append(copy)

            def arrive(plan=plan):
                for slot, part, bit, entry in plan:
                    view = zone(flip_all(flip(dp, bit), entry), part)
                    remote(chunk, slot, view, view, (flip(dp, bit), fs)).wait_recv()

            steps.append(go)
            waits = [arrive]
        last = [(next(slots), entry) for entry in combos(bits)]

        def cross(before=tuple(waits)):
            for wait in before:
                wait()
            for slot, entry in last:
                view = zone(flip_all(dp, entry), None)
                copy = remote(chunk, slot, view, view, (flip(dp, 1), fs))
                copy.start()
                sends.append(copy)

        def finish():
            for slot, entry in last:
                view = zone(flip_all(flip(dp, 1), entry), None)
                remote(chunk, slot, view, view, (flip(dp, 1), fs)).wait_recv()

        steps += [cross, finish]
        return steps

    plans = [stages(chunk) for chunk in range(n_out)]
    depth = len(plans[0])
    for wave in range(n_out + depth - 1):
        for chunk in range(n_out):
            stage = wave - chunk
            if 0 <= stage < depth:
                plans[chunk][stage]()
    for copy in sends:
        copy.wait_send()


def slot_count(n_dp, n_fs):
    nb = len(plan_bits(n_dp))
    return n_fs - 1 + 2 * (2**nb - 1) + 2**nb


def gather_all(n_dp, n_fs, arrays, collective_id):
    layers = tuple(a.shape[0] for a in arrays)
    outs = []
    for a in arrays:
        outs += [jax.ShapeDtypeStruct((n_dp * n_fs,) + a.shape[1:], a.dtype)] * a.shape[0]
    count = slot_count(n_dp, n_fs)
    return pl.pallas_call(
        partial(gather_kernel, n_dp, n_fs, layers),
        out_shape=outs,
        in_specs=[pl.BlockSpec(memory_space=pltpu.HBM)] * len(arrays),
        out_specs=[pl.BlockSpec(memory_space=pltpu.HBM)] * len(outs),
        scratch_shapes=[
            pltpu.SemaphoreType.DMA((len(outs), count)),
            pltpu.SemaphoreType.DMA((len(outs), count)),
            pltpu.SemaphoreType.DMA((len(outs),)),
        ],
        compiler_params=pltpu.CompilerParams(collective_id=collective_id, has_side_effects=True),
        name="gather_parameters",
    )(*arrays)


def scatter_kernel(n_dp, n_fs, n_chunks, *refs):
    ins, outs = refs[:n_chunks], refs[n_chunks : 2 * n_chunks]
    per = 4
    scratch = refs[2 * n_chunks : 2 * n_chunks + per * n_chunks]
    send_sem, recv_sem, local_sem = refs[2 * n_chunks + per * n_chunks :]
    dp, fs = lax.axis_index("dp"), lax.axis_index("fsdp")
    bits = plan_bits(n_dp)
    nb = len(bits)
    orders = (bits[::-1], bits)
    half = n_fs // 2
    index = {entry: at for at, entry in enumerate(combos(bits))}
    greet(dp, fs, n_dp, n_fs)
    sends = []

    def remote(chunk, slot, src, dst, device):
        return pltpu.make_async_remote_copy(
            src_ref=src,
            dst_ref=dst,
            send_sem=send_sem.at[chunk, slot],
            recv_sem=recv_sem.at[chunk, slot],
            device_id=device,
            device_id_type=MESH,
        )

    def add_into(kept, other):
        count = kept.shape[0]

        def body(at, _):
            total = kept[at].astype(F32) + other[at].astype(F32)
            kept[at] = total.astype(BF16)
            return 0

        lax.fori_loop(0, count, body, 0)

    def stages(chunk):
        src, out = ins[chunk], outs[chunk]
        first, own, later, last = scratch[per * chunk : per * chunk + per]
        slots = itertools.count()
        pieces = [(next(slots), entry, index[entry]) for entry in combos(bits)]
        loads = [
            pltpu.make_async_copy(
                src.at[pl.ds(flip_all(dp, entry) * n_fs, n_fs)], own.at[at], local_sem.at[chunk, at]
            )
            for _, entry, at in pieces
        ]

        def start():
            for slot, entry, at in pieces:
                view = src.at[pl.ds(flip_all(flip(dp, 1), entry) * n_fs, n_fs)]
                copy = remote(chunk, slot, view, first.at[at], (flip(dp, 1), fs))
                copy.start()
                sends.append(copy)
            for load in loads:
                load.start()

        def fold_first():
            for load, (slot, entry, at) in zip(loads, pieces):
                load.wait()
                remote(chunk, slot, first.at[at], first.at[at], (flip(dp, 1), fs)).wait_recv()
                add_into(own.at[at], first.at[at])

        steps = [start]
        folds = [fold_first]
        used = 0
        for depth in range(nb):
            plan = []
            for part, order in enumerate(orders):
                bit, gone = order[depth], order[:depth]
                keep = [e for e in combos(bits) if not (set(e) & set(gone)) and bit not in e]
                for entry in keep:
                    away = tuple(sorted(entry + (bit,)))
                    plan.append((next(slots), part, bit, index[away], index[entry], used))
                    used += 1

            def go(plan=plan, before=tuple(folds)):
                for fold in before:
                    fold()
                for slot, part, bit, away, kept, place in plan:
                    copy = remote(
                        chunk,
                        slot,
                        own.at[away, pl.ds(part * half, half)],
                        later.at[place],
                        (flip(dp, bit), fs),
                    )
                    copy.start()
                    sends.append(copy)

            def fold(plan=plan):
                for slot, part, bit, away, kept, place in plan:
                    view = later.at[place]
                    remote(chunk, slot, view, view, (flip(dp, bit), fs)).wait_recv()
                    add_into(own.at[kept, pl.ds(part * half, half)], view)

            steps.append(go)
            folds = [fold]
        z_slots = [next(slots) for _ in range(1, n_fs)]

        def cross(before=tuple(folds)):
            for fold in before:
                fold()
            for step in range(1, n_fs):
                to = lax.rem(fs + step, n_fs)
                copy = remote(chunk, z_slots[step - 1], own.at[0, to], last.at[step - 1], (dp, to))
                copy.start()
                sends.append(copy)

        def finish():
            total = own[0, fs].astype(F32)
            for step in range(1, n_fs):
                view = last.at[step - 1]
                remote(chunk, z_slots[step - 1], view, view, (dp, fs)).wait_recv()
                total = total + last[step - 1].astype(F32)
            out[...] = total

        steps += [cross, finish]
        return steps

    plans = [stages(chunk) for chunk in range(n_chunks)]
    depth = len(plans[0])
    for wave in range(n_chunks + depth - 1):
        for chunk in range(n_chunks):
            stage = wave - chunk
            if 0 <= stage < depth:
                plans[chunk][stage]()
    for copy in sends:
        copy.wait_send()


def scatter_all(n_dp, n_fs, arrays, collective_id):
    nb = len(plan_bits(n_dp))
    pieces = 2**nb
    scratch = []
    for a in arrays:
        tail = a.shape[1:]
        scratch += [
            pltpu.VMEM((pieces, n_fs) + tail, BF16),
            pltpu.VMEM((pieces, n_fs) + tail, BF16),
            pltpu.VMEM((2 * (pieces - 1), n_fs // 2) + tail, BF16),
            pltpu.VMEM((n_fs - 1,) + tail, BF16),
        ]
    count = slot_count(n_dp, n_fs)
    n = len(arrays)
    return pl.pallas_call(
        partial(scatter_kernel, n_dp, n_fs, n),
        out_shape=[jax.ShapeDtypeStruct(a.shape[1:], F32) for a in arrays],
        in_specs=[pl.BlockSpec(memory_space=pltpu.HBM)] * n,
        out_specs=[pl.BlockSpec(memory_space=pltpu.VMEM)] * n,
        scratch_shapes=scratch
        + [
            pltpu.SemaphoreType.DMA((n, count)),
            pltpu.SemaphoreType.DMA((n, count)),
            pltpu.SemaphoreType.DMA((n, pieces)),
        ],
        compiler_params=pltpu.CompilerParams(
            collective_id=collective_id, has_side_effects=True, vmem_limit_bytes=48 << 20
        ),
        name="scatter_gradients",
    )(*arrays)


def exchange_kernel(n_dp, n_fs, x_ref, out_ref, octet, line, send_sem, recv_sem):
    dp, fs = lax.axis_index("dp"), lax.axis_index("fsdp")
    barrier = pltpu.get_barrier_semaphore()
    for step in range(1, n_dp):
        pl.semaphore_signal(
            barrier, inc=1, device_id=(lax.rem(dp + step, n_dp), fs), device_id_type=MESH
        )
    for step in range(1, n_fs):
        pl.semaphore_signal(
            barrier, inc=1, device_id=(dp, lax.rem(fs + step, n_fs)), device_id_type=MESH
        )
    pl.semaphore_wait(barrier, n_dp + n_fs - 2)
    sends = []
    octet[0] = x_ref[...]
    for step in range(1, n_dp):
        copy = pltpu.make_async_remote_copy(
            src_ref=octet.at[0],
            dst_ref=octet.at[step],
            send_sem=send_sem.at[step],
            recv_sem=recv_sem.at[step],
            device_id=(lax.rem(dp + step, n_dp), fs),
            device_id_type=MESH,
        )
        copy.start()
        sends.append(copy)
    for copy in sends:
        copy.wait_recv()
    total = octet[0]
    for step in range(1, n_dp):
        total = total + octet[step]
    line[0] = total
    more = []
    for step in range(1, n_fs):
        copy = pltpu.make_async_remote_copy(
            src_ref=line.at[0],
            dst_ref=line.at[step],
            send_sem=send_sem.at[n_dp + step],
            recv_sem=recv_sem.at[n_dp + step],
            device_id=(dp, lax.rem(fs + step, n_fs)),
            device_id_type=MESH,
        )
        copy.start()
        more.append(copy)
    for copy in more:
        copy.wait_recv()
    total = line[0]
    for step in range(1, n_fs):
        total = total + line[step]
    out_ref[...] = total
    for copy in sends + more:
        copy.wait_send()


def exchange(n_dp, n_fs, x, collective_id):
    return pl.pallas_call(
        partial(exchange_kernel, n_dp, n_fs),
        out_shape=jax.ShapeDtypeStruct(x.shape, F32),
        in_specs=[pl.BlockSpec(memory_space=pltpu.VMEM)],
        out_specs=pl.BlockSpec(memory_space=pltpu.VMEM),
        scratch_shapes=[
            pltpu.VMEM((n_dp,) + x.shape, F32),
            pltpu.VMEM((n_fs,) + x.shape, F32),
            pltpu.SemaphoreType.DMA((n_dp + n_fs,)),
            pltpu.SemaphoreType.DMA((n_dp + n_fs,)),
        ],
        compiler_params=pltpu.CompilerParams(collective_id=collective_id, has_side_effects=True),
        name="exchange_sums",
    )(x)


TILE = 512
STATES = 32
TAPS = 15
REACH = 8
EPSILON = 1e-05
CHUNK = 256
ROWS = 128
SPAN = 32
VMEM_LIMIT = 60 << 20


def sigmoid(v):
    return 0.5 * jnp.tanh(0.5 * v) + 0.5


def dot_nn(a, b):
    return jnp.dot(a, b, preferred_element_type=F32)


def dot_nt(a, b):
    return lax.dot_general(a, b, (((1,), (1,)), ((), ())), preferred_element_type=F32)


def dot_tn(a, b):
    return lax.dot_general(a, b, (((0,), (0,)), ((), ())), preferred_element_type=F32)


def norm_parts(v):
    centered = v - jnp.mean(v, axis=-1, keepdims=True)
    inv = lax.rsqrt(jnp.mean(centered * centered, axis=-1, keepdims=True) + EPSILON)
    return centered * inv, inv


def norm_back(grad, e, inv, gain):
    d = grad * gain
    return (
        d - jnp.mean(d, axis=-1, keepdims=True) - e * jnp.mean(d * e, axis=-1, keepdims=True)
    ) * inv


def fold8(v):
    return jnp.sum(v.reshape((v.shape[0] // 8, 8, v.shape[1])), axis=0)


def by_rows(body, rows=TILE, step=ROWS):
    def run(at, _):
        body(pl.ds(pl.multiple_of(at * step, step), step))
        return 0

    lax.fori_loop(0, rows // step, run, 0)


def columns(at, width=CHUNK):
    return pl.ds(pl.multiple_of(at * width, width), width)


def merge_rows(parts, low_half):
    for distance in (1, 2, 4):
        low = low_half[distance]
        parts = [
            jnp.where(low, a, b) + pltpu.roll(jnp.where(low, b, a), distance, 0)
            for a, b in zip(parts[0::2], parts[1::2])
        ]
    return parts[0]


def half_masks(width):
    row = lax.broadcasted_iota(jnp.int32, (8, width), 0)
    return {d: (row // d) % 2 == 0 for d in (4, 2, 1)}


def fold_states(v):
    return jnp.sum(v.reshape((STATES // 8, 8, v.shape[1])), axis=0)


def fill_halo(padded, flags_ref, tiles):
    pitch = TILE + 2 * REACH
    for at in range(tiles):
        base = at * pitch
        if at == 0:
            padded[:, base : base + REACH, :] = jnp.zeros_like(padded[:, base : base + REACH, :])
        if at == tiles - 1:
            end = base + REACH + TILE
            padded[:, end : end + REACH, :] = jnp.zeros_like(padded[:, end : end + REACH, :])
        else:
            keep = flags_ref[at + 1].astype(F32)
            end = base + REACH + TILE
            padded[:, end : end + REACH, :] = (
                padded[:, base + pitch + REACH : base + pitch + 2 * REACH, :] * keep
            )
            padded[:, base + pitch : base + pitch + REACH, :] = (
                padded[:, end - REACH : end, :] * keep
            )


def taps_over(padded, taps_ref, store, tiles, reverse, block=64):
    pitch = TILE + 2 * REACH
    per = TILE // block
    lanes = padded.shape[0]
    for lane in range(lanes):
        weights = [
            jnp.broadcast_to(taps_ref[k : k + 1, lane * 128 : lane * 128 + 128], (block, 128))
            for k in range(TAPS)
        ]

        def run(at, _):
            tile, inner = at // per, at % per
            base = tile * pitch + inner * block
            total = jnp.zeros((block, 128), F32)
            for k in range(TAPS):
                shift = REACH + (TAPS // 2 - k if reverse else k - TAPS // 2)
                total = total + weights[k] * padded[lane, pl.ds(base + shift, block), :]
            store(lane, tile * TILE + inner * block, base, total)
            return 0

        lax.fori_loop(0, tiles * per, run, 0)


def front_kernel(
    flags_ref,
    x_ref,
    up_ref,
    down_ref,
    mixin_ref,
    mixout_ref,
    convin_ref,
    bias_ref,
    vec_ref,
    taps_ref,
    decay_ref,
    map_ref,
    h_out,
    x1_out,
    u_out,
    v_out,
    y_out,
    gated_out,
    x2_out,
    p_out,
    hold_out,
    w_out,
    stat_out,
    low_scr,
    sum_scr,
    state_scr,
    padded,
):
    at = pl.program_id(0)
    tiles = pl.num_programs(0)
    channels = x_ref.shape[1]
    lanes = channels // 128
    gain = lambda k: vec_ref[k : k + 1, :]
    shift = lambda k: vec_ref[6 + k : 7 + k, :]

    def first(rows):
        e, _ = norm_parts(x_ref[rows, :].astype(F32))
        low_scr[rows, :] = (e * gain(0) + shift(0)).astype(BF16)
        sum_scr[rows, :] = jnp.zeros((ROWS, channels), F32)

    by_rows(first)

    def hidden(c, _):
        cols = columns(c)
        h = dot_nn(low_scr[...], up_ref[:, cols]) + bias_ref[0:1, cols]
        h_out[:, cols] = h.astype(BF16)
        active = (h * sigmoid(h)).astype(BF16)
        sum_scr[...] += dot_nn(active, down_ref[cols, :])
        return 0

    lax.fori_loop(0, up_ref.shape[1] // CHUNK, hidden, 0)

    def second(rows):
        x1 = x_ref[rows, :].astype(F32) + 0.5 * (sum_scr[rows, :] + shift(6))
        x1_out[rows, :] = x1
        e, _ = norm_parts(x1)
        low_scr[rows, :] = (e * gain(1) + shift(1)).astype(BF16)

    by_rows(second)

    def project(c, _):
        cols = columns(c)
        right = columns(c + channels // CHUNK)
        u_out[:, cols] = dot_nn(low_scr[...], mixin_ref[:, cols])
        v_out[:, cols] = dot_nn(low_scr[...], mixin_ref[:, right]).astype(BF16)
        return 0

    lax.fori_loop(0, channels // CHUNK, project, 0)

    low_half = half_masks(128)
    keep = flags_ref[at].astype(F32)

    @pl.when(at == 0)
    def _():
        state_scr[...] = jnp.zeros_like(state_scr)

    state_scr[...] = state_scr[...] * keep

    def scan_span(span, _):
        hold_out[span] = state_scr[...]

        def scan(step, _):
            start = pl.multiple_of(span * SPAN + step * 8, 8)
            for lane in range(lanes):
                cols = slice(lane * 128, lane * 128 + 128)
                state = state_scr[:, cols]
                decay = decay_ref[:, cols]
                maps = map_ref[:, cols]
                drive = u_out[pl.ds(start, 8), cols]
                parts = []
                for j in range(8):
                    state = decay * state + jnp.broadcast_to(drive[j : j + 1, :], (STATES, 128))
                    parts.append(fold_states(maps * state))
                state_scr[:, cols] = state
                sum_scr[pl.ds(start, 8), cols] = merge_rows(parts, low_half)
            return 0

        lax.fori_loop(0, SPAN // 8, scan, 0)
        return 0

    lax.fori_loop(0, TILE // SPAN, scan_span, 0)

    def gate(rows):
        y = sum_scr[rows, :] + shift(11) * u_out[rows, :]
        v = v_out[rows, :].astype(F32)
        y_out[rows, :] = y.astype(BF16)
        gated = (y * (v * sigmoid(v))).astype(BF16)
        gated_out[rows, :] = gated

    by_rows(gate)
    sum_scr[...] = dot_nn(gated_out[...], mixout_ref[...])

    def third(rows):
        x2 = x1_out[rows, :] + (sum_scr[rows, :] + shift(8))
        x2_out[rows, :] = x2
        e, _ = norm_parts(x2)
        low_scr[rows, :] = (e * gain(2) + shift(2)).astype(BF16)

    by_rows(third)
    pitch = TILE + 2 * REACH

    def widen(c, _):
        cols = columns(c)
        right = columns(c + channels // CHUNK)
        left_part = dot_nn(low_scr[...], convin_ref[:, cols]) + vec_ref[15:16, cols]
        right_part = dot_nn(low_scr[...], convin_ref[:, right]) + vec_ref[16:17, cols]
        p_out[:, cols] = left_part.astype(BF16)
        p_out[:, right] = right_part.astype(BF16)
        g = left_part * sigmoid(right_part)
        place = pl.ds(pl.multiple_of(at * pitch + REACH, 8), TILE)
        for k in range(CHUNK // 128):
            padded[c * (CHUNK // 128) + k, place, :] = g[:, k * 128 : k * 128 + 128]
        return 0

    lax.fori_loop(0, channels // CHUNK, widen, 0)

    @pl.when(at == tiles - 1)
    def _():
        count = w_out.shape[0] // TILE
        fill_halo(padded, flags_ref, count)

        def store(lane, row, base, total):
            w_out[pl.ds(pl.multiple_of(row, 64), 64), lane * 128 : lane * 128 + 128] = total

        taps_over(padded, taps_ref, store, count, False)
        stat_out[...] = jnp.zeros_like(stat_out)

        def total(at, _):
            rows = pl.ds(pl.multiple_of(at * ROWS, ROWS), ROWS)
            stat_out[0:8, :] += fold8(w_out[rows, :])
            return 0

        lax.fori_loop(0, w_out.shape[0] // ROWS, total, 0)
        center = jnp.sum(stat_out[0:8, :], axis=0, keepdims=True) * (1.0 / w_out.shape[0])

        def spread(at, _):
            rows = pl.ds(pl.multiple_of(at * ROWS, ROWS), ROWS)
            off = w_out[rows, :] - center
            stat_out[8:16, :] += fold8(off * off)
            return 0

        lax.fori_loop(0, w_out.shape[0] // ROWS, spread, 0)
        stat_out[0:8, :] = jnp.broadcast_to(center, (8, channels))
        stat_out[8:16, :] = jnp.broadcast_to(
            jnp.sum(stat_out[8:16, :], axis=0, keepdims=True), (8, channels)
        )


def whole(shape):
    zeros = (0,) * len(shape)
    return pl.BlockSpec(shape, lambda *_: zeros)


def params():
    return pltpu.CompilerParams(
        dimension_semantics=("arbitrary",), vmem_limit_bytes=VMEM_LIMIT
    )


def front(flags, x, up, down, mixin, mixout, convin, bias, vec, taps, decay, maps):
    frames, channels = x.shape
    hidden = up.shape[1]
    tiles = frames // TILE
    row = lambda width: pl.BlockSpec((TILE, width), lambda i, *_: (i, 0))
    shape = lambda width, kind: jax.ShapeDtypeStruct((frames, width), kind)
    spans = TILE // SPAN
    return pl.pallas_call(
        front_kernel,
        grid_spec=pltpu.PrefetchScalarGridSpec(
            num_scalar_prefetch=1,
            grid=(tiles,),
            in_specs=[row(channels)]
            + [whole(a.shape) for a in (up, down, mixin, mixout, convin, bias, vec, taps, decay, maps)],
            out_specs=[
                row(hidden),
                row(channels),
                row(channels),
                row(channels),
                row(channels),
                row(channels),
                row(channels),
                row(2 * channels),
                pl.BlockSpec((spans, STATES, channels), lambda i, *_: (i, 0, 0)),
                whole((frames, channels)),
                whole((16, channels)),
            ],
            scratch_shapes=[
                pltpu.VMEM((TILE, channels), BF16),
                pltpu.VMEM((TILE, channels), F32),
                pltpu.VMEM((STATES, channels), F32),
                pltpu.VMEM((channels // 128, tiles * (TILE + 2 * REACH), 128), F32),
            ],
        ),
        out_shape=[
            shape(hidden, BF16),
            shape(channels, F32),
            shape(channels, F32),
            shape(channels, BF16),
            shape(channels, BF16),
            shape(channels, BF16),
            shape(channels, F32),
            shape(2 * channels, BF16),
            jax.ShapeDtypeStruct((frames // SPAN, STATES, channels), F32),
            shape(channels, F32),
            jax.ShapeDtypeStruct((16, channels), F32),
        ],
        compiler_params=params(),
        name="front",
    )(flags, x, up, down, mixin, mixout, convin, bias, vec, taps, decay, maps)


def ffn_back(low_t, grad_t, grad_ref, h_load, up_ref, down_ref, up_acc, down_acc, bias_acc, back_scr, hidden):
    def chunk(c, _):
        cols = columns(c)
        h = h_load(cols)
        sig = sigmoid(h)
        active = h * sig
        gate = dot_nt(grad_ref[...], down_ref[cols, :])
        grad_h = (gate * (sig * (1.0 + h - active))).astype(BF16)
        bias_acc[:, cols] += fold8(grad_h.astype(F32))
        down_acc[cols, :] += dot_tn(active.astype(BF16), grad_ref[...])
        up_acc[:, cols] += dot_nn(low_t[...], grad_h)
        back_scr[...] += dot_nt(grad_h, up_ref[:, cols])
        return 0

    lax.fori_loop(0, hidden // CHUNK, chunk, 0)


def middle_kernel(
    x2_ref,
    w_ref,
    cot_ref,
    up_ref,
    down_ref,
    convout_ref,
    bias_ref,
    vec_ref,
    stat_ref,
    out_ref,
    gx3_ref,
    gnb_ref,
    gup_out,
    gdown_out,
    gconvout_out,
    gbias_out,
    gvec_out,
    up_acc,
    down_acc,
    convout_acc,
    bias_acc,
    vec_acc,
    h_scr,
    low_scr,
    turn_scr,
    act_scr,
    grad_scr,
    sum_scr,
    x3_scr,
):
    at = pl.program_id(0)
    tiles = pl.num_programs(0)
    channels = x2_ref.shape[1]
    hidden = up_ref.shape[1]
    gain = lambda k: vec_ref[k : k + 1, :]
    shift = lambda k: vec_ref[6 + k : 7 + k, :]
    center, scale = stat_ref[0:1, :], stat_ref[1:2, :]

    @pl.when(at == 0)
    def _():
        for ref in (up_acc, down_acc, convout_acc, bias_acc, vec_acc):
            ref[...] = jnp.zeros_like(ref)

    def normed(rows):
        e = (w_ref[rows, :] - center) * scale
        return e, e * gain(5) + shift(5)

    def first(rows):
        _, nb = normed(rows)
        act_scr[rows, :] = (nb * sigmoid(nb)).astype(BF16)

    by_rows(first)
    sum_scr[...] = dot_nn(act_scr[...], convout_ref[...])

    def second(rows):
        x3 = x2_ref[rows, :] + (sum_scr[rows, :] + vec_ref[18:19, :])
        x3_scr[rows, :] = x3
        e, _ = norm_parts(x3)
        low_scr[rows, :] = (e * gain(3) + shift(3)).astype(BF16)
        sum_scr[rows, :] = jnp.zeros((ROWS, channels), F32)

    by_rows(second)

    def forward(c, _):
        cols = columns(c)
        h = dot_nn(low_scr[...], up_ref[:, cols]) + bias_ref[1:2, cols]
        h_scr[:, cols] = h
        active = (h * sigmoid(h)).astype(BF16)
        sum_scr[...] += dot_nn(active, down_ref[cols, :])
        return 0

    lax.fori_loop(0, hidden // CHUNK, forward, 0)
    turn_scr[...] = low_scr[...].T

    def last(rows):
        x4 = x3_scr[rows, :] + 0.5 * (sum_scr[rows, :] + shift(7))
        e, inv = norm_parts(x4)
        out_ref[rows, :] = (e * gain(4) + shift(4)).astype(BF16)
        cot = cot_ref[rows, :].astype(F32)
        vec_acc[0] += fold8(cot * e)
        vec_acc[1] += fold8(cot)
        gx4 = norm_back(cot, e, inv, gain(4))
        gx3_ref[rows, :] = gx4
        low = (0.5 * gx4).astype(BF16)
        grad_scr[rows, :] = low
        vec_acc[2] += fold8(low.astype(F32))
        sum_scr[rows, :] = jnp.zeros((ROWS, channels), F32)

    by_rows(last)
    ffn_back(
        turn_scr,
        None,
        grad_scr,
        lambda cols: h_scr[:, cols],
        up_ref,
        down_ref,
        up_acc,
        down_acc,
        bias_acc,
        sum_scr,
        hidden,
    )

    def fourth(rows):
        e, inv = norm_parts(x3_scr[rows, :])
        grad = sum_scr[rows, :]
        vec_acc[3] += fold8(grad * e)
        vec_acc[4] += fold8(grad)
        gx3 = gx3_ref[rows, :] + norm_back(grad, e, inv, gain(3))
        gx3_ref[rows, :] = gx3
        low = gx3.astype(BF16)
        grad_scr[rows, :] = low
        vec_acc[5] += fold8(low.astype(F32))

    by_rows(fourth)
    convout_acc[...] += dot_tn(act_scr[...], grad_scr[...])
    sum_scr[...] = dot_nt(grad_scr[...], convout_ref[...])

    def fifth(rows):
        e, nb = normed(rows)
        sig = sigmoid(nb)
        gnb = sum_scr[rows, :] * (sig * (1.0 + nb * (1.0 - sig)))
        gnb_ref[rows, :] = gnb
        vec_acc[6] += fold8(gnb * e)
        vec_acc[7] += fold8(gnb)

    by_rows(fifth)

    @pl.when(at == tiles - 1)
    def _():
        by_rows(lambda rows: gup_out.__setitem__((rows, slice(None)), up_acc[rows, :].astype(BF16)), channels)
        by_rows(lambda rows: gdown_out.__setitem__((rows, slice(None)), down_acc[rows, :].astype(BF16)), hidden)
        by_rows(lambda rows: gconvout_out.__setitem__((rows, slice(None)), convout_acc[rows, :].astype(BF16)), channels)
        gbias_out[...] = jnp.broadcast_to(jnp.sum(bias_acc[...], axis=0, keepdims=True), gbias_out.shape)
        for k in range(8):
            gvec_out[k : k + 1, :] = jnp.sum(vec_acc[k], axis=0, keepdims=True)


def middle(x2, w, cot, up, down, convout, bias, vec, stat):
    frames, channels = x2.shape
    hidden = up.shape[1]
    tiles = frames // TILE
    row = lambda width: pl.BlockSpec((TILE, width), lambda i: (i, 0))
    big = lambda a: pltpu.VMEM(a.shape, F32)
    shapes = [
        jax.ShapeDtypeStruct((frames, channels), BF16),
        jax.ShapeDtypeStruct((frames, channels), F32),
        jax.ShapeDtypeStruct((frames, channels), F32),
        jax.ShapeDtypeStruct(up.shape, BF16),
        jax.ShapeDtypeStruct(down.shape, BF16),
        jax.ShapeDtypeStruct(convout.shape, BF16),
        jax.ShapeDtypeStruct((8, hidden), F32),
        jax.ShapeDtypeStruct((8, channels), F32),
    ]
    return pl.pallas_call(
        middle_kernel,
        grid=(tiles,),
        in_specs=[row(channels)] * 3
        + [whole(a.shape) for a in (up, down, convout, bias, vec, stat)],
        out_specs=[row(channels)] * 3 + [whole(s.shape) for s in shapes[3:]],
        out_shape=shapes,
        scratch_shapes=[
            big(up),
            big(down),
            big(convout),
            pltpu.VMEM((8, hidden), F32),
            pltpu.VMEM((8, 8, channels), F32),
            pltpu.VMEM((TILE, hidden), F32),
            pltpu.VMEM((TILE, channels), BF16),
            pltpu.VMEM((channels, TILE), BF16),
            pltpu.VMEM((TILE, channels), BF16),
            pltpu.VMEM((TILE, channels), BF16),
            pltpu.VMEM((TILE, channels), F32),
            pltpu.VMEM((TILE, channels), F32),
        ],
        compiler_params=params(),
        name="middle",
    )(x2, w, cot, up, down, convout, bias, vec, stat)


def conv_back_kernel(flags_ref, w_ref, gnb_ref, p_ref, taps_ref, vec_ref, stat_ref, gg_ref, gtaps_ref, padded, gpad):
    frames, channels = w_ref.shape
    tiles = frames // TILE
    pitch = TILE + 2 * REACH
    center, scale = stat_ref[0:1, :], stat_ref[1:2, :]
    plain, cross = stat_ref[2:3, :], stat_ref[3:4, :]

    for tile in range(tiles):

        def fill(at, _, tile=tile):
            rows = pl.ds(pl.multiple_of(tile * TILE + at * 64, 64), 64)
            place = pl.ds(pl.multiple_of(tile * pitch + REACH + at * 64, 8), 64)
            e = (w_ref[rows, :] - center) * scale
            d = gnb_ref[rows, :] * vec_ref[5:6, :]
            gw = scale * (d - plain - e * cross)
            g = p_ref[rows, :channels].astype(F32) * sigmoid(p_ref[rows, channels:].astype(F32))
            for lane in range(channels // 128):
                cols = slice(lane * 128, lane * 128 + 128)
                padded[lane, place, :] = gw[:, cols]
                gpad[lane, place, :] = g[:, cols]
            return 0

        lax.fori_loop(0, TILE // 64, fill, 0)
    fill_halo(padded, flags_ref, tiles)
    fill_halo(gpad, flags_ref, tiles)

    def store(lane, row, base, total):
        gg_ref[pl.ds(pl.multiple_of(row, 64), 64), lane * 128 : lane * 128 + 128] = total

    taps_over(padded, taps_ref, store, tiles, True)
    block = 64
    per = TILE // block
    for lane in range(channels // 128):

        def corr(at, sums, lane=lane):
            base = (at // per) * pitch + (at % per) * block
            here = padded[lane, pl.ds(pl.multiple_of(base + REACH, 8), block), :]
            return tuple(
                s + fold8(here * gpad[lane, pl.ds(base + REACH + k - TAPS // 2, block), :])
                for k, s in enumerate(sums)
            )

        sums = lax.fori_loop(0, tiles * per, corr, (jnp.zeros((8, 128), F32),) * TAPS)
        for k in range(TAPS):
            gtaps_ref[k : k + 1, lane * 128 : lane * 128 + 128] = jnp.sum(sums[k], axis=0, keepdims=True)


def conv_back(flags, w, gnb, p, taps, vec, stat):
    frames, channels = w.shape
    tiles = frames // TILE
    pad = pltpu.VMEM((channels // 128, tiles * (TILE + 2 * REACH), 128), F32)
    return pl.pallas_call(
        conv_back_kernel,
        in_specs=[pl.BlockSpec(memory_space=pltpu.SMEM)] + [pl.BlockSpec(memory_space=pltpu.VMEM)] * 6,
        out_specs=[pl.BlockSpec(memory_space=pltpu.VMEM)] * 2,
        out_shape=[
            jax.ShapeDtypeStruct((frames, channels), F32),
            jax.ShapeDtypeStruct((16, channels), F32),
        ],
        scratch_shapes=[pad, pad],
        compiler_params=pltpu.CompilerParams(vmem_limit_bytes=VMEM_LIMIT),
        name="conv_back",
    )(flags, w, gnb, p, taps, vec, stat)


def back_kernel(
    flags_ref,
    gg_ref,
    p_ref,
    x2_ref,
    gx3_ref,
    gated_ref,
    y_ref,
    v_ref,
    u_ref,
    x1_ref,
    hold_ref,
    convin_ref,
    mixout_ref,
    mixin_ref,
    vec_ref,
    decay_ref,
    map_ref,
    gx1_ref,
    gconvin_out,
    gmixout_out,
    gmixin_out,
    gvec_out,
    gmap_out,
    gdecay_out,
    convin_acc,
    mixout_acc,
    mixin_acc,
    vec_acc,
    map_acc,
    decay_acc,
    adj_scr,
    track,
    low_scr,
    wide_scr,
    sum_scr,
    gy_scr,
):
    step = pl.program_id(0)
    tiles = pl.num_programs(0)
    at = tiles - 1 - step
    channels = x2_ref.shape[1]
    lanes = channels // 128
    gain = lambda k: vec_ref[k : k + 1, :]
    shift = lambda k: vec_ref[6 + k : 7 + k, :]

    @pl.when(step == 0)
    def _():
        for ref in (convin_acc, mixout_acc, mixin_acc, vec_acc, map_acc, decay_acc, adj_scr):
            ref[...] = jnp.zeros_like(ref)

    left, right = slice(0, channels), slice(channels, 2 * channels)

    def first(rows):
        grad = gg_ref[rows, :]
        sig = sigmoid(p_ref[rows, right].astype(F32))
        gl = (grad * sig).astype(BF16)
        gr = (grad * p_ref[rows, left].astype(F32) * (sig * (1.0 - sig))).astype(BF16)
        wide_scr[rows, left] = gl
        wide_scr[rows, right] = gr
        vec_acc[0] += fold8(gl.astype(F32))
        vec_acc[1] += fold8(gr.astype(F32))
        e, _ = norm_parts(x2_ref[rows, :])
        low_scr[rows, :] = (e * gain(2) + shift(2)).astype(BF16)

    by_rows(first)
    turned = low_scr[...].T
    convin_acc[...] += dot_nn(turned, wide_scr[...])
    sum_scr[...] = dot_nt(wide_scr[...], convin_ref[...])

    def second(rows):
        e, inv = norm_parts(x2_ref[rows, :])
        grad = sum_scr[rows, :]
        vec_acc[2] += fold8(grad * e)
        vec_acc[3] += fold8(grad)
        gx2 = gx3_ref[rows, :] + norm_back(grad, e, inv, gain(2))
        gx1_ref[rows, :] = gx2
        low = gx2.astype(BF16)
        low_scr[rows, :] = low
        vec_acc[4] += fold8(low.astype(F32))

    by_rows(second)
    mixout_acc[...] += dot_tn(gated_ref[...], low_scr[...])
    sum_scr[...] = dot_nt(low_scr[...], mixout_ref[...])

    def third(rows):
        grad = sum_scr[rows, :]
        v = v_ref[rows, :].astype(F32)
        sig = sigmoid(v)
        swish = v * sig
        gy = grad * swish
        gy_scr[rows, :] = gy
        wide_scr[rows, right] = (
            grad * y_ref[rows, :].astype(F32) * (sig * (1.0 + v - swish))
        ).astype(BF16)
        vec_acc[5] += fold8(gy * u_ref[rows, :])

    by_rows(third)
    low_half = half_masks(128)
    later = jnp.minimum(at + 1, tiles - 1)
    adj_scr[...] = adj_scr[...] * flags_ref[later].astype(F32)

    def span_back(index, _):
        span = TILE // SPAN - 1 - index
        base = pl.multiple_of(span * SPAN, SPAN)
        for lane in range(lanes):
            cols = slice(lane * 128, lane * 128 + 128)
            decay = decay_ref[:, cols]

            def forward(block, state):
                drive = u_ref[pl.ds(pl.multiple_of(base + block * 8, 8), 8), cols]
                for j in range(8):
                    track[block * 8 + j, :, cols] = state
                    state = decay * state + jnp.broadcast_to(drive[j : j + 1, :], (STATES, 128))
                return state

            lax.fori_loop(0, SPAN // 8, forward, hold_ref[span, :, cols])

        def backward(index, _):
            block = SPAN // 8 - 1 - index
            start = pl.multiple_of(base + block * 8, 8)
            for lane in range(lanes):
                cols = slice(lane * 128, lane * 128 + 128)
                decay = decay_ref[:, cols]
                maps = map_ref[:, cols]
                adj = adj_scr[:, cols]
                drive = u_ref[pl.ds(start, 8), cols]
                grad = gy_scr[pl.ds(start, 8), cols]
                gmap = map_acc[:, cols]
                gdecay = decay_acc[:, cols]
                parts = [None] * 8
                for j in range(7, -1, -1):
                    adj = decay * adj + jnp.broadcast_to(grad[j : j + 1, :], (STATES, 128))
                    parts[j] = fold_states(maps * adj)
                    gmap = gmap + adj * jnp.broadcast_to(drive[j : j + 1, :], (STATES, 128))
                    gdecay = gdecay + adj * track[block * 8 + j, :, cols]
                adj_scr[:, cols] = adj
                map_acc[:, cols] = gmap
                decay_acc[:, cols] = gdecay
                sum_scr[pl.ds(start, 8), cols] = merge_rows(parts, low_half)
            return 0

        lax.fori_loop(0, SPAN // 8, backward, 0)
        return 0

    lax.fori_loop(0, TILE // SPAN, span_back, 0)

    def fourth(rows):
        gu = sum_scr[rows, :] + shift(11) * gy_scr[rows, :]
        wide_scr[rows, left] = gu.astype(BF16)
        e, _ = norm_parts(x1_ref[rows, :])
        low_scr[rows, :] = (e * gain(1) + shift(1)).astype(BF16)

    by_rows(fourth)
    turned = low_scr[...].T
    mixin_acc[...] += dot_nn(turned, wide_scr[...])
    sum_scr[...] = dot_nt(wide_scr[...], mixin_ref[...])

    def fifth(rows):
        e, inv = norm_parts(x1_ref[rows, :])
        grad = sum_scr[rows, :]
        vec_acc[6] += fold8(grad * e)
        vec_acc[7] += fold8(grad)
        gx1_ref[rows, :] = gx1_ref[rows, :] + norm_back(grad, e, inv, gain(1))

    by_rows(fifth)

    @pl.when(step == tiles - 1)
    def _():
        for out, acc in ((gconvin_out, convin_acc), (gmixout_out, mixout_acc), (gmixin_out, mixin_acc)):
            by_rows(
                lambda rows, out=out, acc=acc: out.__setitem__((rows, slice(None)), acc[rows, :].astype(BF16)),
                channels,
            )
        for k in range(8):
            gvec_out[k : k + 1, :] = jnp.sum(vec_acc[k], axis=0, keepdims=True)
        gmap_out[...] = map_acc[...]
        gdecay_out[...] = decay_acc[...] * map_ref[...]


def back(flags, gg, p, x2, gx3, gated, y, v, u, x1, hold, convin, mixout, mixin, vec, decay, maps):
    frames, channels = x2.shape
    tiles = frames // TILE
    row = lambda width: pl.BlockSpec((TILE, width), lambda i, *_: (tiles - 1 - i, 0))
    spans = TILE // SPAN
    big = lambda a: pltpu.VMEM(a.shape, F32)
    shapes = [
        jax.ShapeDtypeStruct((frames, channels), F32),
        jax.ShapeDtypeStruct(convin.shape, BF16),
        jax.ShapeDtypeStruct(mixout.shape, BF16),
        jax.ShapeDtypeStruct(mixin.shape, BF16),
        jax.ShapeDtypeStruct((8, channels), F32),
        jax.ShapeDtypeStruct((STATES, channels), F32),
        jax.ShapeDtypeStruct((STATES, channels), F32),
    ]
    return pl.pallas_call(
        back_kernel,
        grid_spec=pltpu.PrefetchScalarGridSpec(
            num_scalar_prefetch=1,
            grid=(tiles,),
            in_specs=[row(channels), row(2 * channels)]
            + [row(channels)] * 7
            + [pl.BlockSpec((spans, STATES, channels), lambda i, *_: (tiles - 1 - i, 0, 0))]
            + [whole(a.shape) for a in (convin, mixout, mixin, vec, decay, maps)],
            out_specs=[row(channels)] + [whole(s.shape) for s in shapes[1:]],
            scratch_shapes=[
                big(convin),
                big(mixout),
                big(mixin),
                pltpu.VMEM((8, 8, channels), F32),
                pltpu.VMEM((STATES, channels), F32),
                pltpu.VMEM((STATES, channels), F32),
                pltpu.VMEM((STATES, channels), F32),
                pltpu.VMEM((SPAN, STATES, channels), F32),
                pltpu.VMEM((TILE, channels), BF16),
                pltpu.VMEM((TILE, 2 * channels), BF16),
                pltpu.VMEM((TILE, channels), F32),
                pltpu.VMEM((TILE, channels), F32),
            ],
        ),
        out_shape=shapes,
        compiler_params=params(),
        name="back",
    )(flags, gg, p, x2, gx3, gated, y, v, u, x1, hold, convin, mixout, mixin, vec, decay, maps)


def tail_kernel(
    x_ref,
    h_ref,
    gx1_ref,
    up_ref,
    down_ref,
    vec_ref,
    gx_ref,
    gup_out,
    gdown_out,
    gbias_out,
    gvec_out,
    up_acc,
    down_acc,
    bias_acc,
    vec_acc,
    low_scr,
    turn_scr,
    grad_scr,
    sum_scr,
):
    at = pl.program_id(0)
    tiles = pl.num_programs(0)
    channels = x_ref.shape[1]
    hidden = up_ref.shape[1]

    @pl.when(at == 0)
    def _():
        for ref in (up_acc, down_acc, bias_acc, vec_acc):
            ref[...] = jnp.zeros_like(ref)

    def first(rows):
        e, _ = norm_parts(x_ref[rows, :].astype(F32))
        low_scr[rows, :] = (e * vec_ref[0:1, :] + vec_ref[6:7, :]).astype(BF16)
        low = (0.5 * gx1_ref[rows, :]).astype(BF16)
        grad_scr[rows, :] = low
        vec_acc[0] += fold8(low.astype(F32))
        sum_scr[rows, :] = jnp.zeros((ROWS, channels), F32)

    by_rows(first)
    turn_scr[...] = low_scr[...].T
    ffn_back(
        turn_scr,
        None,
        grad_scr,
        lambda cols: h_ref[:, cols].astype(F32),
        up_ref,
        down_ref,
        up_acc,
        down_acc,
        bias_acc,
        sum_scr,
        hidden,
    )

    def second(rows):
        e, inv = norm_parts(x_ref[rows, :].astype(F32))
        grad = sum_scr[rows, :]
        vec_acc[1] += fold8(grad * e)
        vec_acc[2] += fold8(grad)
        gx_ref[rows, :] = gx1_ref[rows, :] + norm_back(grad, e, inv, vec_ref[0:1, :])

    by_rows(second)

    @pl.when(at == tiles - 1)
    def _():
        by_rows(lambda rows: gup_out.__setitem__((rows, slice(None)), up_acc[rows, :].astype(BF16)), channels)
        by_rows(lambda rows: gdown_out.__setitem__((rows, slice(None)), down_acc[rows, :].astype(BF16)), hidden)
        gbias_out[...] = jnp.broadcast_to(jnp.sum(bias_acc[...], axis=0, keepdims=True), gbias_out.shape)
        for k in range(3):
            gvec_out[k : k + 1, :] = jnp.sum(vec_acc[k], axis=0, keepdims=True)


def tail(x, h, gx1, up, down, vec):
    frames, channels = x.shape
    hidden = up.shape[1]
    tiles = frames // TILE
    row = lambda width: pl.BlockSpec((TILE, width), lambda i: (i, 0))
    big = lambda a: pltpu.VMEM(a.shape, F32)
    shapes = [
        jax.ShapeDtypeStruct((frames, channels), F32),
        jax.ShapeDtypeStruct(up.shape, BF16),
        jax.ShapeDtypeStruct(down.shape, BF16),
        jax.ShapeDtypeStruct((8, hidden), F32),
        jax.ShapeDtypeStruct((8, channels), F32),
    ]
    return pl.pallas_call(
        tail_kernel,
        grid=(tiles,),
        in_specs=[row(channels), row(hidden), row(channels)]
        + [whole(a.shape) for a in (up, down, vec)],
        out_specs=[row(channels)] + [whole(s.shape) for s in shapes[1:]],
        out_shape=shapes,
        scratch_shapes=[
            big(up),
            big(down),
            pltpu.VMEM((8, hidden), F32),
            pltpu.VMEM((8, 8, channels), F32),
            pltpu.VMEM((TILE, channels), BF16),
            pltpu.VMEM((channels, TILE), BF16),
            pltpu.VMEM((TILE, channels), BF16),
            pltpu.VMEM((TILE, channels), F32),
        ],
        compiler_params=params(),
        name="tail",
    )(x, h, gx1, up, down, vec)


def pack_small(bias_up, conv_bias, rate, maps, taps, gains, shifts, devices=1):
    layers, hidden = bias_up.shape
    channels = conv_bias.shape[0]
    ratio = hidden // channels
    bias = bias_up.reshape((layers, devices, ratio, channels // devices))
    bias = bias.transpose((0, 2, 1, 3)).reshape((layers * ratio, channels))
    rows = jnp.concatenate(
        [bias, conv_bias[None], rate, maps.reshape((-1, channels)), taps, gains, shifts], axis=0
    )
    rows = jnp.pad(rows, ((0, 256 - rows.shape[0]), (0, 0)))
    return rows.T


def unpack_small(small, devices, layers=2, ratio=4, states=STATES, width=TAPS):
    rows = small.T
    channels = rows.shape[1]
    at = layers * ratio
    bias = rows[:at].reshape((layers, ratio, devices, channels // devices))
    bias = bias.transpose((0, 2, 1, 3)).reshape((layers, ratio * channels))
    out = [bias, rows[at]]
    at += 1
    for count in (states, 2 * states, width, 6, 12):
        out.append(rows[at : at + count])
        at += count
    out[3] = out[3].reshape((2, states, channels))
    return tuple(out)


def state_weights(log_rate, coupling):
    log_decay = -jnp.exp(log_rate)
    input_map = coupling[0] * jnp.sqrt(-jnp.expm1(2.0 * log_decay))
    return jnp.exp(log_decay), input_map * coupling[1]


def on_device(
    n_dp,
    n_fs,
    frames,
    seq_lengths,
    seq_offsets,
    seq_counts,
    ffn_up,
    ffn_down,
    ffn_bias_up,
    mix_in,
    mix_out,
    conv_in,
    conv_out,
    conv_out_bias,
    ssm_rate,
    ssm_map,
    conv_kernel,
    gains,
    shifts,
    cotangent,
):
    devices = n_dp * n_fs
    gathered = gather_all(
        n_dp,
        n_fs,
        [
            pack_small(ffn_bias_up, conv_out_bias, ssm_rate, ssm_map, conv_kernel, gains, shifts)[
                None
            ],
            ffn_up,
            ffn_down,
            mix_in[None],
            mix_out[None],
            conv_in[None],
            conv_out[None],
        ],
        1,
    )
    small, up0, up1, down0, down1, mixin, mixout, convin, convout = [
        g.reshape((-1, g.shape[-1])) for g in gathered
    ]
    bias, conv_bias, rate, maps, taps, gain_set, shift_set = unpack_small(
        small.astype(F32), devices
    )
    frames_dev, channels = frames.shape
    tiles = frames_dev // TILE
    slot = jnp.arange(seq_offsets.shape[1], dtype=jnp.int32)
    begins = (seq_offsets[0][None, :] == TILE * jnp.arange(tiles, dtype=jnp.int32)[:, None]) & (
        slot < seq_counts[0]
    )
    flags = 1 - jnp.max(begins.astype(jnp.int32), axis=1)
    vec = jnp.concatenate([gain_set, shift_set, conv_bias[None], jnp.zeros((5, channels), F32)])
    taps = jnp.pad(taps, ((0, 1), (0, 0)))
    (decay, coupling), weights_back = jax.vjp(state_weights, rate, maps)
    h0, x1, u, v, y, gated, x2, p, hold, w, stat = front(
        flags, frames, up0, down0, mixin, mixout, convin, bias, vec, taps, decay, coupling
    )
    count_all = float(frames_dev * devices)
    center = exchange(n_dp, n_fs, stat[0:1], 2) / devices
    shift_from = stat[0:1] - center
    spread = exchange(n_dp, n_fs, stat[8:9] + frames_dev * shift_from * shift_from, 3)
    scale = lax.rsqrt(spread / count_all + EPSILON)
    stat = jnp.concatenate([center, scale, jnp.zeros((6, channels), F32)])
    result, gx3, gnb, gup1, gdown1, gconvout, gbias1, gvec1 = middle(
        x2, w, cotangent, up1, down1, convout, bias, vec, stat
    )
    sums = exchange(n_dp, n_fs, gvec1[6:8], 4) * (gain_set[5:6] / count_all)
    stat = jnp.concatenate([center, scale, sums[1:2], sums[0:1], jnp.zeros((4, channels), F32)])
    gg, gtaps = conv_back(flags, w, gnb, p, taps, vec, stat)
    gx1, gconvin, gmixout, gmixin, gvec2, gmap, gdecay = back(
        flags, gg, p, x2, gx3, gated, y, v, u, x1, hold, convin, mixout, mixin, vec, decay, coupling
    )
    gx, gup0, gdown0, gbias0, gvec3 = tail(frames, h0, gx1, up0, down0, vec)
    rate_grad, map_grad = weights_back((gdecay, gmap))
    gain_grad = jnp.stack([gvec3[1], gvec2[6], gvec2[2], gvec1[3], gvec1[0], gvec1[6]])
    shift_grad = jnp.stack(
        [
            gvec3[2],
            gvec2[7],
            gvec2[3],
            gvec1[4],
            gvec1[1],
            gvec1[7],
            gvec3[0],
            gvec1[2],
            gvec2[4],
            gvec2[0],
            gvec2[1],
            gvec2[5],
        ]
    )
    small_grad = pack_small(
        jnp.concatenate([gbias0[:1], gbias1[:1]]),
        gvec1[5],
        rate_grad,
        map_grad,
        gtaps[:TAPS],
        gain_grad,
        shift_grad,
        devices,
    ).astype(BF16)
    reduced = scatter_all(
        n_dp,
        n_fs,
        [
            g.reshape((devices, g.shape[0] // devices, g.shape[1]))
            for g in (gup1, gdown1, gconvout, gconvin, gmixout, gmixin, gup0, gdown0, small_grad)
        ],
        5,
    )
    small = unpack_small(reduced[8], 1)
    return (
        result,
        gx,
        jnp.stack([reduced[6], reduced[0]]),
        jnp.stack([reduced[7], reduced[1]]),
        small[0],
        reduced[5],
        reduced[4],
        reduced[3],
        reduced[2],
    ) + small[1:]


def solution(mesh):
    both = ("dp", "fsdp")
    row, row1 = P(both, None), P(both)
    col, col3, mid = P(None, both), P(None, None, both), P(None, both, None)
    in_specs = (
        row,
        row,
        row,
        row1,
        mid,
        mid,
        col,
        row,
        row,
        row,
        row,
        row1,
        col,
        col3,
        col,
        col,
        col,
        row,
    )
    out_specs = (row, row, mid, mid, col, row, row, row, row, row1, col, col3, col, col, col)
    return jax.shard_map(
        partial(on_device, mesh.shape["dp"], mesh.shape["fsdp"]),
        mesh=mesh,
        in_specs=in_specs,
        out_specs=out_specs,
        check_vma=False,
    )
```

profile of v0, /device:TPU:0, one launch (start us, length us, event | category | flops | bytes accessed | tf_op | source)
XLA Modules:
  0.0 507.2 jit_solution(8925565576507208542)
XLA Ops:
  6.7 81.5 %gather_parameters.1 = (bf16[32,16,256]{2,1,0:T(8,128)(2,1)}, bf16[32,16,2048]{2,1,0:T(8,128)(2,1)}, bf16[32,16,2048]{2,1,0:T(8,128)(2,1)}, bf16[32,64,512]{2,1,...) custom-call(bf16[1,16,256]{2,1,0:T(8,128)(2,1)} %pad_bitcast_fusion., ...), custom_call_target="tpu_custom_call" | custom-call | tf_op jit(solution)/shard_map/gather_parameters/pallas_call | solution.py:172
  88.3 1.0 bitcast_convert_fusion
  94.0 64.4 %front.1 = (bf16[1536,2048]{1,0:T(8,128)(2,1)}, f32[1536,512]{1,0:T(8,128)}, f32[1536,512]{1,0:T(8,128)}, bf16[1536,512]{1,0:T(8,128)(2,1)}, bf16[1536,512]{1,0:...) custom-call(s32[3]{0:T(128)} %broadcast_subtract_fusion.flags_ref, ...), custom_call_target="tpu_custom_call" | custom-call | tf_op jit(solution)/shard_map/front/pallas_call | solution.py:723
  158.4 1.3 slice.162.x_ref
  159.7 12.8 %exchange_sums.3 = f32[1,512]{1,0:T(1,128)} custom-call(f32[1,512]{1,0:T(1,128)} %slice.162.x_ref), custom_call_target="tpu_custom_call" | custom-call | tf_op jit(solution)/shard_map/exchange_sums/pallas_call | solution.py:402
  172.4 1.3 broadcast_multiply_fusion.1
  173.8 10.0 %exchange_sums.4 = f32[1,512]{1,0:T(1,128)} custom-call(f32[1,512]{1,0:T(1,128)} %get-tuple-element.189.x_ref), custom_call_target="tpu_custom_call" | custom-call | tf_op jit(solution)/shard_map/exchange_sums/pallas_call | solution.py:402
  185.2 61.9 %middle.1 = (bf16[1536,512]{1,0:T(8,128)(2,1)}, f32[1536,512]{1,0:T(8,128)}, f32[1536,512]{1,0:T(8,128)}, bf16[512,2048]{1,0:T(8,128)(2,1)}, bf16[2048,512]{1,0:...) custom-call(f32[1536,512]{1,0:T(8,128)} %get-tuple-element.72.x2_ref, ...), custom_call_target="tpu_custom_call" | custom-call | tf_op jit(solution)/shard_map/middle/pallas_call | solution.py:940
  247.2 1.3 slice.164.x_ref
  248.5 10.0 %exchange_sums.5 = f32[2,512]{1,0:T(2,128)} custom-call(f32[2,512]{1,0:T(2,128)} %slice.164.x_ref), custom_call_target="tpu_custom_call" | custom-call | tf_op jit(solution)/shard_map/exchange_sums/pallas_call | solution.py:402
  259.8 16.5 %conv_back.1 = (f32[1536,512]{1,0:T(8,128)}, f32[16,512]{1,0:T(8,128)}) custom-call(s32[3]{0:T(128)} %broadcast_subtract_fusion.flags_ref, f32[1536,512]{1,0:T(8,128)} %get-tuple-element.73.w_ref, f32[1536,512]{1,0:T(8,128)} %get-tuple-element.80.gnb_ref, bf16[1536,1024]{1,0:T(8,128)(2,1)} %get-tuple-element.81.p_ref, f32[16,512]{1,0:T(8,128)} %pad.20.taps_ref, ...), custom_call_target="tpu_custom_call" | custom-call | tf_op jit(solution)/shard_map/conv_back/pallas_call | solution.py:1017
  276.2 86.9 %back.1 = (f32[1536,512]{1,0:T(8,128)}, bf16[512,1024]{1,0:T(8,128)(2,1)}, bf16[512,512]{1,0:T(8,128)(2,1)}, bf16[512,1024]{1,0:T(8,128)(2,1)}, f32[8,512]{1,0:T...) custom-call(s32[3]{0:T(128)} %broadcast_subtract_fusion.flags_ref, f32[1536,512]{1,0:T(8,128)} %get-tuple-element.83.gg_ref, ...), custom_call_target="tpu_custom_call" | custom-call | tf_op jit(solution)/shard_map/back/pallas_call | solution.py:1226
  363.1 1.0 multiply_bitcast_fusion.1
  365.0 34.5 %tail.1 = (f32[1536,512]{1,0:T(8,128)}, bf16[512,2048]{1,0:T(8,128)(2,1)}, bf16[2048,512]{1,0:T(8,128)(2,1)}, f32[8,2048]{1,0:T(8,128)}, f32[8,512]{1,0:T(8,128)}) custom-call(bf16[1536,512]{1,0:T(8,128)(2,1)} %x_ref.3, bf16[1536,2048]{1,0:T(8,128)(2,1)} %get-tuple-element.79.h_ref, f32[1536,512]{1,0:T(8,128)} %get-tuple-element.91.gx1_ref, ...), custom_call_target="tpu_custom_call" | custom-call | tf_op jit(solution)/shard_map/tail/pallas_call | solution.py:1343
  399.6 0.9 slice.270
  400.4 0.8 slice.269
  403.1 0.8 copy.117
  403.9 0.8 copy.123
  404.7 0.8 copy.129
  405.6 0.8 copy.118
  406.4 0.8 copy.119
  407.2 0.8 copy.124
  408.8 0.8 copy.131
  409.6 0.8 copy.133
  410.4 0.8 copy.132
  412.1 0.8 copy.113
  412.9 0.8 copy.120
  413.7 0.8 copy.121
  415.3 0.8 copy.126
  416.1 0.8 copy.127
  418.5 3.0 concatenate.26
  421.6 76.6 %scatter_gradients.1 = (f32[16,2048]{1,0:T(8,128)S(1)}, f32[64,512]{1,0:T(8,128)S(1)}, f32[16,512]{1,0:T(8,128)S(1)}, f32[16,1024]{1,0:T(8,128)S(1)}, f32[16,512...) custom-call(bf16[32,16,2048]{2,1,0:T(8,128)(2,1)} %bitcast.80, ...), custom_call_target="tpu_custom_call" | custom-call | tf_op jit(solution)/shard_map/scatter_gradients/pallas_call | solution.py:330
  (93 shorter events, 28.6 us)
Async XLA Ops:
  0.6 92.6 %copy-start.7 = (s32[1,3]{1,0:T(1,128)S(1)}, s32[1,3]{1,0:T(1,128)}, u32[]{:S(2)}) copy-start(s32[1,3]{1,0:T(1,128)} %param.19) | copy-start | bytes 40
  365.0 40.5 %copy-start.5 = (f32[8,512]{1,0:T(8,128)S(1)}, f32[8,512]{1,0:T(8,128)}, u32[]{:S(2)}) copy-start(f32[8,512]{1,0:T(8,128)} %get-tuple-element.107) | copy-start | bytes 49156
  365.0 46.2 %copy-start.6 = (f32[16,512]{1,0:T(8,128)S(1)}, f32[16,512]{1,0:T(8,128)}, u32[]{:S(2)}) copy-start(f32[16,512]{1,0:T(8,128)} %get-tuple-element.105) | copy-start | bytes 98308
  399.6 12.5 %copy-start.4 = (f32[8,512]{1,0:T(8,128)S(1)}, f32[8,512]{1,0:T(8,128)}, u32[]{:S(2)}) copy-start(f32[8,512]{1,0:T(8,128)} %get-tuple-element.82) | copy-start | bytes 49156
  415.3 6.3 %copy-start = (bf16[512,1024]{1,0:T(8,128)(2,1)S(1)}, bf16[512,1024]{1,0:T(8,128)(2,1)}, u32[]{:S(2)}) copy-start(bf16[512,1024]{1,0:T(8,128)(2,1)} %get-tuple-element.96) | copy-start | bytes 3145732
  415.3 6.3 %copy-start.1 = (bf16[512,1024]{1,0:T(8,128)(2,1)S(1)}, bf16[512,1024]{1,0:T(8,128)(2,1)}, u32[]{:S(2)}) copy-start(bf16[512,1024]{1,0:T(8,128)(2,1)} %get-tuple-element.98) | copy-start | bytes 3145732
  415.3 6.3 %copy-start.2 = (bf16[512,512]{1,0:T(8,128)(2,1)S(1)}, bf16[512,512]{1,0:T(8,128)(2,1)}, u32[]{:S(2)}) copy-start(bf16[512,512]{1,0:T(8,128)(2,1)} %get-tuple-element.95) | copy-start | bytes 1572868
  415.3 6.3 %copy-start.3 = (bf16[512,512]{1,0:T(8,128)(2,1)S(1)}, bf16[512,512]{1,0:T(8,128)(2,1)}, u32[]{:S(2)}) copy-start(bf16[512,512]{1,0:T(8,128)(2,1)} %get-tuple-element.97) | copy-start | bytes 1572868
where the time goes:
time: 508 us; the launch traced here: 507 us
  Pallas kernels  455 us (90%)
  local copies, waits for them, and re-layouts  40.9 us (8%)
  other arithmetic  9.66 us (2%)
    pallas_call x1, Pallas kernels, back(): pl.pallas_call(back_kernel, grid_spec=pltpu.PrefetchScalarGridSpec(num_sc...  86.9 us
    pallas_call x1, Pallas kernels, gather_all(): pl.pallas_call(partial(gather_kernel, n_dp, n_fs, layers), out_shape=outs...  81.5 us
    pallas_call x1, Pallas kernels, scatter_all(): pl.pallas_call(partial(scatter_kernel, n_dp, n_fs, n), out_shape=[jax.Sha...  76.6 us
    pallas_call x1, Pallas kernels, front(): pl.pallas_call(front_kernel, grid_spec=pltpu.PrefetchScalarGridSpec(num_s...  64.4 us
    pallas_call x1, Pallas kernels, middle(): pl.pallas_call(middle_kernel, grid=(tiles,), in_specs=[row(channels)] * 3...  61.9 us
    pallas_call x1, Pallas kernels, tail(): pl.pallas_call(tail_kernel, grid=(tiles,), in_specs=[row(channels), row(h...  34.5 us
    pallas_call x3, Pallas kernels, exchange(): pl.pallas_call(partial(exchange_kernel, n_dp, n_fs), out_shape=jax.ShapeD...  32.7 us
    pallas_call x1, Pallas kernels, conv_back(): pl.pallas_call(conv_back_kernel, in_specs=[pl.BlockSpec(memory_space=pltp...  16.5 us

commit v1 on v0

--- a/solution.py
+++ b/solution.py
@@ -40,14 +40,119 @@
 
 def greet(dp, fs, n_dp, n_fs):
     barrier = pltpu.get_barrier_semaphore()
-    bits = (1,) + plan_bits(n_dp)
-    for bit in bits:
-        pl.semaphore_signal(barrier, inc=1, device_id=(flip(dp, bit), fs), device_id_type=MESH)
+    for step in range(1, n_dp):
+        pl.semaphore_signal(
+            barrier, inc=1, device_id=(lax.rem(dp + step, n_dp), fs), device_id_type=MESH
+        )
     for step in range(1, n_fs):
         pl.semaphore_signal(
             barrier, inc=1, device_id=(dp, lax.rem(fs + step, n_fs)), device_id_type=MESH
         )
-    pl.semaphore_wait(barrier, len(bits) + n_fs - 1)
+    pl.semaphore_wait(barrier, n_dp + n_fs - 2)
+
+
+def gather_plan(dp, fs, n_dp, n_fs, sources, outs, send_sem, recv_sem, local_sem):
+    bits = plan_bits(n_dp)
+    orders = (bits, bits[::-1])
+    half = n_fs // 2
+    sends = []
+
+    def stages(chunk):
+        src, out = sources[chunk], outs[chunk]
+        slots = itertools.count()
+
+        def zone(where, part):
+            if part is None:
+                return out.at[pl.ds(where * n_fs, n_fs)]
+            return out.at[pl.ds(where * n_fs + part * half, half)]
+
+        def remote(slot, view_from, view_to, device):
+            return pltpu.make_async_remote_copy(
+                src_ref=view_from,
+                dst_ref=view_to,
+                send_sem=send_sem.at[chunk, slot],
+                recv_sem=recv_sem.at[chunk, slot],
+                device_id=device,
+                device_id_type=MESH,
+            )
+
+        def launch(make):
+            make().start()
+            sends.append(lambda: make().wait_send())
+
+        z_slots = [next(slots) for _ in range(1, n_fs)]
+
+        def own_copy():
+            return pltpu.make_async_copy(src, out.at[dp * n_fs + fs], local_sem.at[chunk])
+
+        def start():
+            own_copy().start()
+            for step in range(1, n_fs):
+                launch(
+                    lambda step=step: remote(
+                        z_slots[step - 1],
+                        src,
+                        out.at[dp * n_fs + fs],
+                        (dp, lax.rem(fs + step, n_fs)),
+                    )
+                )
+
+        def wait_z():
+            own_copy().wait()
+            for step in range(1, n_fs):
+                origin = dp * n_fs + lax.rem(fs + n_fs - step, n_fs)
+                remote(z_slots[step - 1], src, out.at[origin], (dp, fs)).wait_recv()
+
+        steps, before = [start], wait_z
+        for depth in range(len(bits)):
+            plan = []
+            for part, order in enumerate(orders):
+                for entry in combos(order[:depth]):
+                    plan.append((next(slots), part, order[depth], entry))
+
+            def view(slot, part, bit, entry, arrived):
+                where = flip_all(flip(dp, bit) if arrived else dp, entry)
+                return remote(slot, zone(where, part), zone(where, part), (flip(dp, bit), fs))
+
+            def go(plan=plan, before=before, view=view):
+                before()
+                for item in plan:
+                    launch(lambda item=item: view(*item, False))
+
+            def arrive(plan=plan, view=view):
+                for item in plan:
+                    view(*item, True).wait_recv()
+
+            steps.append(go)
+            before = arrive
+        last = [(next(slots), entry) for entry in combos(bits)]
+
+        def across(slot, entry, arrived):
+            where = flip_all(flip(dp, 1) if arrived else dp, entry)
+            return remote(slot, zone(where, None), zone(where, None), (flip(dp, 1), fs))
+
+        def cross(before=before):
+            before()
+            for item in last:
+                launch(lambda item=item: across(*item, False))
+
+        def finish():
+            for item in last:
+                across(*item, True).wait_recv()
+
+        return steps + [cross, finish]
+
+    return [stages(chunk) for chunk in range(len(outs))], sends
+
+
+def waves(plans):
+    depth = len(plans[0])
+    out = []
+    for wave in range(len(plans) + depth - 1):
+        out.append(
+            [plans[c][wave - c] for c in range(len(plans)) if 0 <= wave - c < depth]
+        )
+    return out
 
 
 def gather_kernel(n_dp, n_fs, layers, *refs):
@@ -59,103 +164,13 @@
     for ref, count in zip(ins, layers):
         sources += [ref.at[layer] for layer in range(count)]
     dp, fs = lax.axis_index("dp"), lax.axis_index("fsdp")
-    bits = plan_bits(n_dp)
-    orders = (bits, bits[::-1])
-    half = n_fs // 2
     greet(dp, fs, n_dp, n_fs)
-    sends = []
-
-    def remote(chunk, slot, src, dst, device):
-        return pltpu.make_async_remote_copy(
-            src_ref=src,
-            dst_ref=dst,
-            send_sem=send_sem.at[chunk, slot],
-            recv_sem=recv_sem.at[chunk, slot],
-            device_id=device,
-            device_id_type=MESH,
-        )
-
-    def stages(chunk):
-        src, out = sources[chunk], outs[chunk]
-        mine = dp * n_fs + fs
-        slots = itertools.count()
-
-        def zone(where, part):
-            if part is None:
-                return out.at[pl.ds(where * n_fs, n_fs)]
-            return out.at[pl.ds(where * n_fs + part * half, half)]
-
-        steps = []
-        z_slots = [next(slots) for _ in range(1, n_fs)]
-        local = pltpu.make_async_copy(src, out.at[mine], local_sem.at[chunk])
-
-        def start():
-            local.start()
-            for step in range(1, n_fs):
-                to = (dp, lax.rem(fs + step, n_fs))
-                copy = remote(chunk, z_slots[step - 1], src, out.at[mine], to)
-                copy.start()
-                sends.append(copy)
-
-        steps.append(start)
-
-        def wait_z():
-            local.wait()
-            for step in range(1, n_fs):
-                origin = dp * n_fs + lax.rem(fs + n_fs - step, n_fs)
-                remote(chunk, z_slots[step - 1], src, out.at[origin], (dp, fs)).wait_recv()
-
-        waits = [wait_z]
-        for depth in range(len(bits)):
-            plan = []
-            for part, order in enumerate(orders):
-                for entry in combos(order[:depth]):
-                    plan.append((next(slots), part, order[depth], entry))
-
-            def go(plan=plan, before=tuple(waits)):
-                for wait in before:
-                    wait()
-                for slot, part, bit, entry in plan:
-                    view = zone(flip_all(dp, entry), part)
-                    copy = remote(chunk, slot, view, view, (flip(dp, bit), fs))
-                    copy.start()
-                    sends.append(copy)
-
-            def arrive(plan=plan):
-                for slot, part, bit, entry in plan:
-                    view = zone(flip_all(flip(dp, bit), entry), part)
-                    remote(chunk, slot, view, view, (flip(dp, bit), fs)).wait_recv()
-
-            steps.append(go)
-            waits = [arrive]
-        last = [(next(slots), entry) for entry in combos(bits)]
-
-        def cross(before=tuple(waits)):
-            for wait in before:
-                wait()
-            for slot, entry in last:
-                view = zone(flip_all(dp, entry), None)
-                copy = remote(chunk, slot, view, view, (flip(dp, 1), fs))
-                copy.start()
-                sends.append(copy)
-
-        def finish():
-            for slot, entry in last:
-                view = zone(flip_all(flip(dp, 1), entry), None)
-                remote(chunk, slot, view, view, (flip(dp, 1), fs)).wait_recv()
-
-        steps += [cross, finish]
-        return steps
-
-    plans = [stages(chunk) for chunk in range(n_out)]
-    depth = len(plans[0])
-    for wave in range(n_out + depth - 1):
-        for chunk in range(n_out):
-            stage = wave - chunk
-            if 0 <= stage < depth:
-                plans[chunk][stage]()
-    for copy in sends:
-        copy.wait_send()
+    plans, sends = gather_plan(dp, fs, n_dp, n_fs, sources, outs, send_sem, recv_sem, local_sem)
+    for wave in waves(plans):
+        for stage in wave:
+            stage()
+    for wait in sends:
+        wait()
 
 
 def slot_count(n_dp, n_fs):
@@ -184,160 +199,168 @@
     )(*arrays)
 
 
-def scatter_kernel(n_dp, n_fs, n_chunks, *refs):
-    ins, outs = refs[:n_chunks], refs[n_chunks : 2 * n_chunks]
-    per = 4
-    scratch = refs[2 * n_chunks : 2 * n_chunks + per * n_chunks]
-    send_sem, recv_sem, local_sem = refs[2 * n_chunks + per * n_chunks :]
-    dp, fs = lax.axis_index("dp"), lax.axis_index("fsdp")
+def scatter_plan(dp, fs, n_dp, n_fs, ins, emit, scratch, send_sem, recv_sem, local_sem, first=0):
     bits = plan_bits(n_dp)
-    nb = len(bits)
     orders = (bits[::-1], bits)
     half = n_fs // 2
     index = {entry: at for at, entry in enumerate(combos(bits))}
-    greet(dp, fs, n_dp, n_fs)
     sends = []
 
-    def remote(chunk, slot, src, dst, device):
-        return pltpu.make_async_remote_copy(
-            src_ref=src,
-            dst_ref=dst,
-            send_sem=send_sem.at[chunk, slot],
-            recv_sem=recv_sem.at[chunk, slot],
-            device_id=device,
-            device_id_type=MESH,
-        )
-
     def add_into(kept, other):
-        count = kept.shape[0]
-
         def body(at, _):
-            total = kept[at].astype(F32) + other[at].astype(F32)
-            kept[at] = total.astype(BF16)
+            kept[at] = (kept[at].astype(F32) + other[at].astype(F32)).astype(BF16)
             return 0
 
-        lax.fori_loop(0, count, body, 0)
+        lax.fori_loop(0, kept.shape[0], body, 0)
 
     def stages(chunk):
-        src, out = ins[chunk], outs[chunk]
-        first, own, later, last = scratch[per * chunk : per * chunk + per]
+        src = ins[chunk]
+        cross_in, own, later, last = scratch[4 * chunk : 4 * chunk + 4]
         slots = itertools.count()
+
+        def remote(slot, view_from, view_to, device):
+            return pltpu.make_async_remote_copy(
+                src_ref=view_from,
+                dst_ref=view_to,
+                send_sem=send_sem.at[first + chunk, slot],
+                recv_sem=recv_sem.at[first + chunk, slot],
+                device_id=device,
+                device_id_type=MESH,
+            )
+
+        def launch(make):
+            make().start()
+            sends.append(lambda: make().wait_send())
+
+        def zone(entry, crossed):
+            return src.at[pl.ds(flip_all(flip(dp, 1) if crossed else dp, entry) * n_fs, n_fs)]
+
         pieces = [(next(slots), entry, index[entry]) for entry in combos(bits)]
-        loads = [
-            pltpu.make_async_copy(
-                src.at[pl.ds(flip_all(dp, entry) * n_fs, n_fs)], own.at[at], local_sem.at[chunk, at]
+
+        def load(entry, at):
+            return pltpu.make_async_copy(
+                zone(entry, False), own.at[at], local_sem.at[first + chunk, at]
             )
-            for _, entry, at in pieces
-        ]
+
+        def across(slot, entry, at):
+            return remote(slot, zone(entry, True), cross_in.at[at], (flip(dp, 1), fs))
 
         def start():
+            for item in pieces:
+                launch(lambda item=item: across(*item))
+            for _, entry, at in pieces:
+                load(entry, at).start()
+
+        def fold_cross():
             for slot, entry, at in pieces:
-                view = src.at[pl.ds(flip_all(flip(dp, 1), entry) * n_fs, n_fs)]
-                copy = remote(chunk, slot, view, first.at[at], (flip(dp, 1), fs))
-                copy.start()
-                sends.append(copy)
-            for load in loads:
-                load.start()
-
-        def fold_first():
-            for load, (slot, entry, at) in zip(loads, pieces):
-                load.wait()
-                remote(chunk, slot, first.at[at], first.at[at], (flip(dp, 1), fs)).wait_recv()
-                add_into(own.at[at], first.at[at])
-
-        steps = [start]
-        folds = [fold_first]
+                load(entry, at).wait()
+                across(slot, entry, at).wait_recv()
+                add_into(own.at[at], cross_in.at[at])
+
+        steps, before = [start], fold_cross
         used = 0
-        for depth in range(nb):
+        for depth in range(len(bits)):
             plan = []
             for part, order in enumerate(orders):
                 bit, gone = order[depth], order[:depth]
-                keep = [e for e in combos(bits) if not (set(e) & set(gone)) and bit not in e]
-                for entry in keep:
-                    away = tuple(sorted(entry + (bit,)))
-                    plan.append((next(slots), part, bit, index[away], index[entry], used))
-                    used += 1
-
-            def go(plan=plan, before=tuple(folds)):
-                for fold in before:
-                    fold()
-                for slot, part, bit, away, kept, place in plan:
-                    copy = remote(
-                        chunk,
-                        slot,
-                        own.at[away, pl.ds(part * half, half)],
-                        later.at[place],
-                        (flip(dp, bit), fs),
-                    )
-                    copy.start()
-                    sends.append(copy)
-
-            def fold(plan=plan):
-                for slot, part, bit, away, kept, place in plan:
-                    view = later.at[place]
-                    remote(chunk, slot, view, view, (flip(dp, bit), fs)).wait_recv()
-                    add_into(own.at[kept, pl.ds(part * half, half)], view)
+                for entry in combos(bits):
+                    if not (set(entry) & set(gone)) and bit not in entry:
+                        away = tuple(sorted(entry + (bit,)))
+                        plan.append((next(slots), part, bit, index[away], index[entry], used))
+                        used += 1
+
+            def move(slot, part, bit, away, kept, place):
+                return remote(
+                    slot,
+                    own.at[away, pl.ds(part * half, half)],
+                    later.at[place],
+                    (flip(dp, bit), fs),
+                )
+
+            def go(plan=plan, before=before, move=move):
+                before()
+                for item in plan:
+                    launch(lambda item=item: move(*item))
+
+            def fold(plan=plan, move=move):
+                for item in plan:
+                    move(*item).wait_recv()
+                    _, part, _, _, kept, place = item
+                    add_into(own.at[kept, pl.ds(part * half, half)], later.at[place])
 
             steps.append(go)
-            folds = [fold]
+            before = fold
         z_slots = [next(slots) for _ in range(1, n_fs)]
 
-        def cross(before=tuple(folds)):
-            for fold in before:
-                fold()
+        def along(step):
+            to = lax.rem(fs + step, n_fs)
+            return remote(z_slots[step - 1], own.at[0, to], last.at[step - 1], (dp, to))
+
+        def spread(before=before):
+            before()
             for step in range(1, n_fs):
-                to = lax.rem(fs + step, n_fs)
-                copy = remote(chunk, z_slots[step - 1], own.at[0, to], last.at[step - 1], (dp, to))
-                copy.start()
-                sends.append(copy)
+                launch(lambda step=step: along(step))
 
         def finish():
             total = own[0, fs].astype(F32)
             for step in range(1, n_fs):
-                view = last.at[step - 1]
-                remote(chunk, z_slots[step - 1], view, view, (dp, fs)).wait_recv()
+                along(step).wait_recv()
                 total = total + last[step - 1].astype(F32)
-            out[...] = total
-
-        steps += [cross, finish]
-        return steps
-
-    plans = [stages(chunk) for chunk in range(n_chunks)]
-    depth = len(plans[0])
-    for wave in range(n_chunks + depth - 1):
-        for chunk in range(n_chunks):
-            stage = wave - chunk
-            if 0 <= stage < depth:
-                plans[chunk][stage]()
-    for copy in sends:
-        copy.wait_send()
-
-
-def scatter_all(n_dp, n_fs, arrays, collective_id):
-    nb = len(plan_bits(n_dp))
-    pieces = 2**nb
+            emit(chunk, total)
+
+        return steps + [spread, finish]
+
+    return [stages(chunk) for chunk in range(len(ins))], sends
+
+
+def scatter_scratch(n_dp, n_fs, tails):
+    pieces = 2 ** len(plan_bits(n_dp))
     scratch = []
-    for a in arrays:
-        tail = a.shape[1:]
+    for tail in tails:
         scratch += [
             pltpu.VMEM((pieces, n_fs) + tail, BF16),
             pltpu.VMEM((pieces, n_fs) + tail, BF16),
             pltpu.VMEM((2 * (pieces - 1), n_fs // 2) + tail, BF16),
             pltpu.VMEM((n_fs - 1,) + tail, BF16),
         ]
+    return scratch
+
+
+def scatter_sems(n_dp, n_fs, chunks):
     count = slot_count(n_dp, n_fs)
+    return [
+        pltpu.SemaphoreType.DMA((chunks, count)),
+        pltpu.SemaphoreType.DMA((chunks, count)),
+        pltpu.SemaphoreType.DMA((chunks, 2 ** len(plan_bits(n_dp)))),
+    ]
+
+
+def scatter_kernel(n_dp, n_fs, n_chunks, *refs):
+    ins, outs = refs[:n_chunks], refs[n_chunks : 2 * n_chunks]
+    scratch = refs[2 * n_chunks : 6 * n_chunks]
+    dp, fs = lax.axis_index("dp"), lax.axis_index("fsdp")
+    greet(dp, fs, n_dp, n_fs)
+
+    def emit(chunk, total):
+        outs[chunk][...] = total
+
+    plans, sends = scatter_plan(dp, fs, n_dp, n_fs, ins, emit, scratch, *refs[6 * n_chunks :])
+    for wave in waves(plans):
+        for stage in wave:
+            stage()
+    for wait in sends:
+        wait()
+
+
+def scatter_all(n_dp, n_fs, arrays, collective_id):
     n = len(arrays)
     return pl.pallas_call(
         partial(scatter_kernel, n_dp, n_fs, n),
         out_shape=[jax.ShapeDtypeStruct(a.shape[1:], F32) for a in arrays],
         in_specs=[pl.BlockSpec(memory_space=pltpu.HBM)] * n,
         out_specs=[pl.BlockSpec(memory_space=pltpu.VMEM)] * n,
-        scratch_shapes=scratch
-        + [
-            pltpu.SemaphoreType.DMA((n, count)),
-            pltpu.SemaphoreType.DMA((n, count)),
-            pltpu.SemaphoreType.DMA((n, pieces)),
-        ],
+        scratch_shapes=scatter_scratch(n_dp, n_fs, [a.shape[1:] for a in arrays])
+        + scatter_sems(n_dp, n_fs, n),
         compiler_params=pltpu.CompilerParams(
             collective_id=collective_id, has_side_effects=True, vmem_limit_bytes=48 << 20
         ),
@@ -345,73 +368,100 @@
     )(*arrays)
 
 
-def exchange_kernel(n_dp, n_fs, x_ref, out_ref, octet, line, send_sem, recv_sem):
-    dp, fs = lax.axis_index("dp"), lax.axis_index("fsdp")
-    barrier = pltpu.get_barrier_semaphore()
-    for step in range(1, n_dp):
-        pl.semaphore_signal(
-            barrier, inc=1, device_id=(lax.rem(dp + step, n_dp), fs), device_id_type=MESH
-        )
-    for step in range(1, n_fs):
-        pl.semaphore_signal(
-            barrier, inc=1, device_id=(dp, lax.rem(fs + step, n_fs)), device_id_type=MESH
-        )
-    pl.semaphore_wait(barrier, n_dp + n_fs - 2)
-    sends = []
-    octet[0] = x_ref[...]
-    for step in range(1, n_dp):
-        copy = pltpu.make_async_remote_copy(
-            src_ref=octet.at[0],
-            dst_ref=octet.at[step],
+def swap_rows(axis, place, count, buffer, send_sem, recv_sem):
+    def make(step):
+        return pltpu.make_async_remote_copy(
+            src_ref=buffer.at[0],
+            dst_ref=buffer.at[step],
             send_sem=send_sem.at[step],
             recv_sem=recv_sem.at[step],
-            device_id=(lax.rem(dp + step, n_dp), fs),
+            device_id={axis: lax.rem(place + step, count)},
             device_id_type=MESH,
         )
-        copy.start()
-        sends.append(copy)
-    for copy in sends:
-        copy.wait_recv()
+
+    for step in range(1, count):
+        make(step).start()
+    for step in range(1, count):
+        make(step).wait_recv()
+    for step in range(1, count):
+        make(step).wait_send()
+
+
+def sum_over(x, dp, fs, n_dp, n_fs, octet, line, send_sem, recv_sem):
+    octet[0] = x
+    swap_rows("dp", dp, n_dp, octet, send_sem.at[0], recv_sem.at[0])
     total = octet[0]
     for step in range(1, n_dp):
         total = total + octet[step]
     line[0] = total
-    more = []
-    for step in range(1, n_fs):
-        copy = pltpu.make_async_remote_copy(
-            src_ref=line.at[0],
-            dst_ref=line.at[step],
-            send_sem=send_sem.at[n_dp + step],
-            recv_sem=recv_sem.at[n_dp + step],
-            device_id=(dp, lax.rem(fs + step, n_fs)),
-            device_id_type=MESH,
-        )
-        copy.start()
-        more.append(copy)
-    for copy in more:
-        copy.wait_recv()
+    swap_rows("fsdp", fs, n_fs, line, send_sem.at[1], recv_sem.at[1])
     total = line[0]
     for step in range(1, n_fs):
         total = total + line[step]
-    out_ref[...] = total
-    for copy in sends + more:
-        copy.wait_send()
-
-
-def exchange(n_dp, n_fs, x, collective_id):
+    return total
+
+
+def pooled(buffer, count, weight):
+    means = [buffer[k, 0:1, :] for k in range(count)]
+    center = sum(means[1:], means[0]) * (1.0 / count)
+    spread = buffer[0, 1:2, :]
+    for k in range(1, count):
+        spread = spread + buffer[k, 1:2, :]
+    off = (means[0] - center) * (means[0] - center)
+    for mean in means[1:]:
+        off = off + (mean - center) * (mean - center)
+    return center, spread + weight * off
+
+
+def pool_over(center, spread, frames, dp, fs, n_dp, n_fs, octet, line, send_sem, recv_sem):
+    octet[0] = jnp.zeros(octet.shape[1:], F32)
+    line[0] = jnp.zeros(line.shape[1:], F32)
+    octet[0, 0:1, :] = center
+    octet[0, 1:2, :] = spread
+    swap_rows("dp", dp, n_dp, octet, send_sem.at[0], recv_sem.at[0])
+    center, spread = pooled(octet, n_dp, float(frames))
+    line[0, 0:1, :] = center
+    line[0, 1:2, :] = spread
+    swap_rows("fsdp", fs, n_fs, line, send_sem.at[1], recv_sem.at[1])
+    return pooled(line, n_fs, float(frames * n_dp))
+
+
+def swap_scratch(n_dp, n_fs, channels):
+    return [
+        pltpu.VMEM((n_dp, 8, channels), F32),
+        pltpu.VMEM((n_fs, 8, channels), F32),
+        pltpu.SemaphoreType.DMA((2, max(n_dp, n_fs))),
+        pltpu.SemaphoreType.DMA((2, max(n_dp, n_fs))),
+    ]
+
+
+def pool_kernel(n_dp, n_fs, frames, x_ref, out_ref, octet, line, send_sem, recv_sem):
+    dp, fs = lax.axis_index("dp"), lax.axis_index("fsdp")
+    greet(dp, fs, n_dp, n_fs)
+    octet[0] = x_ref[...]
+    center, spread = pool_over(
+        x_ref[0:1, :], x_ref[1:2, :], frames, dp, fs, n_dp, n_fs, octet, line, send_sem, recv_sem
+    )
+    out_ref[...] = x_ref[...]
+    out_ref[0:1, :] = center
+    out_ref[1:2, :] = spread
+
+
+def total_kernel(n_dp, n_fs, frames, x_ref, out_ref, octet, line, send_sem, recv_sem):
+    dp, fs = lax.axis_index("dp"), lax.axis_index("fsdp")
+    greet(dp, fs, n_dp, n_fs)
+    out_ref[...] = sum_over(x_ref[...], dp, fs, n_dp, n_fs, octet, line, send_sem, recv_sem)
+
+
+def exchange(n_dp, n_fs, x, frames, collective_id, kernel):
     return pl.pallas_call(
-        partial(exchange_kernel, n_dp, n_fs),
+        partial(kernel, n_dp, n_fs, frames),
         out_shape=jax.ShapeDtypeStruct(x.shape, F32),
         in_specs=[pl.BlockSpec(memory_space=pltpu.VMEM)],
         out_specs=pl.BlockSpec(memory_space=pltpu.VMEM),
-        scratch_shapes=[
-            pltpu.VMEM((n_dp,) + x.shape, F32),
-            pltpu.VMEM((n_fs,) + x.shape, F32),
-            pltpu.SemaphoreType.DMA((n_dp + n_fs,)),
-            pltpu.SemaphoreType.DMA((n_dp + n_fs,)),
-        ],
+        scratch_shapes=swap_scratch(n_dp, n_fs, x.shape[1]),
         compiler_params=pltpu.CompilerParams(collective_id=collective_id, has_side_effects=True),
-        name="exchange_sums",
+        name="exchange_rows",
     )(x)
 
 
@@ -424,6 +474,11 @@
 ROWS = 128
 SPAN = 32
 VMEM_LIMIT = 60 << 20
+TAP_ROW = 24
+RATE = 40
+MAP_IN = 72
+MAP_OUT = 104
+TABLE = 136
 
 
 def sigmoid(v):
@@ -510,13 +565,15 @@
             )
 
 
-def taps_over(padded, taps_ref, store, tiles, reverse, block=64):
+def taps_over(padded, table_ref, store, tiles, reverse, block=64):
     pitch = TILE + 2 * REACH
     per = TILE // block
     lanes = padded.shape[0]
     for lane in range(lanes):
         weights = [
-            jnp.broadcast_to(taps_ref[k : k + 1, lane * 128 : lane * 128 + 128], (block, 128))
+            jnp.broadcast_to(
+                table_ref[TAP_ROW + k : TAP_ROW + k + 1, lane * 128 : lane * 128 + 128], (block, 128)
+            )
             for k in range(TAPS)
         ]
 
@@ -533,173 +590,286 @@
         lax.fori_loop(0, tiles * per, run, 0)
 
 
-def front_kernel(
-    flags_ref,
-    x_ref,
-    up_ref,
-    down_ref,
-    mixin_ref,
-    mixout_ref,
-    convin_ref,
-    bias_ref,
-    vec_ref,
-    taps_ref,
-    decay_ref,
-    map_ref,
-    h_out,
-    x1_out,
-    u_out,
-    v_out,
-    y_out,
-    gated_out,
-    x2_out,
-    p_out,
-    hold_out,
-    w_out,
-    stat_out,
-    low_scr,
-    sum_scr,
-    state_scr,
-    padded,
-):
-    at = pl.program_id(0)
-    tiles = pl.num_programs(0)
+def small_exp(v):
+    return 1.0 + v * (1.0 + v * (0.5 + v * (1.0 / 6 + v * (1.0 / 24 + v * (1.0 / 120)))))
+
+
+def small_expm1_over(v):
+    return 1.0 + v * (
+        0.5 + v * (1.0 / 6 + v * (1.0 / 24 + v * (1.0 / 120 + v * (1.0 / 720 + v * (1.0 / 5040)))))
+    )
+
+
+def state_terms(table_ref):
+    log_decay = -jnp.exp(table_ref[RATE : RATE + STATES, :])
+    root = jnp.sqrt(-2.0 * log_decay * small_expm1_over(2.0 * log_decay))
+    maps_in = table_ref[MAP_IN : MAP_IN + STATES, :]
+    maps_out = table_ref[MAP_OUT : MAP_OUT + STATES, :]
+    return log_decay, small_exp(log_decay), root, maps_in, maps_out
+
+
+def ref_rows(ref):
+    return ref.reshape((ref.shape[0] * ref.shape[1], ref.shape[2]))
+
+
+WEIGHTS = 6
+
+
+def front_kernel(mesh_size, *refs):
+    fused = mesh_size is not None
+    refs = list(refs)
+    take = lambda count: [refs.pop(0) for _ in range(count)]
+    flags_ref, x_ref = take(2)
+    if fused:
+        n_dp, n_fs = mesh_size
+        shards = take(7)
+    else:
+        up_ref, down_ref, mixin_ref, mixout_ref, convin_ref, table_in, bias_in = take(7)
+    (
+        h_out,
+        x1_out,
+        u_out,
+        v_out,
+        y_out,
+        gated_out,
+        x2_out,
+        p_out,
+        hold_out,
+        w_out,
+        stat_out,
+        table_ref,
+        bias_ref,
+        decay_ref,
+        map_ref,
+    ) = take(15)
+    gathered = take(9) if fused else []
+    x1_scr, low_all, low_scr, sum_scr, state_scr, padded = take(6)
+    step = pl.program_id(0)
     channels = x_ref.shape[1]
+    frames = w_out.shape[0]
+    tiles = frames // TILE
     lanes = channels // 128
-    gain = lambda k: vec_ref[k : k + 1, :]
-    shift = lambda k: vec_ref[6 + k : 7 + k, :]
-
-    def first(rows):
-        e, _ = norm_parts(x_ref[rows, :].astype(F32))
-        low_scr[rows, :] = (e * gain(0) + shift(0)).astype(BF16)
-        sum_scr[rows, :] = jnp.zeros((ROWS, channels), F32)
-
-    by_rows(first)
-
-    def hidden(c, _):
-        cols = columns(c)
-        h = dot_nn(low_scr[...], up_ref[:, cols]) + bias_ref[0:1, cols]
-        h_out[:, cols] = h.astype(BF16)
-        active = (h * sigmoid(h)).astype(BF16)
-        sum_scr[...] += dot_nn(active, down_ref[cols, :])
-        return 0
-
-    lax.fori_loop(0, up_ref.shape[1] // CHUNK, hidden, 0)
-
-    def second(rows):
-        x1 = x_ref[rows, :].astype(F32) + 0.5 * (sum_scr[rows, :] + shift(6))
-        x1_out[rows, :] = x1
-        e, _ = norm_parts(x1)
-        low_scr[rows, :] = (e * gain(1) + shift(1)).astype(BF16)
-
-    by_rows(second)
-
-    def project(c, _):
-        cols = columns(c)
-        right = columns(c + channels // CHUNK)
-        u_out[:, cols] = dot_nn(low_scr[...], mixin_ref[:, cols])
-        v_out[:, cols] = dot_nn(low_scr[...], mixin_ref[:, right]).astype(BF16)
-        return 0
-
-    lax.fori_loop(0, channels // CHUNK, project, 0)
-
-    low_half = half_masks(128)
-    keep = flags_ref[at].astype(F32)
-
-    @pl.when(at == 0)
+    gain = lambda k: table_ref[k : k + 1, :]
+    shift = lambda k: table_ref[6 + k : 7 + k, :]
+    here = lambda rows, tile: pl.ds(pl.multiple_of(tile * TILE + rows.start, ROWS), ROWS)
+    if fused:
+        small_v, up_v, down_v, mixin_v, mixout_v, convin_v = take(WEIGHTS)
+        send_sem, recv_sem, local_sem, load_sem = take(4)
+        swap = take(4)
+        dp, fs = lax.axis_index("dp"), lax.axis_index("fsdp")
+        small_s, up_s, down_s, mixin_s, mixout_s, convin_s, convout_s = shards
+        sources = [
+            small_s.at[0],
+            up_s.at[0],
+            down_s.at[0],
+            mixin_s.at[0],
+            mixout_s.at[0],
+            convin_s.at[0],
+            convout_s.at[0],
+            up_s.at[1],
+            down_s.at[1],
+        ]
+        plans, sends = gather_plan(
+            dp, fs, n_dp, n_fs, sources, gathered, send_sem, recv_sem, local_sem
+        )
+        order = waves(plans)
+        ready = len(plans[0]) + 2
+        held = (small_v, up_v, down_v, mixin_v, mixout_v, convin_v)
+
+        def load(chunk):
+            return pltpu.make_async_copy(gathered[chunk], held[chunk], load_sem.at[chunk])
+
+        up_ref, down_ref, mixin_ref, mixout_ref, convin_ref = [ref_rows(r) for r in held[1:]]
+
+        @pl.when(step == 0)
+        def _():
+            greet(dp, fs, n_dp, n_fs)
+            for wave in order[:ready]:
+                for stage in wave:
+                    stage()
+            for chunk in range(3):
+                load(chunk).start()
+            load(0).wait()
+            table_ref[...] = ref_rows(small_v)[:, :256].astype(F32).T[: table_ref.shape[0], :]
+            total = small_v[0, :, 256:].astype(F32)
+            for k in range(1, n_dp * n_fs):
+                total = total + small_v[k, :, 256:].astype(F32)
+            bias_ref[...] = total
+            load(1).wait()
+            load(2).wait()
+
+        for k in range(1, tiles + 1):
+
+            @pl.when(step == k)
+            def _(k=k):
+                for stage in order[ready + k - 1]:
+                    stage()
+                if k == tiles:
+                    for chunk in range(3, 6):
+                        load(chunk).start()
+                    for chunk in range(3, 6):
+                        load(chunk).wait()
+
+        rest = order[ready + tiles :]
+        for k in range(tiles):
+
+            @pl.when(step == tiles + 1 + k)
+            def _(k=k):
+                for wave in rest[k :: tiles] if k < tiles - 1 else rest[k:]:
+                    for stage in wave:
+                        stage()
+                if k == tiles - 1:
+                    for wait in sends:
+                        wait()
+
+    else:
+
+        @pl.when(step == 0)
+        def _():
+            table_ref[...] = table_in[...]
+            bias_ref[...] = bias_in[...]
+
+    @pl.when(step == 0)
     def _():
+        _, decay, root, maps_in, maps_out = state_terms(table_ref)
+        decay_ref[...] = decay
+        map_ref[...] = maps_in * root * maps_out
         state_scr[...] = jnp.zeros_like(state_scr)
 
-    state_scr[...] = state_scr[...] * keep
-
-    def scan_span(span, _):
-        hold_out[span] = state_scr[...]
-
-        def scan(step, _):
-            start = pl.multiple_of(span * SPAN + step * 8, 8)
-            for lane in range(lanes):
-                cols = slice(lane * 128, lane * 128 + 128)
-                state = state_scr[:, cols]
-                decay = decay_ref[:, cols]
-                maps = map_ref[:, cols]
-                drive = u_out[pl.ds(start, 8), cols]
-                parts = []
-                for j in range(8):
-                    state = decay * state + jnp.broadcast_to(drive[j : j + 1, :], (STATES, 128))
-                    parts.append(fold_states(maps * state))
-                state_scr[:, cols] = state
-                sum_scr[pl.ds(start, 8), cols] = merge_rows(parts, low_half)
+    @pl.when(step < tiles)
+    def _():
+        def first(rows):
+            e, _ = norm_parts(x_ref[rows, :].astype(F32))
+            low_scr[rows, :] = (e * gain(0) + shift(0)).astype(BF16)
+            sum_scr[rows, :] = jnp.zeros((ROWS, channels), F32)
+
+        by_rows(first)
+
+        def hidden(c, _):
+            cols = columns(c)
+            h = dot_nn(low_scr[...], up_ref[:, cols]) + bias_ref[pl.ds(c, 1), :]
+            h_out[:, cols] = h.astype(BF16)
+            active = (h * sigmoid(h)).astype(BF16)
+            sum_scr[...] += dot_nn(active, down_ref[cols, :])
             return 0
 
-        lax.fori_loop(0, SPAN // 8, scan, 0)
-        return 0
-
-    lax.fori_loop(0, TILE // SPAN, scan_span, 0)
-
-    def gate(rows):
-        y = sum_scr[rows, :] + shift(11) * u_out[rows, :]
-        v = v_out[rows, :].astype(F32)
-        y_out[rows, :] = y.astype(BF16)
-        gated = (y * (v * sigmoid(v))).astype(BF16)
-        gated_out[rows, :] = gated
-
-    by_rows(gate)
-    sum_scr[...] = dot_nn(gated_out[...], mixout_ref[...])
-
-    def third(rows):
-        x2 = x1_out[rows, :] + (sum_scr[rows, :] + shift(8))
-        x2_out[rows, :] = x2
-        e, _ = norm_parts(x2)
-        low_scr[rows, :] = (e * gain(2) + shift(2)).astype(BF16)
-
-    by_rows(third)
-    pitch = TILE + 2 * REACH
-
-    def widen(c, _):
-        cols = columns(c)
-        right = columns(c + channels // CHUNK)
-        left_part = dot_nn(low_scr[...], convin_ref[:, cols]) + vec_ref[15:16, cols]
-        right_part = dot_nn(low_scr[...], convin_ref[:, right]) + vec_ref[16:17, cols]
-        p_out[:, cols] = left_part.astype(BF16)
-        p_out[:, right] = right_part.astype(BF16)
-        g = left_part * sigmoid(right_part)
-        place = pl.ds(pl.multiple_of(at * pitch + REACH, 8), TILE)
-        for k in range(CHUNK // 128):
-            padded[c * (CHUNK // 128) + k, place, :] = g[:, k * 128 : k * 128 + 128]
-        return 0
-
-    lax.fori_loop(0, channels // CHUNK, widen, 0)
-
-    @pl.when(at == tiles - 1)
+        lax.fori_loop(0, up_ref.shape[1] // CHUNK, hidden, 0)
+
+        def second(rows):
+            x1 = x_ref[rows, :].astype(F32) + 0.5 * (sum_scr[rows, :] + shift(6))
+            x1_out[rows, :] = x1
+            x1_scr[here(rows, step), :] = x1
+            e, _ = norm_parts(x1)
+            low_all[here(rows, step), :] = (e * gain(1) + shift(1)).astype(BF16)
+
+        by_rows(second)
+
+    @pl.when((step >= tiles) & (step < 2 * tiles))
     def _():
-        count = w_out.shape[0] // TILE
-        fill_halo(padded, flags_ref, count)
+        at = step - tiles
+        whole_tile = pl.ds(pl.multiple_of(at * TILE, TILE), TILE)
+
+        def project(c, _):
+            cols = columns(c)
+            right = columns(c + channels // CHUNK)
+            u_out[:, cols] = dot_nn(low_all[whole_tile, :], mixin_ref[:, cols])
+            v_out[:, cols] = dot_nn(low_all[whole_tile, :], mixin_ref[:, right]).astype(BF16)
+            return 0
+
+        lax.fori_loop(0, channels // CHUNK, project, 0)
+        low_half = half_masks(128)
+        state_scr[...] = state_scr[...] * flags_ref[at].astype(F32)
+
+        def scan_span(span, _):
+            hold_out[span] = state_scr[...]
+
+            def scan(block, _):
+                start = pl.multiple_of(span * SPAN + block * 8, 8)
+                for lane in range(lanes):
+                    cols = slice(lane * 128, lane * 128 + 128)
+                    state = state_scr[:, cols]
+                    decay = decay_ref[:, cols]
+                    maps = map_ref[:, cols]
+                    drive = u_out[pl.ds(start, 8), cols]
+                    parts = []
+                    for j in range(8):
+                        state = decay * state + jnp.broadcast_to(drive[j : j + 1, :], (STATES, 128))
+                        parts.append(fold_states(maps * state))
+                    state_scr[:, cols] = state
+                    sum_scr[pl.ds(start, 8), cols] = merge_rows(parts, low_half)
+                return 0
+
+            lax.fori_loop(0, SPAN // 8, scan, 0)
+            return 0
+
+        lax.fori_loop(0, TILE // SPAN, scan_span, 0)
+
+        def gate(rows):
+            y = sum_scr[rows, :] + shift(11) * u_out[rows, :]
+            v = v_out[rows, :].astype(F32)
+            y_out[rows, :] = y.astype(BF16)
+            gated_out[rows, :] = (y * (v * sigmoid(v))).astype(BF16)
+
+        by_rows(gate)
+        sum_scr[...] = dot_nn(gated_out[...], mixout_ref[...])
+
+        def third(rows):
+            x2 = x1_scr[here(rows, at), :] + (sum_scr[rows, :] + shift(8))
+            x2_out[rows, :] = x2
+            e, _ = norm_parts(x2)
+            low_scr[rows, :] = (e * gain(2) + shift(2)).astype(BF16)
+
+        by_rows(third)
+        pitch = TILE + 2 * REACH
+
+        def widen(c, _):
+            cols = columns(c)
+            right = columns(c + channels // CHUNK)
+            left_part = dot_nn(low_scr[...], convin_ref[:, cols]) + table_ref[15:16, cols]
+            right_part = dot_nn(low_scr[...], convin_ref[:, right]) + table_ref[16:17, cols]
+            p_out[:, cols] = left_part.astype(BF16)
+            p_out[:, right] = right_part.astype(BF16)
+            g = left_part * sigmoid(right_part)
+            place = pl.ds(pl.multiple_of(at * pitch + REACH, 8), TILE)
+            for k in range(CHUNK // 128):
+                padded[c * (CHUNK // 128) + k, place, :] = g[:, k * 128 : k * 128 + 128]
+            return 0
+
+        lax.fori_loop(0, channels // CHUNK, widen, 0)
+
+    @pl.when(step == 2 * tiles)
+    def _():
+        fill_halo(padded, flags_ref, tiles)
 
         def store(lane, row, base, total):
             w_out[pl.ds(pl.multiple_of(row, 64), 64), lane * 128 : lane * 128 + 128] = total
 
-        taps_over(padded, taps_ref, store, count, False)
+        taps_over(padded, table_ref, store, tiles, False)
         stat_out[...] = jnp.zeros_like(stat_out)
 
         def total(at, _):
             rows = pl.ds(pl.multiple_of(at * ROWS, ROWS), ROWS)
-            stat_out[0:8, :] += fold8(w_out[rows, :])
+            stat_out[...] += fold8(w_out[rows, :])
             return 0
 
-        lax.fori_loop(0, w_out.shape[0] // ROWS, total, 0)
-        center = jnp.sum(stat_out[0:8, :], axis=0, keepdims=True) * (1.0 / w_out.shape[0])
+        lax.fori_loop(0, frames // ROWS, total, 0)
+        center = jnp.sum(stat_out[...], axis=0, keepdims=True) * (1.0 / frames)
+        stat_out[...] = jnp.zeros_like(stat_out)
 
         def spread(at, _):
             rows = pl.ds(pl.multiple_of(at * ROWS, ROWS), ROWS)
             off = w_out[rows, :] - center
-            stat_out[8:16, :] += fold8(off * off)
+            stat_out[...] += fold8(off * off)
             return 0
 
-        lax.fori_loop(0, w_out.shape[0] // ROWS, spread, 0)
-        stat_out[0:8, :] = jnp.broadcast_to(center, (8, channels))
-        stat_out[8:16, :] = jnp.broadcast_to(
-            jnp.sum(stat_out[8:16, :], axis=0, keepdims=True), (8, channels)
-        )
+        lax.fori_loop(0, frames // ROWS, spread, 0)
+        around = jnp.sum(stat_out[...], axis=0, keepdims=True)
+        if fused:
+            center, around = pool_over(center, around, frames, dp, fs, n_dp, n_fs, *swap)
+            around = lax.rsqrt(around * (1.0 / (frames * n_dp * n_fs)) + EPSILON)
+        stat_out[...] = jnp.zeros_like(stat_out)
+        stat_out[0:1, :] = center
+        stat_out[1:2, :] = around
 
 
 def whole(shape):
@@ -707,62 +877,93 @@
     return pl.BlockSpec(shape, lambda *_: zeros)
 
 
-def params():
+def params(collective_id=None):
+    if collective_id is None:
+        return pltpu.CompilerParams(
+            dimension_semantics=("arbitrary",), vmem_limit_bytes=VMEM_LIMIT
+        )
     return pltpu.CompilerParams(
-        dimension_semantics=("arbitrary",), vmem_limit_bytes=VMEM_LIMIT
+        dimension_semantics=("arbitrary",),
+        vmem_limit_bytes=VMEM_LIMIT,
+        collective_id=collective_id,
+        has_side_effects=True,
     )
 
 
-def front(flags, x, up, down, mixin, mixout, convin, bias, vec, taps, decay, maps):
+def front(mesh_size, flags, x, weights, collective_id=None):
+    fused = mesh_size is not None
     frames, channels = x.shape
-    hidden = up.shape[1]
+    hidden = weights[1].shape[-1] if fused else weights[0].shape[1]
     tiles = frames // TILE
-    row = lambda width: pl.BlockSpec((TILE, width), lambda i, *_: (i, 0))
+    early = lambda width: pl.BlockSpec((TILE, width), lambda i: (jnp.minimum(i, tiles - 1), 0))
+    place = lambda i: jnp.clip(i - tiles, 0, tiles - 1)
+    late = lambda width: pl.BlockSpec((TILE, width), lambda i: (place(i), 0))
     shape = lambda width, kind: jax.ShapeDtypeStruct((frames, width), kind)
     spans = TILE // SPAN
+    state = jax.ShapeDtypeStruct((STATES, channels), F32)
+    out_shape = [
+        shape(hidden, BF16),
+        shape(channels, F32),
+        shape(channels, F32),
+        shape(channels, BF16),
+        shape(channels, BF16),
+        shape(channels, BF16),
+        shape(channels, F32),
+        shape(2 * channels, BF16),
+        jax.ShapeDtypeStruct((frames // SPAN, STATES, channels), F32),
+        shape(channels, F32),
+        jax.ShapeDtypeStruct((8, channels), F32),
+        jax.ShapeDtypeStruct((TABLE, channels), F32),
+        jax.ShapeDtypeStruct((16, CHUNK), F32),
+        state,
+        state,
+    ]
+    out_specs = [early(hidden), early(channels)]
+    out_specs += [late(channels)] * 5
+    out_specs += [
+        late(2 * channels),
+        pl.BlockSpec((spans, STATES, channels), lambda i: (place(i), 0, 0)),
+    ]
+    out_specs += [whole(s.shape) for s in out_shape[9:]]
+    scratch = [
+        pltpu.VMEM((frames, channels), F32),
+        pltpu.VMEM((frames, channels), BF16),
+        pltpu.VMEM((TILE, channels), BF16),
+        pltpu.VMEM((TILE, channels), F32),
+        pltpu.VMEM((STATES, channels), F32),
+        pltpu.VMEM((channels // 128, tiles * (TILE + 2 * REACH), 128), F32),
+    ]
+    in_specs = [pl.BlockSpec(memory_space=pltpu.SMEM), early(channels)]
+    if fused:
+        n_dp, n_fs = mesh_size
+        hbm = pl.BlockSpec(memory_space=pltpu.HBM)
+        in_specs += [hbm] * len(weights)
+        chunks = []
+        for at in (0, 1, 2, 3, 4, 5, 6, 1, 2):
+            chunks.append(jax.ShapeDtypeStruct((n_dp * n_fs,) + weights[at].shape[1:], BF16))
+        out_shape += chunks
+        out_specs += [hbm] * len(chunks)
+        scratch += [pltpu.VMEM(c.shape, BF16) for c in chunks[:WEIGHTS]]
+        count = slot_count(n_dp, n_fs)
+        scratch += [
+            pltpu.SemaphoreType.DMA((len(chunks), count)),
+            pltpu.SemaphoreType.DMA((len(chunks), count)),
+            pltpu.SemaphoreType.DMA((len(chunks),)),
+            pltpu.SemaphoreType.DMA((WEIGHTS,)),
+        ]
+        scratch += swap_scratch(n_dp, n_fs, channels)
+    else:
+        in_specs += [whole(a.shape) for a in weights]
     return pl.pallas_call(
-        front_kernel,
-        grid_spec=pltpu.PrefetchScalarGridSpec(
-            num_scalar_prefetch=1,
-            grid=(tiles,),
-            in_specs=[row(channels)]
-            + [whole(a.shape) for a in (up, down, mixin, mixout, convin, bias, vec, taps, decay, maps)],
-            out_specs=[
-                row(hidden),
-                row(channels),
-                row(channels),
-                row(channels),
-                row(channels),
-                row(channels),
-                row(channels),
-                row(2 * channels),
-                pl.BlockSpec((spans, STATES, channels), lambda i, *_: (i, 0, 0)),
-                whole((frames, channels)),
-                whole((16, channels)),
-            ],
-            scratch_shapes=[
-                pltpu.VMEM((TILE, channels), BF16),
-                pltpu.VMEM((TILE, channels), F32),
-                pltpu.VMEM((STATES, channels), F32),
-                pltpu.VMEM((channels // 128, tiles * (TILE + 2 * REACH), 128), F32),
-            ],
-        ),
-        out_shape=[
-            shape(hidden, BF16),
-            shape(channels, F32),
-            shape(channels, F32),
-            shape(channels, BF16),
-            shape(channels, BF16),
-            shape(channels, BF16),
-            shape(channels, F32),
-            shape(2 * channels, BF16),
-            jax.ShapeDtypeStruct((frames // SPAN, STATES, channels), F32),
-            shape(channels, F32),
-            jax.ShapeDtypeStruct((16, channels), F32),
-        ],
-        compiler_params=params(),
+        partial(front_kernel, mesh_size),
+        grid=(2 * tiles + 1,),
+        in_specs=in_specs,
+        out_specs=out_specs,
+        out_shape=out_shape,
+        scratch_shapes=scratch,
+        compiler_params=params(collective_id),
         name="front",
-    )(flags, x, up, down, mixin, mixout, convin, bias, vec, taps, decay, maps)
+    )(flags, x, *weights)
 
 
 def ffn_back(low_t, grad_t, grad_ref, h_load, up_ref, down_ref, up_acc, down_acc, bias_acc, back_scr, hidden):
@@ -848,7 +1049,7 @@
 
     def forward(c, _):
         cols = columns(c)
-        h = dot_nn(low_scr[...], up_ref[:, cols]) + bias_ref[1:2, cols]
+        h = dot_nn(low_scr[...], up_ref[:, cols]) + bias_ref[pl.ds(8 + c, 1), :]
         h_scr[:, cols] = h
         active = (h * sigmoid(h)).astype(BF16)
         sum_scr[...] += dot_nn(active, down_ref[cols, :])
@@ -963,7 +1164,7 @@
     )(x2, w, cot, up, down, convout, bias, vec, stat)
 
 
-def conv_back_kernel(flags_ref, w_ref, gnb_ref, p_ref, taps_ref, vec_ref, stat_ref, gg_ref, gtaps_ref, padded, gpad):
+def conv_back_kernel(flags_ref, w_ref, gnb_ref, p_ref, vec_ref, stat_ref, gg_ref, gtaps_ref, padded, gpad):
     frames, channels = w_ref.shape
     tiles = frames // TILE
     pitch = TILE + 2 * REACH
@@ -992,7 +1193,7 @@
     def store(lane, row, base, total):
         gg_ref[pl.ds(pl.multiple_of(row, 64), 64), lane * 128 : lane * 128 + 128] = total
 
-    taps_over(padded, taps_ref, store, tiles, True)
+    taps_over(padded, vec_ref, store, tiles, True)
     block = 64
     per = TILE // block
     for lane in range(channels // 128):
@@ -1010,13 +1211,13 @@
             gtaps_ref[k : k + 1, lane * 128 : lane * 128 + 128] = jnp.sum(sums[k], axis=0, keepdims=True)
 
 
-def conv_back(flags, w, gnb, p, taps, vec, stat):
+def conv_back(flags, w, gnb, p, vec, stat):
     frames, channels = w.shape
     tiles = frames // TILE
     pad = pltpu.VMEM((channels // 128, tiles * (TILE + 2 * REACH), 128), F32)
     return pl.pallas_call(
         conv_back_kernel,
-        in_specs=[pl.BlockSpec(memory_space=pltpu.SMEM)] + [pl.BlockSpec(memory_space=pltpu.VMEM)] * 6,
+        in_specs=[pl.BlockSpec(memory_space=pltpu.SMEM)] + [pl.BlockSpec(memory_space=pltpu.VMEM)] * 5,
         out_specs=[pl.BlockSpec(memory_space=pltpu.VMEM)] * 2,
         out_shape=[
             jax.ShapeDtypeStruct((frames, channels), F32),
@@ -1025,7 +1226,7 @@
         scratch_shapes=[pad, pad],
         compiler_params=pltpu.CompilerParams(vmem_limit_bytes=VMEM_LIMIT),
         name="conv_back",
-    )(flags, w, gnb, p, taps, vec, stat)
+    )(flags, w, gnb, p, vec, stat)
 
 
 def back_kernel(
@@ -1362,38 +1563,32 @@
     )(x, h, gx1, up, down, vec)
 
 
-def pack_small(bias_up, conv_bias, rate, maps, taps, gains, shifts, devices=1):
-    layers, hidden = bias_up.shape
-    channels = conv_bias.shape[0]
-    ratio = hidden // channels
-    bias = bias_up.reshape((layers, devices, ratio, channels // devices))
-    bias = bias.transpose((0, 2, 1, 3)).reshape((layers * ratio, channels))
-    rows = jnp.concatenate(
-        [bias, conv_bias[None], rate, maps.reshape((-1, channels)), taps, gains, shifts], axis=0
+def pack_table(gains, shifts, conv_bias, taps, rate, maps):
+    channels = gains.shape[1]
+    blank = lambda rows: jnp.zeros((rows, channels), gains.dtype)
+    parts = [gains, shifts, conv_bias[None], blank(TAP_ROW - 19), taps, blank(RATE - TAP_ROW - TAPS)]
+    parts += [rate, maps[0], maps[1], blank(256 - TABLE)]
+    return jnp.concatenate(parts, axis=0).T
+
+
+def pack_bias(bias, place):
+    layers, count = bias.shape
+    hidden = 16 * CHUNK // layers
+    wide = lax.dynamic_update_slice(
+        jnp.zeros((layers, hidden), bias.dtype), bias, (0, place * count)
     )
-    rows = jnp.pad(rows, ((0, 256 - rows.shape[0]), (0, 0)))
-    return rows.T
-
-
-def unpack_small(small, devices, layers=2, ratio=4, states=STATES, width=TAPS):
-    rows = small.T
-    channels = rows.shape[1]
-    at = layers * ratio
-    bias = rows[:at].reshape((layers, ratio, devices, channels // devices))
-    bias = bias.transpose((0, 2, 1, 3)).reshape((layers, ratio * channels))
-    out = [bias, rows[at]]
-    at += 1
-    for count in (states, 2 * states, width, 6, 12):
-        out.append(rows[at : at + count])
-        at += count
-    out[3] = out[3].reshape((2, states, channels))
-    return tuple(out)
-
-
-def state_weights(log_rate, coupling):
-    log_decay = -jnp.exp(log_rate)
-    input_map = coupling[0] * jnp.sqrt(-jnp.expm1(2.0 * log_decay))
-    return jnp.exp(log_decay), input_map * coupling[1]
+    return wide.reshape((16, CHUNK))
+
+
+def unpack_table(table):
+    return (
+        table[0:6],
+        table[6:18],
+        table[18],
+        table[TAP_ROW : TAP_ROW + TAPS],
+        table[RATE:MAP_IN],
+        jnp.stack([table[MAP_IN:MAP_OUT], table[MAP_OUT:TABLE]]),
+    )
 
 
 def on_device(
@@ -1419,28 +1614,7 @@
     cotangent,
 ):
     devices = n_dp * n_fs
-    gathered = gather_all(
-        n_dp,
-        n_fs,
-        [
-            pack_small(ffn_bias_up, conv_out_bias, ssm_rate, ssm_map, conv_kernel, gains, shifts)[
-                None
-            ],
-            ffn_up,
-            ffn_down,
-            mix_in[None],
-            mix_out[None],
-            conv_in[None],
-            conv_out[None],
-        ],
-        1,
-    )
-    small, up0, up1, down0, down1, mixin, mixout, convin, convout = [
-        g.reshape((-1, g.shape[-1])) for g in gathered
-    ]
-    bias, conv_bias, rate, maps, taps, gain_set, shift_set = unpack_small(
-        small.astype(F32), devices
-    )
+    mine = lax.axis_index("dp") * n_fs + lax.axis_index("fsdp")
     frames_dev, channels = frames.shape
     tiles = frames_dev // TILE
     slot = jnp.arange(seq_offsets.shape[1], dtype=jnp.int32)
@@ -1448,29 +1622,59 @@
         slot < seq_counts[0]
     )
     flags = 1 - jnp.max(begins.astype(jnp.int32), axis=1)
-    vec = jnp.concatenate([gain_set, shift_set, conv_bias[None], jnp.zeros((5, channels), F32)])
-    taps = jnp.pad(taps, ((0, 1), (0, 0)))
-    (decay, coupling), weights_back = jax.vjp(state_weights, rate, maps)
-    h0, x1, u, v, y, gated, x2, p, hold, w, stat = front(
-        flags, frames, up0, down0, mixin, mixout, convin, bias, vec, taps, decay, coupling
+    small = pack_table(gains, shifts, conv_out_bias, conv_kernel, ssm_rate, ssm_map)
+    bias = pack_bias(ffn_bias_up, mine)
+    fused = small.shape[0] % 16 == 0
+    shards = [ffn_up, ffn_down, mix_in[None], mix_out[None], conv_in[None], conv_out[None]]
+    if fused:
+        small = jnp.concatenate([small, bias], axis=1)
+        made = front((n_dp, n_fs), flags, frames, [small[None]] + shards, 1)
+        _, up0, down0, mixin, mixout, convin, convout, up1, down1 = [
+            g.reshape((-1, g.shape[-1])) for g in made[15:]
+        ]
+        stat = made[10]
+    else:
+        got = gather_all(n_dp, n_fs, [small[None], bias[None]] + shards, 1)
+        small, _, up0, up1, down0, down1, mixin, mixout, convin, convout = [
+            g.reshape((-1, g.shape[-1])) for g in got
+        ]
+        made = front(
+            None,
+            flags,
+            frames,
+            [
+                up0,
+                down0,
+                mixin,
+                mixout,
+                convin,
+                small.astype(F32).T[:TABLE],
+                jnp.sum(got[1].astype(F32), axis=0),
+            ],
+        )
+        pool = exchange(n_dp, n_fs, made[10], frames_dev, 2, pool_kernel)
+        scale = lax.rsqrt(pool[1:2] / (frames_dev * devices) + EPSILON)
+        stat = jnp.concatenate([pool[0:1], scale, jnp.zeros((6, channels), F32)])
+    h0, x1, u, v, y, gated, x2, p, hold, w, _, table, bias, decay, coupling = made[:15]
+    result, gx3, gnb, gup1, gdown1, gconvout, gbias1, gvec1 = middle(
+        x2, w, cotangent, up1, down1, convout, bias, table, stat
     )
-    count_all = float(frames_dev * devices)
-    center = exchange(n_dp, n_fs, stat[0:1], 2) / devices
-    shift_from = stat[0:1] - center
-    spread = exchange(n_dp, n_fs, stat[8:9] + frames_dev * shift_from * shift_from, 3)
-    scale = lax.rsqrt(spread / count_all + EPSILON)
-    stat = jnp.concatenate([center, scale, jnp.zeros((6, channels), F32)])
-    result, gx3, gnb, gup1, gdown1, gconvout, gbias1, gvec1 = middle(
-        x2, w, cotangent, up1, down1, convout, bias, vec, stat
+    sums = exchange(n_dp, n_fs, gvec1, 1, 4, total_kernel)[6:8]
+    sums = sums * (table[5:6] / (frames_dev * devices))
+    stat = jnp.concatenate([stat[0:2], sums[1:2], sums[0:1], jnp.zeros((4, channels), F32)])
+    gg, gtaps = conv_back(flags, w, gnb, p, table, stat)
+    gx1, gconvin, gmixout, gmixin, gvec2, gmap, gdecay = back(
+        flags, gg, p, x2, gx3, gated, y, v, u, x1, hold, convin, mixout, mixin, table, decay, coupling
     )
-    sums = exchange(n_dp, n_fs, gvec1[6:8], 4) * (gain_set[5:6] / count_all)
-    stat = jnp.concatenate([center, scale, sums[1:2], sums[0:1], jnp.zeros((4, channels), F32)])
-    gg, gtaps = conv_back(flags, w, gnb, p, taps, vec, stat)
-    gx1, gconvin, gmixout, gmixin, gvec2, gmap, gdecay = back(
-        flags, gg, p, x2, gx3, gated, y, v, u, x1, hold, convin, mixout, mixin, vec, decay, coupling
-    )
-    gx, gup0, gdown0, gbias0, gvec3 = tail(frames, h0, gx1, up0, down0, vec)
-    rate_grad, map_grad = weights_back((gdecay, gmap))
+    gx, gup0, gdown0, gbias0, gvec3 = tail(frames, h0, gx1, up0, down0, table)
+
+    def weights_of(log_rate, maps):
+        log_decay = -jnp.exp(log_rate)
+        root = jnp.sqrt(-jnp.expm1(2.0 * log_decay))
+        return jnp.exp(log_decay), maps[0] * root * maps[1]
+
+    rate, maps = unpack_table(table)[4:]
+    rate_grad, map_grad = jax.vjp(weights_of, rate, maps)[1]((gdecay, gmap))
     gain_grad = jnp.stack([gvec3[1], gvec2[6], gvec2[2], gvec1[3], gvec1[0], gvec1[6]])
     shift_grad = jnp.stack(
         [
@@ -1488,37 +1692,42 @@
             gvec2[5],
         ]
     )
-    small_grad = pack_small(
-        jnp.concatenate([gbias0[:1], gbias1[:1]]),
-        gvec1[5],
-        rate_grad,
-        map_grad,
-        gtaps[:TAPS],
-        gain_grad,
-        shift_grad,
-        devices,
-    ).astype(BF16)
+    small_grad = pack_table(gain_grad, shift_grad, gvec1[5], gtaps[:TAPS], rate_grad, map_grad)
+    bias_grad = jnp.concatenate([gbias0[:1], gbias1[:1]]).reshape((16, CHUNK))
+    wide = lambda g: g.reshape((devices, g.shape[0] // devices, g.shape[1]))
     reduced = scatter_all(
         n_dp,
         n_fs,
-        [
-            g.reshape((devices, g.shape[0] // devices, g.shape[1]))
-            for g in (gup1, gdown1, gconvout, gconvin, gmixout, gmixin, gup0, gdown0, small_grad)
+        [wide(g) for g in (gup1, gdown1, gconvout, gconvin, gmixout, gmixin, gup0, gdown0)]
+        + [
+            wide(small_grad.astype(BF16)),
+            jnp.broadcast_to(bias_grad.astype(BF16), (devices, 16, CHUNK)),
         ],
         5,
     )
-    small = unpack_small(reduced[8], 1)
+    gains_grad, shifts_grad, conv_bias_grad, taps_grad, rate_grad, map_grad = unpack_table(
+        reduced[8].T
+    )
+    bias_grad = reduced[9].reshape((2, -1))
+    count = bias_grad.shape[1] // devices
+    bias_grad = lax.dynamic_slice(bias_grad, (0, mine * count), (2, count))
     return (
         result,
         gx,
         jnp.stack([reduced[6], reduced[0]]),
         jnp.stack([reduced[7], reduced[1]]),
-        small[0],
+        bias_grad,
         reduced[5],
         reduced[4],
         reduced[3],
         reduced[2],
-    ) + small[1:]
+        conv_bias_grad,
+        rate_grad,
+        map_grad,
+        taps_grad,
+        gains_grad,
+        shifts_grad,
+    )
 
 
 def solution(mesh):

time: 508 us -> 461 us (0.907)
  Pallas kernels: 455 us -> 414 us
    pallas_call x5 -> x2, Pallas kernels: 179 us -> 134 us  [the longest x1 124 us: front(): pl.pallas_call(partial(front_kernel, mesh_size), grid=(2 * tiles + 1,), i...]
where the time goes in v1:
time: 461 us; the launch traced here: 460 us
  Pallas kernels  414 us (90%)
  local copies, waits for them, and re-layouts  36.7 us (8%)
  other arithmetic  7.03 us (2%)
    pallas_call x1, Pallas kernels, front(): pl.pallas_call(partial(front_kernel, mesh_size), grid=(2 * tiles + 1,), i...  124 us
    pallas_call x1, Pallas kernels, back(): pl.pallas_call(back_kernel, grid_spec=pltpu.PrefetchScalarGridSpec(num_sc...  87 us
    pallas_call x1, Pallas kernels, scatter_all(): pl.pallas_call(partial(scatter_kernel, n_dp, n_fs, n), out_shape=[jax.Sha...  79.7 us
    pallas_call x1, Pallas kernels, middle(): pl.pallas_call(middle_kernel, grid=(tiles,), in_specs=[row(channels)] * 3...  62 us
    pallas_call x1, Pallas kernels, tail(): pl.pallas_call(tail_kernel, grid=(tiles,), in_specs=[row(channels), row(h...  34.8 us
    pallas_call x1, Pallas kernels, conv_back(): pl.pallas_call(conv_back_kernel, in_specs=[pl.BlockSpec(memory_space=pltp...  16.5 us
    pallas_call x1, Pallas kernels, exchange(): pl.pallas_call(partial(kernel, n_dp, n_fs, frames), out_shape=jax.ShapeDt...  10.7 us

profile of v1, /device:TPU:0, one launch (start us, length us, event | category | flops | bytes accessed | tf_op | source)
XLA Modules:
  0.0 459.6 jit_solution(14346628210792451216)
XLA Ops:
  0.7 0.8 dynamic_update_slice.3
  5.3 0.8 concatenate.18
  7.3 0.8 convert_reduce_fusion
  8.7 123.7 %front.1 = (bf16[1536,2048]{1,0:T(8,128)(2,1)}, f32[1536,512]{1,0:T(8,128)}, f32[1536,512]{1,0:T(8,128)}, bf16[1536,512]{1,0:T(8,128)(2,1)}, bf16[1536,512]{1,0:...) custom-call(s32[3]{0:T(128)} %broadcast_subtract_fusion.refs_0_.flag, ...), custom_call_target="tpu_custom_call" | custom-call | tf_op jit(solution)/shard_map/front/pallas_call | solution.py:957
  132.3 62.0 %middle.1 = (bf16[1536,512]{1,0:T(8,128)(2,1)}, f32[1536,512]{1,0:T(8,128)}, f32[1536,512]{1,0:T(8,128)}, bf16[512,2048]{1,0:T(8,128)(2,1)}, bf16[2048,512]{1,0:...) custom-call(f32[1536,512]{1,0:T(8,128)} %get-tuple-element.70.x2_ref, ...), custom_call_target="tpu_custom_call" | custom-call | tf_op jit(solution)/shard_map/middle/pallas_call | solution.py:1141
  194.4 10.7 %exchange_rows.1 = f32[8,512]{1,0:T(8,128)} custom-call(f32[8,512]{1,0:T(8,128)} %get-tuple-element.82.x_ref), custom_call_target="tpu_custom_call" | custom-call | tf_op jit(solution)/shard_map/exchange_rows/pallas_call | solution.py:457
  208.0 16.5 %conv_back.1 = (f32[1536,512]{1,0:T(8,128)}, f32[16,512]{1,0:T(8,128)}) custom-call(s32[3]{0:T(128)} %broadcast_subtract_fusion.refs_0_.flags_ref, f32[1536,512]{1,0:T(8,128)} %get-tuple-element.71.w_ref, f32[1536,512]{1,0:T(8,128)} %get-tuple-element.80.gnb_ref, bf16[1536,1024]{1,0:T(8,128)(2,1)} %get-tuple-element.81.p_ref, ...), custom_call_target="tpu_custom_call" | custom-call | tf_op jit(solution)/shard_map/conv_back/pallas_call | solution.py:1218
  224.5 87.0 %back.1 = (f32[1536,512]{1,0:T(8,128)}, bf16[512,1024]{1,0:T(8,128)(2,1)}, bf16[512,512]{1,0:T(8,128)(2,1)}, bf16[512,1024]{1,0:T(8,128)(2,1)}, f32[8,512]{1,0:T...) custom-call(s32[3]{0:T(128)} %broadcast_subtract_fusion.refs_0_.flags_ref, f32[1536,512]{1,0:T(8,128)} %get-tuple-element.83.gg_ref, ...), custom_call_target="tpu_custom_call" | custom-call | tf_op jit(solution)/shard_map/back/pallas_call | solution.py:1427
  311.6 34.8 %tail.1 = (f32[1536,512]{1,0:T(8,128)}, bf16[512,2048]{1,0:T(8,128)(2,1)}, bf16[2048,512]{1,0:T(8,128)(2,1)}, f32[8,2048]{1,0:T(8,128)}, f32[8,512]{1,0:T(8,128)}) custom-call(bf16[1536,512]{1,0:T(8,128)(2,1)} %x_ref.1, bf16[1536,2048]{1,0:T(8,128)(2,1)} %get-tuple-element.79.h_ref, f32[1536,512]{1,0:T(8,128)} %get-tuple-element.96.gx1_ref, ...), custom_call_target="tpu_custom_call" | custom-call | tf_op jit(solution)/shard_map/tail/pallas_call | solution.py:1544
  346.4 0.9 slice.245
  347.3 0.8 slice.244
  349.5 0.8 copy.100
  350.3 0.8 copy.106
  351.1 0.8 copy.94
  351.9 0.8 copy.101
  352.8 0.8 copy.102
  353.6 0.8 copy.108
  354.4 0.8 copy.110
  355.2 0.8 copy.95
  356.0 0.8 copy.96
  356.8 0.8 copy.109
  358.5 0.8 copy.103
  359.3 0.8 copy.104
  360.1 0.8 copy.105
  360.9 0.8 copy.107
  361.7 0.8 copy.111
  362.5 0.8 copy.97
  363.4 0.8 copy.98
  364.2 0.8 copy.99
  367.0 3.1 concatenate.21
  370.2 1.0 copy-done.3
  371.2 79.7 %scatter_gradients.1 = (f32[16,2048]{1,0:T(8,128)S(1)}, f32[64,512]{1,0:T(8,128)S(1)}, f32[16,512]{1,0:T(8,128)S(1)}, f32[16,1024]{1,0:T(8,128)S(1)}, f32[16,512...) custom-call(bf16[32,16,2048]{2,1,0:T(8,128)(2,1)} %bitcast.68, ...), custom_call_target="tpu_custom_call" | custom-call | tf_op jit(solution)/shard_map/scatter_gradients/pallas_call | solution.py:357
  (78 shorter events, 20.8 us)
Async XLA Ops:
  311.6 36.6 %copy-start.4 = (f32[136,512]{1,0:T(8,128)S(1)}, f32[136,512]{1,0:T(8,128)}, u32[]{:S(2)}) copy-start(f32[136,512]{1,0:T(8,128)} %get-tuple-element.76.vec_ref) | copy-start | bytes 835588
  311.6 36.6 %copy-start.5 = (f32[32,512]{1,0:T(8,128)S(1)}, f32[32,512]{1,0:T(8,128)}, u32[]{:S(2)}) copy-start(f32[32,512]{1,0:T(8,128)} %get-tuple-element.112) | copy-start | bytes 196612
  311.6 36.6 %copy-start.6 = (f32[32,512]{1,0:T(8,128)S(1)}, f32[32,512]{1,0:T(8,128)}, u32[]{:S(2)}) copy-start(f32[32,512]{1,0:T(8,128)} %get-tuple-element.111) | copy-start | bytes 196612
  346.4 5.5 %copy-start.8 = (f32[8,512]{1,0:T(8,128)S(1)}, f32[8,512]{1,0:T(8,128)}, u32[]{:S(2)}) copy-start(f32[8,512]{1,0:T(8,128)} %get-tuple-element.109) | copy-start | bytes 49156
  346.4 11.3 %copy-start.9 = (f32[16,512]{1,0:T(8,128)S(1)}, f32[16,512]{1,0:T(8,128)}, u32[]{:S(2)}) copy-start(f32[16,512]{1,0:T(8,128)} %get-tuple-element.110) | copy-start | bytes 98308
  346.4 12.0 %copy-start.7 = (f32[8,512]{1,0:T(8,128)S(1)}, f32[8,512]{1,0:T(8,128)}, u32[]{:S(2)}) copy-start(f32[8,512]{1,0:T(8,128)} %get-tuple-element.82.x_ref) | copy-start | bytes 49156
  363.4 6.8 %copy-start = (bf16[512,1024]{1,0:T(8,128)(2,1)S(1)}, bf16[512,1024]{1,0:T(8,128)(2,1)}, u32[]{:S(2)}) copy-start(bf16[512,1024]{1,0:T(8,128)(2,1)} %get-tuple-element.103) | copy-start | bytes 3145732
  363.4 6.8 %copy-start.1 = (bf16[512,1024]{1,0:T(8,128)(2,1)S(1)}, bf16[512,1024]{1,0:T(8,128)(2,1)}, u32[]{:S(2)}) copy-start(bf16[512,1024]{1,0:T(8,128)(2,1)} %get-tuple-element.105) | copy-start | bytes 3145732
  363.4 6.8 %copy-start.2 = (bf16[512,512]{1,0:T(8,128)(2,1)S(1)}, bf16[512,512]{1,0:T(8,128)(2,1)}, u32[]{:S(2)}) copy-start(bf16[512,512]{1,0:T(8,128)(2,1)} %get-tuple-element.102) | copy-start | bytes 1572868
  370.2 1.0 copy-start.3

commit v2 on v1

--- a/solution.py
+++ b/solution.py
@@ -368,28 +368,41 @@
     )(*arrays)
 
 
-def swap_rows(axis, place, count, buffer, send_sem, recv_sem):
-    def make(step):
-        return pltpu.make_async_remote_copy(
-            src_ref=buffer.at[0],
-            dst_ref=buffer.at[step],
-            send_sem=send_sem.at[step],
-            recv_sem=recv_sem.at[step],
-            device_id={axis: lax.rem(place + step, count)},
-            device_id_type=MESH,
-        )
-
+def swap_copy(axis, place, count, buffer, send_sem, recv_sem, step):
+    return pltpu.make_async_remote_copy(
+        src_ref=buffer.at[0],
+        dst_ref=buffer.at[step],
+        send_sem=send_sem.at[step],
+        recv_sem=recv_sem.at[step],
+        device_id={axis: lax.rem(place + step, count)},
+        device_id_type=MESH,
+    )
+
+
+def swap_start(axis, place, count, *rest):
     for step in range(1, count):
-        make(step).start()
+        swap_copy(axis, place, count, *rest, step).start()
+
+
+def swap_wait(axis, place, count, *rest):
     for step in range(1, count):
-        make(step).wait_recv()
+        swap_copy(axis, place, count, *rest, step).wait_recv()
     for step in range(1, count):
-        make(step).wait_send()
-
-
-def sum_over(x, dp, fs, n_dp, n_fs, octet, line, send_sem, recv_sem):
+        swap_copy(axis, place, count, *rest, step).wait_send()
+
+
+def swap_rows(*args):
+    swap_start(*args)
+    swap_wait(*args)
+
+
+def sum_over(x, dp, fs, n_dp, n_fs, octet, line, send_sem, recv_sem, between=None):
+    first = ("dp", dp, n_dp, octet, send_sem.at[0], recv_sem.at[0])
     octet[0] = x
-    swap_rows("dp", dp, n_dp, octet, send_sem.at[0], recv_sem.at[0])
+    swap_start(*first)
+    if between is not None:
+        between()
+    swap_wait(*first)
     total = octet[0]
     for step in range(1, n_dp):
         total = total + octet[step]
@@ -874,7 +887,7 @@
 
 def whole(shape):
     zeros = (0,) * len(shape)
-    return pl.BlockSpec(shape, lambda *_: zeros)
+    return pl.BlockSpec(shape, lambda *_: zeros, pipeline_mode=pl.Buffered(1))
 
 
 def params(collective_id=None):
@@ -983,7 +996,17 @@
     lax.fori_loop(0, hidden // CHUNK, chunk, 0)
 
 
+def convert_rows(out, acc, step=64):
+    def run(at, _):
+        rows = pl.ds(pl.multiple_of(at * step, step), step)
+        out[rows, :] = acc[rows, :].astype(BF16)
+        return 0
+
+    lax.fori_loop(0, acc.shape[0] // step, run, 0)
+
+
 def middle_kernel(
+    mesh_size,
     x2_ref,
     w_ref,
     cot_ref,
@@ -1001,6 +1024,7 @@
     gconvout_out,
     gbias_out,
     gvec_out,
+    stat_out,
     up_acc,
     down_acc,
     convout_acc,
@@ -1013,10 +1037,19 @@
     grad_scr,
     sum_scr,
     x3_scr,
+    *swap,
 ):
     at = pl.program_id(0)
     tiles = pl.num_programs(0)
     channels = x2_ref.shape[1]
+    if mesh_size is not None:
+        n_dp, n_fs = mesh_size
+        dp, fs = lax.axis_index("dp"), lax.axis_index("fsdp")
+
+        @pl.when(at == 0)
+        def _():
+            greet(dp, fs, n_dp, n_fs)
+
     hidden = up_ref.shape[1]
     gain = lambda k: vec_ref[k : k + 1, :]
     shift = lambda k: vec_ref[6 + k : 7 + k, :]
@@ -1114,15 +1147,28 @@
 
     @pl.when(at == tiles - 1)
     def _():
-        by_rows(lambda rows: gup_out.__setitem__((rows, slice(None)), up_acc[rows, :].astype(BF16)), channels)
-        by_rows(lambda rows: gdown_out.__setitem__((rows, slice(None)), down_acc[rows, :].astype(BF16)), hidden)
-        by_rows(lambda rows: gconvout_out.__setitem__((rows, slice(None)), convout_acc[rows, :].astype(BF16)), channels)
-        gbias_out[...] = jnp.broadcast_to(jnp.sum(bias_acc[...], axis=0, keepdims=True), gbias_out.shape)
         for k in range(8):
             gvec_out[k : k + 1, :] = jnp.sum(vec_acc[k], axis=0, keepdims=True)
 
-
-def middle(x2, w, cot, up, down, convout, bias, vec, stat):
+        def convert():
+            convert_rows(gup_out, up_acc)
+            convert_rows(gdown_out, down_acc)
+            convert_rows(gconvout_out, convout_acc)
+            gbias_out[...] = jnp.broadcast_to(
+                jnp.sum(bias_acc[...], axis=0, keepdims=True), gbias_out.shape
+            )
+
+        stat_out[...] = stat_ref[...]
+        if mesh_size is None:
+            convert()
+        else:
+            total = sum_over(gvec_out[...], dp, fs, n_dp, n_fs, *swap, between=convert)
+            share = gain(5) * (1.0 / (TILE * tiles * n_dp * n_fs))
+            stat_out[2:3, :] = total[7:8, :] * share
+            stat_out[3:4, :] = total[6:7, :] * share
+
+
+def middle(mesh_size, x2, w, cot, up, down, convout, bias, vec, stat, collective_id=None):
     frames, channels = x2.shape
     hidden = up.shape[1]
     tiles = frames // TILE
@@ -1137,9 +1183,11 @@
         jax.ShapeDtypeStruct(convout.shape, BF16),
         jax.ShapeDtypeStruct((8, hidden), F32),
         jax.ShapeDtypeStruct((8, channels), F32),
+        jax.ShapeDtypeStruct((8, channels), F32),
     ]
+    swap = [] if mesh_size is None else swap_scratch(*mesh_size, channels)
     return pl.pallas_call(
-        middle_kernel,
+        partial(middle_kernel, mesh_size),
         grid=(tiles,),
         in_specs=[row(channels)] * 3
         + [whole(a.shape) for a in (up, down, convout, bias, vec, stat)],
@@ -1158,409 +1206,694 @@
             pltpu.VMEM((TILE, channels), BF16),
             pltpu.VMEM((TILE, channels), F32),
             pltpu.VMEM((TILE, channels), F32),
-        ],
-        compiler_params=params(),
+        ]
+        + swap,
+        compiler_params=params(collective_id),
         name="middle",
     )(x2, w, cot, up, down, convout, bias, vec, stat)
 
 
-def conv_back_kernel(flags_ref, w_ref, gnb_ref, p_ref, vec_ref, stat_ref, gg_ref, gtaps_ref, padded, gpad):
-    frames, channels = w_ref.shape
-    tiles = frames // TILE
+def back_kernel(mesh_size, *refs):
+    fused = mesh_size is not None
+    refs = list(refs)
+    take = lambda count: [refs.pop(0) for _ in range(count)]
+    (
+        flags_ref,
+        w_ref,
+        gnb_ref,
+        p_all,
+        x2_ref,
+        gx3_ref,
+        gated_ref,
+        y_ref,
+        v_ref,
+        u_ref,
+        x1_ref,
+        hold_ref,
+        convin_ref,
+        mixout_ref,
+        mixin_ref,
+        vec_ref,
+        stat_ref,
+        decay_ref,
+        map_ref,
+    ) = take(19)
+    sources = take(3) if fused else []
+    (
+        gx1_ref,
+        gconvin_out,
+        gmixout_out,
+        gmixin_out,
+        gvec_out,
+        gtaps_ref,
+        gmap_out,
+        gdecay_out,
+    ) = take(8)
+    reduced = take(3) if fused else []
+    (
+        convin_acc,
+        mixout_acc,
+        mixin_acc,
+        vec_acc,
+        map_acc,
+        decay_acc,
+        adj_scr,
+        track,
+        low_scr,
+        wide_scr,
+        sum_scr,
+        gy_scr,
+        padded,
+        gpad,
+    ) = take(14)
+    step = pl.program_id(0)
+    tiles = pl.num_programs(0) - 1
+    at = tiles - jnp.maximum(step, 1)
+    channels = x2_ref.shape[1]
+    lanes = channels // 128
     pitch = TILE + 2 * REACH
-    center, scale = stat_ref[0:1, :], stat_ref[1:2, :]
-    plain, cross = stat_ref[2:3, :], stat_ref[3:4, :]
-
-    for tile in range(tiles):
-
-        def fill(at, _, tile=tile):
-            rows = pl.ds(pl.multiple_of(tile * TILE + at * 64, 64), 64)
-            place = pl.ds(pl.multiple_of(tile * pitch + REACH + at * 64, 8), 64)
+    gain = lambda k: vec_ref[k : k + 1, :]
+    shift = lambda k: vec_ref[6 + k : 7 + k, :]
+    left, right = slice(0, channels), slice(channels, 2 * channels)
+    if fused:
+        n_dp, n_fs = mesh_size
+        scratch = take(12)
+        dp, fs = lax.axis_index("dp"), lax.axis_index("fsdp")
+
+        def emit(chunk, total):
+            reduced[chunk][...] = total
+
+        plans, sends = scatter_plan(dp, fs, n_dp, n_fs, sources, emit, scratch, *take(3))
+        order = waves(plans)
+        points = [(0, 0), (0, 1), (0, 2), (1, 0), (1, 3), (1, 4), (2, 0), (2, 3), (2, 4)]
+        points += [(tiles, 4)] * (len(order) - len(points))
+
+    def progress(point):
+        if not fused:
+            return
+        for wave, place in zip(order, points):
+            if place[1] == point:
+
+                @pl.when(step == place[0])
+                def _(wave=wave):
+                    for stage in wave:
+                        stage()
+
+    @pl.when(step == 0)
+    def _():
+        for ref in (convin_acc, mixout_acc, mixin_acc, vec_acc, map_acc, decay_acc, adj_scr):
+            ref[...] = jnp.zeros_like(ref)
+        if fused:
+            greet(dp, fs, n_dp, n_fs)
+
+    progress(0)
+
+    @pl.when(step == 0)
+    def _():
+        center, scale = stat_ref[0:1, :], stat_ref[1:2, :]
+        plain, cross = stat_ref[2:3, :], stat_ref[3:4, :]
+        per = TILE // 64
+
+        def fill(index, _):
+            tile, inner = index // per, index % per
+            rows = pl.ds(pl.multiple_of(index * 64, 64), 64)
+            place = pl.ds(pl.multiple_of(tile * pitch + REACH + inner * 64, 8), 64)
             e = (w_ref[rows, :] - center) * scale
-            d = gnb_ref[rows, :] * vec_ref[5:6, :]
+            d = gnb_ref[rows, :] * gain(5)
             gw = scale * (d - plain - e * cross)
-            g = p_ref[rows, :channels].astype(F32) * sigmoid(p_ref[rows, channels:].astype(F32))
-            for lane in range(channels // 128):
+            g = p_all[rows, left].astype(F32) * sigmoid(p_all[rows, right].astype(F32))
+            for lane in range(lanes):
                 cols = slice(lane * 128, lane * 128 + 128)
                 padded[lane, place, :] = gw[:, cols]
                 gpad[lane, place, :] = g[:, cols]
             return 0
 
-        lax.fori_loop(0, TILE // 64, fill, 0)
-    fill_halo(padded, flags_ref, tiles)
-    fill_halo(gpad, flags_ref, tiles)
-
-    def store(lane, row, base, total):
-        gg_ref[pl.ds(pl.multiple_of(row, 64), 64), lane * 128 : lane * 128 + 128] = total
-
-    taps_over(padded, vec_ref, store, tiles, True)
-    block = 64
-    per = TILE // block
-    for lane in range(channels // 128):
-
-        def corr(at, sums, lane=lane):
-            base = (at // per) * pitch + (at % per) * block
-            here = padded[lane, pl.ds(pl.multiple_of(base + REACH, 8), block), :]
-            return tuple(
-                s + fold8(here * gpad[lane, pl.ds(base + REACH + k - TAPS // 2, block), :])
-                for k, s in enumerate(sums)
-            )
-
-        sums = lax.fori_loop(0, tiles * per, corr, (jnp.zeros((8, 128), F32),) * TAPS)
-        for k in range(TAPS):
-            gtaps_ref[k : k + 1, lane * 128 : lane * 128 + 128] = jnp.sum(sums[k], axis=0, keepdims=True)
-
-
-def conv_back(flags, w, gnb, p, vec, stat):
-    frames, channels = w.shape
-    tiles = frames // TILE
-    pad = pltpu.VMEM((channels // 128, tiles * (TILE + 2 * REACH), 128), F32)
-    return pl.pallas_call(
-        conv_back_kernel,
-        in_specs=[pl.BlockSpec(memory_space=pltpu.SMEM)] + [pl.BlockSpec(memory_space=pltpu.VMEM)] * 5,
-        out_specs=[pl.BlockSpec(memory_space=pltpu.VMEM)] * 2,
-        out_shape=[
-            jax.ShapeDtypeStruct((frames, channels), F32),
-            jax.ShapeDtypeStruct((16, channels), F32),
-        ],
-        scratch_shapes=[pad, pad],
-        compiler_params=pltpu.CompilerParams(vmem_limit_bytes=VMEM_LIMIT),
-        name="conv_back",
-    )(flags, w, gnb, p, vec, stat)
-
-
-def back_kernel(
-    flags_ref,
-    gg_ref,
-    p_ref,
-    x2_ref,
-    gx3_ref,
-    gated_ref,
-    y_ref,
-    v_ref,
-    u_ref,
-    x1_ref,
-    hold_ref,
-    convin_ref,
-    mixout_ref,
-    mixin_ref,
-    vec_ref,
-    decay_ref,
-    map_ref,
-    gx1_ref,
-    gconvin_out,
-    gmixout_out,
-    gmixin_out,
-    gvec_out,
-    gmap_out,
-    gdecay_out,
-    convin_acc,
-    mixout_acc,
-    mixin_acc,
-    vec_acc,
-    map_acc,
-    decay_acc,
-    adj_scr,
-    track,
-    low_scr,
-    wide_scr,
-    sum_scr,
-    gy_scr,
-):
-    step = pl.program_id(0)
-    tiles = pl.num_programs(0)
-    at = tiles - 1 - step
-    channels = x2_ref.shape[1]
-    lanes = channels // 128
-    gain = lambda k: vec_ref[k : k + 1, :]
-    shift = lambda k: vec_ref[6 + k : 7 + k, :]
+        lax.fori_loop(0, tiles * per, fill, 0)
+        fill_halo(padded, flags_ref, tiles)
+        fill_halo(gpad, flags_ref, tiles)
+
+    progress(1)
 
     @pl.when(step == 0)
     def _():
-        for ref in (convin_acc, mixout_acc, mixin_acc, vec_acc, map_acc, decay_acc, adj_scr):
-            ref[...] = jnp.zeros_like(ref)
-
-    left, right = slice(0, channels), slice(channels, 2 * channels)
-
-    def first(rows):
-        grad = gg_ref[rows, :]
-        sig = sigmoid(p_ref[rows, right].astype(F32))
-        gl = (grad * sig).astype(BF16)
-        gr = (grad * p_ref[rows, left].astype(F32) * (sig * (1.0 - sig))).astype(BF16)
-        wide_scr[rows, left] = gl
-        wide_scr[rows, right] = gr
-        vec_acc[0] += fold8(gl.astype(F32))
-        vec_acc[1] += fold8(gr.astype(F32))
-        e, _ = norm_parts(x2_ref[rows, :])
-        low_scr[rows, :] = (e * gain(2) + shift(2)).astype(BF16)
-
-    by_rows(first)
-    turned = low_scr[...].T
-    convin_acc[...] += dot_nn(turned, wide_scr[...])
-    sum_scr[...] = dot_nt(wide_scr[...], convin_ref[...])
-
-    def second(rows):
-        e, inv = norm_parts(x2_ref[rows, :])
-        grad = sum_scr[rows, :]
-        vec_acc[2] += fold8(grad * e)
-        vec_acc[3] += fold8(grad)
-        gx2 = gx3_ref[rows, :] + norm_back(grad, e, inv, gain(2))
-        gx1_ref[rows, :] = gx2
-        low = gx2.astype(BF16)
-        low_scr[rows, :] = low
-        vec_acc[4] += fold8(low.astype(F32))
-
-    by_rows(second)
-    mixout_acc[...] += dot_tn(gated_ref[...], low_scr[...])
-    sum_scr[...] = dot_nt(low_scr[...], mixout_ref[...])
-
-    def third(rows):
-        grad = sum_scr[rows, :]
-        v = v_ref[rows, :].astype(F32)
-        sig = sigmoid(v)
-        swish = v * sig
-        gy = grad * swish
-        gy_scr[rows, :] = gy
-        wide_scr[rows, right] = (
-            grad * y_ref[rows, :].astype(F32) * (sig * (1.0 + v - swish))
-        ).astype(BF16)
-        vec_acc[5] += fold8(gy * u_ref[rows, :])
-
-    by_rows(third)
-    low_half = half_masks(128)
-    later = jnp.minimum(at + 1, tiles - 1)
-    adj_scr[...] = adj_scr[...] * flags_ref[later].astype(F32)
-
-    def span_back(index, _):
-        span = TILE // SPAN - 1 - index
-        base = pl.multiple_of(span * SPAN, SPAN)
+        block = 64
+        per = TILE // block
+        gtaps_ref[...] = jnp.zeros_like(gtaps_ref)
         for lane in range(lanes):
-            cols = slice(lane * 128, lane * 128 + 128)
-            decay = decay_ref[:, cols]
-
-            def forward(block, state):
-                drive = u_ref[pl.ds(pl.multiple_of(base + block * 8, 8), 8), cols]
-                for j in range(8):
-                    track[block * 8 + j, :, cols] = state
-                    state = decay * state + jnp.broadcast_to(drive[j : j + 1, :], (STATES, 128))
-                return state
-
-            lax.fori_loop(0, SPAN // 8, forward, hold_ref[span, :, cols])
-
-        def backward(index, _):
-            block = SPAN // 8 - 1 - index
-            start = pl.multiple_of(base + block * 8, 8)
+
+            def corr(index, sums, lane=lane):
+                base = (index // per) * pitch + (index % per) * block
+                here = padded[lane, pl.ds(pl.multiple_of(base + REACH, 8), block), :]
+                return tuple(
+                    s + fold8(here * gpad[lane, pl.ds(base + REACH + k - TAPS // 2, block), :])
+                    for k, s in enumerate(sums)
+                )
+
+            sums = lax.fori_loop(0, tiles * per, corr, (jnp.zeros((8, 128), F32),) * TAPS)
+            for k in range(TAPS):
+                gtaps_ref[k : k + 1, lane * 128 : lane * 128 + 128] = jnp.sum(
+                    sums[k], axis=0, keepdims=True
+                )
+
+        def store(lane, row, base, total):
+            gpad[lane, pl.ds(pl.multiple_of(base + REACH, 8), 64), :] = total
+
+        taps_over(padded, vec_ref, store, tiles, True)
+
+    progress(2)
+
+    def back_tile():
+        def first(rows):
+            place = pl.ds(pl.multiple_of(at * pitch + REACH + rows.start, 8), ROWS)
+            here = pl.ds(pl.multiple_of(at * TILE + rows.start, ROWS), ROWS)
+            grad = jnp.concatenate([gpad[lane, place, :] for lane in range(lanes)], axis=1)
+            sig = sigmoid(p_all[here, right].astype(F32))
+            gl = (grad * sig).astype(BF16)
+            gr = (grad * p_all[here, left].astype(F32) * (sig * (1.0 - sig))).astype(BF16)
+            wide_scr[rows, left] = gl
+            wide_scr[rows, right] = gr
+            vec_acc[0] += fold8(gl.astype(F32))
+            vec_acc[1] += fold8(gr.astype(F32))
+            e, _ = norm_parts(x2_ref[rows, :])
+            low_scr[rows, :] = (e * gain(2) + shift(2)).astype(BF16)
+
+        by_rows(first)
+        turned = low_scr[...].T
+        convin_acc[...] += dot_nn(turned, wide_scr[...])
+        sum_scr[...] = dot_nt(wide_scr[...], convin_ref[...])
+
+        def second(rows):
+            e, inv = norm_parts(x2_ref[rows, :])
+            grad = sum_scr[rows, :]
+            vec_acc[2] += fold8(grad * e)
+            vec_acc[3] += fold8(grad)
+            gx2 = gx3_ref[rows, :] + norm_back(grad, e, inv, gain(2))
+            gx1_ref[rows, :] = gx2
+            low = gx2.astype(BF16)
+            low_scr[rows, :] = low
+            vec_acc[4] += fold8(low.astype(F32))
+
+        by_rows(second)
+        progress(3)
+        mixout_acc[...] += dot_tn(gated_ref[...], low_scr[...])
+        sum_scr[...] = dot_nt(low_scr[...], mixout_ref[...])
+
+        def third(rows):
+            grad = sum_scr[rows, :]
+            v = v_ref[rows, :].astype(F32)
+            sig = sigmoid(v)
+            swish = v * sig
+            gy = grad * swish
+            gy_scr[rows, :] = gy
+            wide_scr[rows, right] = (
+                grad * y_ref[rows, :].astype(F32) * (sig * (1.0 + v - swish))
+            ).astype(BF16)
+            vec_acc[5] += fold8(gy * u_ref[rows, :])
+
+        by_rows(third)
+        progress(4)
+        low_half = half_masks(128)
+        later = jnp.minimum(at + 1, tiles - 1)
+        adj_scr[...] = adj_scr[...] * flags_ref[later].astype(F32)
+
+        def span_back(index, _):
+            span = TILE // SPAN - 1 - index
+            base = pl.multiple_of(span * SPAN, SPAN)
             for lane in range(lanes):
                 cols = slice(lane * 128, lane * 128 + 128)
                 decay = decay_ref[:, cols]
-                maps = map_ref[:, cols]
-                adj = adj_scr[:, cols]
-                drive = u_ref[pl.ds(start, 8), cols]
-                grad = gy_scr[pl.ds(start, 8), cols]
-                gmap = map_acc[:, cols]
-                gdecay = decay_acc[:, cols]
-                parts = [None] * 8
-                for j in range(7, -1, -1):
-                    adj = decay * adj + jnp.broadcast_to(grad[j : j + 1, :], (STATES, 128))
-                    parts[j] = fold_states(maps * adj)
-                    gmap = gmap + adj * jnp.broadcast_to(drive[j : j + 1, :], (STATES, 128))
-                    gdecay = gdecay + adj * track[block * 8 + j, :, cols]
-                adj_scr[:, cols] = adj
-                map_acc[:, cols] = gmap
-                decay_acc[:, cols] = gdecay
-                sum_scr[pl.ds(start, 8), cols] = merge_rows(parts, low_half)
+
+                def forward(block, state):
+                    drive = u_ref[pl.ds(pl.multiple_of(base + block * 8, 8), 8), cols]
+                    for j in range(8):
+                        track[block * 8 + j, :, cols] = state
+                        state = decay * state + jnp.broadcast_to(drive[j : j + 1, :], (STATES, 128))
+                    return state
+
+                lax.fori_loop(0, SPAN // 8, forward, hold_ref[span, :, cols])
+
+            def backward(index, _):
+                block = SPAN // 8 - 1 - index
+                start = pl.multiple_of(base + block * 8, 8)
+                for lane in range(lanes):
+                    cols = slice(lane * 128, lane * 128 + 128)
+                    decay = decay_ref[:, cols]
+                    maps = map_ref[:, cols]
+                    adj = adj_scr[:, cols]
+                    drive = u_ref[pl.ds(start, 8), cols]
+                    grad = gy_scr[pl.ds(start, 8), cols]
+                    gmap = map_acc[:, cols]
+                    gdecay = decay_acc[:, cols]
+                    parts = [None] * 8
+                    for j in range(7, -1, -1):
+                        adj = decay * adj + jnp.broadcast_to(grad[j : j + 1, :], (STATES, 128))
+                        parts[j] = fold_states(maps * adj)
+                        gmap = gmap + adj * jnp.broadcast_to(drive[j : j + 1, :], (STATES, 128))
+                        gdecay = gdecay + adj * track[block * 8 + j, :, cols]
+                    adj_scr[:, cols] = adj
+                    map_acc[:, cols] = gmap
+                    decay_acc[:, cols] = gdecay
+                    sum_scr[pl.ds(start, 8), cols] = merge_rows(parts, low_half)
+                return 0
+
+            lax.fori_loop(0, SPAN // 8, backward, 0)
             return 0
 
-        lax.fori_loop(0, SPAN // 8, backward, 0)
-        return 0
-
-    lax.fori_loop(0, TILE // SPAN, span_back, 0)
-
-    def fourth(rows):
-        gu = sum_scr[rows, :] + shift(11) * gy_scr[rows, :]
-        wide_scr[rows, left] = gu.astype(BF16)
-        e, _ = norm_parts(x1_ref[rows, :])
-        low_scr[rows, :] = (e * gain(1) + shift(1)).astype(BF16)
-
-    by_rows(fourth)
-    turned = low_scr[...].T
-    mixin_acc[...] += dot_nn(turned, wide_scr[...])
-    sum_scr[...] = dot_nt(wide_scr[...], mixin_ref[...])
-
-    def fifth(rows):
-        e, inv = norm_parts(x1_ref[rows, :])
-        grad = sum_scr[rows, :]
-        vec_acc[6] += fold8(grad * e)
-        vec_acc[7] += fold8(grad)
-        gx1_ref[rows, :] = gx1_ref[rows, :] + norm_back(grad, e, inv, gain(1))
-
-    by_rows(fifth)
-
-    @pl.when(step == tiles - 1)
+        lax.fori_loop(0, TILE // SPAN, span_back, 0)
+
+        def fourth(rows):
+            gu = sum_scr[rows, :] + shift(11) * gy_scr[rows, :]
+            wide_scr[rows, left] = gu.astype(BF16)
+            e, _ = norm_parts(x1_ref[rows, :])
+            low_scr[rows, :] = (e * gain(1) + shift(1)).astype(BF16)
+
+        by_rows(fourth)
+        turned = low_scr[...].T
+        mixin_acc[...] += dot_nn(turned, wide_scr[...])
+        sum_scr[...] = dot_nt(wide_scr[...], mixin_ref[...])
+
+        def fifth(rows):
+            e, inv = norm_parts(x1_ref[rows, :])
+            grad = sum_scr[rows, :]
+            vec_acc[6] += fold8(grad * e)
+            vec_acc[7] += fold8(grad)
+            gx1_ref[rows, :] = gx1_ref[rows, :] + norm_back(grad, e, inv, gain(1))
+
+        by_rows(fifth)
+
+        @pl.when(step == tiles)
+        def _():
+            convert_rows(gconvin_out, convin_acc)
+            convert_rows(gmixout_out, mixout_acc)
+            convert_rows(gmixin_out, mixin_acc)
+            for k in range(8):
+                gvec_out[k : k + 1, :] = jnp.sum(vec_acc[k], axis=0, keepdims=True)
+            gmap_out[...] = map_acc[...]
+            gdecay_out[...] = decay_acc[...] * map_ref[...]
+
+    @pl.when(step > 0)
     def _():
-        for out, acc in ((gconvin_out, convin_acc), (gmixout_out, mixout_acc), (gmixin_out, mixin_acc)):
-            by_rows(
-                lambda rows, out=out, acc=acc: out.__setitem__((rows, slice(None)), acc[rows, :].astype(BF16)),
-                channels,
-            )
-        for k in range(8):
-            gvec_out[k : k + 1, :] = jnp.sum(vec_acc[k], axis=0, keepdims=True)
-        gmap_out[...] = map_acc[...]
-        gdecay_out[...] = decay_acc[...] * map_ref[...]
-
-
-def back(flags, gg, p, x2, gx3, gated, y, v, u, x1, hold, convin, mixout, mixin, vec, decay, maps):
+        back_tile()
+
+    if fused:
+
+        @pl.when(step == tiles)
+        def _():
+            for wait in sends:
+                wait()
+
+
+def back(mesh_size, flags, w, gnb, p, x2, gx3, gated, y, v, u, x1, hold, convin, mixout, mixin, vec, stat, decay, maps, grads=(), collective_id=None):
+    fused = mesh_size is not None
     frames, channels = x2.shape
     tiles = frames // TILE
-    row = lambda width: pl.BlockSpec((TILE, width), lambda i, *_: (tiles - 1 - i, 0))
+    place = lambda i: tiles - jnp.maximum(i, 1)
+    row = lambda width: pl.BlockSpec((TILE, width), lambda i: (place(i), 0))
     spans = TILE // SPAN
     big = lambda a: pltpu.VMEM(a.shape, F32)
+    state = jax.ShapeDtypeStruct((STATES, channels), F32)
     shapes = [
         jax.ShapeDtypeStruct((frames, channels), F32),
         jax.ShapeDtypeStruct(convin.shape, BF16),
         jax.ShapeDtypeStruct(mixout.shape, BF16),
         jax.ShapeDtypeStruct(mixin.shape, BF16),
         jax.ShapeDtypeStruct((8, channels), F32),
-        jax.ShapeDtypeStruct((STATES, channels), F32),
-        jax.ShapeDtypeStruct((STATES, channels), F32),
+        jax.ShapeDtypeStruct((16, channels), F32),
+        state,
+        state,
     ]
+    pad = pltpu.VMEM((channels // 128, tiles * (TILE + 2 * REACH), 128), F32)
+    scratch = [
+        big(convin),
+        big(mixout),
+        big(mixin),
+        pltpu.VMEM((8, 8, channels), F32),
+        pltpu.VMEM((STATES, channels), F32),
+        pltpu.VMEM((STATES, channels), F32),
+        pltpu.VMEM((STATES, channels), F32),
+        pltpu.VMEM((SPAN, STATES, channels), F32),
+        pltpu.VMEM((TILE, channels), BF16),
+        pltpu.VMEM((TILE, 2 * channels), BF16),
+        pltpu.VMEM((TILE, channels), F32),
+        pltpu.VMEM((TILE, channels), F32),
+        pad,
+        pad,
+    ]
+    if fused:
+        tails = [g.shape[1:] for g in grads]
+        shapes += [jax.ShapeDtypeStruct(t, F32) for t in tails]
+        scratch += scatter_scratch(*mesh_size, tails) + scatter_sems(*mesh_size, len(tails))
     return pl.pallas_call(
-        back_kernel,
-        grid_spec=pltpu.PrefetchScalarGridSpec(
-            num_scalar_prefetch=1,
-            grid=(tiles,),
-            in_specs=[row(channels), row(2 * channels)]
-            + [row(channels)] * 7
-            + [pl.BlockSpec((spans, STATES, channels), lambda i, *_: (tiles - 1 - i, 0, 0))]
-            + [whole(a.shape) for a in (convin, mixout, mixin, vec, decay, maps)],
-            out_specs=[row(channels)] + [whole(s.shape) for s in shapes[1:]],
-            scratch_shapes=[
-                big(convin),
-                big(mixout),
-                big(mixin),
-                pltpu.VMEM((8, 8, channels), F32),
-                pltpu.VMEM((STATES, channels), F32),
-                pltpu.VMEM((STATES, channels), F32),
-                pltpu.VMEM((STATES, channels), F32),
-                pltpu.VMEM((SPAN, STATES, channels), F32),
-                pltpu.VMEM((TILE, channels), BF16),
-                pltpu.VMEM((TILE, 2 * channels), BF16),
-                pltpu.VMEM((TILE, channels), F32),
-                pltpu.VMEM((TILE, channels), F32),
-            ],
-        ),
+        partial(back_kernel, mesh_size),
+        grid=(tiles + 1,),
+        in_specs=[pl.BlockSpec(memory_space=pltpu.SMEM)]
+        + [whole(a.shape) for a in (w, gnb, p)]
+        + [row(channels)] * 7
+        + [pl.BlockSpec((spans, STATES, channels), lambda i: (place(i), 0, 0))]
+        + [whole(a.shape) for a in (convin, mixout, mixin, vec, stat, decay, maps)]
+        + [pl.BlockSpec(memory_space=pltpu.HBM)] * len(grads),
+        out_specs=[row(channels)] + [whole(s.shape) for s in shapes[1:]],
         out_shape=shapes,
-        compiler_params=params(),
+        scratch_shapes=scratch,
+        compiler_params=params(collective_id),
         name="back",
-    )(flags, gg, p, x2, gx3, gated, y, v, u, x1, hold, convin, mixout, mixin, vec, decay, maps)
-
-
-def tail_kernel(
-    x_ref,
-    h_ref,
-    gx1_ref,
-    up_ref,
-    down_ref,
-    vec_ref,
-    gx_ref,
-    gup_out,
-    gdown_out,
-    gbias_out,
-    gvec_out,
-    up_acc,
-    down_acc,
-    bias_acc,
-    vec_acc,
-    low_scr,
-    turn_scr,
-    grad_scr,
-    sum_scr,
-):
-    at = pl.program_id(0)
-    tiles = pl.num_programs(0)
-    channels = x_ref.shape[1]
+    )(flags, w, gnb, p, x2, gx3, gated, y, v, u, x1, hold, convin, mixout, mixin, vec, stat, decay, maps, *grads)
+
+
+def small_gradients(out, gvec1, gvec2, gvec3, gtaps, gmap, gdecay, table_ref):
+    out[...] = jnp.zeros_like(out)
+    gains = {1: (gvec2, 6), 2: (gvec2, 2), 3: (gvec1, 3), 4: (gvec1, 0), 5: (gvec1, 6)}
+    shifts = {1: (gvec2, 7), 2: (gvec2, 3), 3: (gvec1, 4), 4: (gvec1, 1), 5: (gvec1, 7)}
+    shifts.update({6: (gvec3, 0), 7: (gvec1, 2), 8: (gvec2, 4), 9: (gvec2, 0), 10: (gvec2, 1)})
+    shifts.update({11: (gvec2, 5), 12: (gvec1, 5)})
+    for at, (ref, row) in gains.items():
+        out[at : at + 1, :] = ref[row : row + 1, :]
+    for at, (ref, row) in shifts.items():
+        out[6 + at : 7 + at, :] = ref[row : row + 1, :]
+    out[TAP_ROW : TAP_ROW + TAPS, :] = gtaps[:TAPS, :]
+    log_decay, decay, root, maps_in, maps_out = state_terms(table_ref)
+    both = gmap[...] * root
+    out[MAP_IN:MAP_OUT, :] = both * maps_out
+    out[MAP_OUT:TABLE, :] = both * maps_in
+    turn = (1.0 - root * root) / root
+    out[RATE:MAP_IN, :] = log_decay * (
+        gdecay[...] * decay - gmap[...] * maps_in * maps_out * turn
+    )
+
+
+def tail_kernel(mesh_size, *refs):
+    fused = mesh_size is not None
+    refs = list(refs)
+    take = lambda count: [refs.pop(0) for _ in range(count)]
+    x_ref, h_ref, gx1_ref, up_ref, down_ref, table_ref = take(6)
+    if fused:
+        gvec1, gvec2, gtaps, gmap, gdecay, gbias1 = take(6)
+        sources = take(3)
+        gx_ref, last_out = take(2)
+        reduced = take(7)
+    else:
+        gx_ref, gvec_out, gbias_out, up_out, down_out = take(5)
+    turn_scr, grad_scr, gh_scr, vec_acc, bias_scr = take(5)
+    step = pl.program_id(0)
+    frames, channels = x_ref.shape
     hidden = up_ref.shape[1]
-
-    @pl.when(at == 0)
+    chunks = hidden // CHUNK
+    tiles = frames // TILE
+    first_b, first_c = 1 + chunks, 1 + 2 * chunks
+    schedule = {}
+    if fused:
+        n_dp, n_fs = mesh_size
+        down_src, left_src, right_src, small_src, small_scr, gvec3 = take(6)
+        scratch = take(28)
+        sems = take(3)
+        swap = take(4)
+        dp, fs = lax.axis_index("dp"), lax.axis_index("fsdp")
+        down_out = ref_rows(down_src)
+        halves = (ref_rows(left_src), ref_rows(right_src))
+
+        def emit(chunk, total):
+            reduced[chunk][...] = total
+
+        plans, sends = scatter_plan(
+            dp,
+            fs,
+            n_dp,
+            n_fs,
+            sources + [down_src, left_src, right_src, small_src],
+            emit,
+            scratch,
+            *sems,
+        )
+        depth = len(plans[0])
+        starts = [0, 0, 0, first_b, first_b + chunks // 2, first_c, first_c]
+        for chunk, begin in enumerate(starts):
+            for stage in range(depth):
+                at = begin + 2 * stage if chunk < 5 else begin + stage
+                schedule.setdefault(min(at, first_c + tiles), []).append((stage, chunk))
+    last_step = first_c + tiles - 1
+
+    def progress(at):
+        for stage, chunk in sorted(schedule.get(at, [])):
+            plans[chunk][stage]()
+
+    @pl.when(step == 0)
     def _():
-        for ref in (up_acc, down_acc, bias_acc, vec_acc):
-            ref[...] = jnp.zeros_like(ref)
-
-    def first(rows):
-        e, _ = norm_parts(x_ref[rows, :].astype(F32))
-        low_scr[rows, :] = (e * vec_ref[0:1, :] + vec_ref[6:7, :]).astype(BF16)
-        low = (0.5 * gx1_ref[rows, :]).astype(BF16)
-        grad_scr[rows, :] = low
-        vec_acc[0] += fold8(low.astype(F32))
-        sum_scr[rows, :] = jnp.zeros((ROWS, channels), F32)
-
-    by_rows(first)
-    turn_scr[...] = low_scr[...].T
-    ffn_back(
-        turn_scr,
-        None,
-        grad_scr,
-        lambda cols: h_ref[:, cols].astype(F32),
-        up_ref,
-        down_ref,
-        up_acc,
-        down_acc,
-        bias_acc,
-        sum_scr,
-        hidden,
-    )
-
-    def second(rows):
-        e, inv = norm_parts(x_ref[rows, :].astype(F32))
-        grad = sum_scr[rows, :]
-        vec_acc[1] += fold8(grad * e)
-        vec_acc[2] += fold8(grad)
-        gx_ref[rows, :] = gx1_ref[rows, :] + norm_back(grad, e, inv, vec_ref[0:1, :])
-
-    by_rows(second)
-
-    @pl.when(at == tiles - 1)
+        if fused:
+            greet(dp, fs, n_dp, n_fs)
+        progress(0)
+        vec_acc[...] = jnp.zeros_like(vec_acc)
+
+        def first(rows):
+            e, _ = norm_parts(x_ref[rows, :].astype(F32))
+            low = (e * table_ref[0:1, :] + table_ref[6:7, :]).astype(BF16)
+            turn_scr[:, rows] = low.T
+            grad = (0.5 * gx1_ref[rows, :]).astype(BF16)
+            grad_scr[rows, :] = grad
+            vec_acc[0] += fold8(grad.astype(F32))
+
+        by_rows(first, frames)
+
+    if fused:
+        for at in range(1, last_step + 1):
+            if at in schedule and at != first_c:
+
+                @pl.when(step == at)
+                def _(at=at):
+                    progress(at)
+
+    @pl.when((step >= 1) & (step < first_b))
     def _():
-        by_rows(lambda rows: gup_out.__setitem__((rows, slice(None)), up_acc[rows, :].astype(BF16)), channels)
-        by_rows(lambda rows: gdown_out.__setitem__((rows, slice(None)), down_acc[rows, :].astype(BF16)), hidden)
-        gbias_out[...] = jnp.broadcast_to(jnp.sum(bias_acc[...], axis=0, keepdims=True), gbias_out.shape)
-        for k in range(3):
-            gvec_out[k : k + 1, :] = jnp.sum(vec_acc[k], axis=0, keepdims=True)
-
-
-def tail(x, h, gx1, up, down, vec):
+        h = h_ref[...].astype(F32)
+        active = (h * sigmoid(h)).astype(BF16)
+        down_out[columns(step - 1), :] = dot_tn(active, grad_scr[...]).astype(BF16)
+
+    def second_half(c, store):
+        cols = columns(c)
+        h = h_ref[...].astype(F32)
+        sig = sigmoid(h)
+        gate = dot_nt(grad_scr[...], down_ref[cols, :])
+        grad_h = (gate * (sig * (1.0 + h * (1.0 - sig)))).astype(BF16)
+        gh_scr[:, cols] = grad_h
+        bias_scr[pl.ds(c, 1), :] = jnp.sum(fold8(grad_h.astype(F32)), axis=0, keepdims=True)
+        store(dot_nn(turn_scr[...], grad_h).astype(BF16))
+
+    if fused:
+        for half in range(2):
+            begin = first_b + half * (chunks // 2)
+
+            @pl.when((step >= begin) & (step < begin + chunks // 2))
+            def _(half=half, begin=begin):
+                def store(value):
+                    halves[half][:, columns(step - begin)] = value
+
+                second_half(step - first_b, store)
+
+    else:
+
+        @pl.when((step >= first_b) & (step < first_c))
+        def _():
+            def store(value):
+                up_out[:, columns(step - first_b)] = value
+
+            second_half(step - first_b, store)
+
+    if fused:
+
+        @pl.when(step == first_c)
+        def _():
+            gvec3[0:1, :] = jnp.sum(vec_acc[0], axis=0, keepdims=True)
+            small_gradients(small_scr, gvec1, gvec2, gvec3, gtaps, gmap, gdecay, table_ref)
+            narrow = small_scr[...].T.astype(BF16)
+            devices = small_src.shape[0]
+            small_src[:, :, :256] = narrow.reshape((devices, 16, 256))
+            for c in range(chunks):
+                bias_scr[chunks + c : chunks + c + 1, :] = gbias1[0:1, c * CHUNK : c * CHUNK + CHUNK]
+            bias = bias_scr[...].astype(BF16)
+            small_src[:, :, 256:] = jnp.broadcast_to(bias[None], (devices, 16, CHUNK))
+            progress(first_c)
+
+    @pl.when(step >= first_c)
+    def _():
+        tile = step - first_c
+        whole_tile = pl.ds(pl.multiple_of(tile * TILE, TILE), TILE)
+        back = [
+            dot_nt(gh_scr[whole_tile, :], up_ref[k * CHUNK : k * CHUNK + CHUNK, :])
+            for k in range(channels // CHUNK)
+        ]
+        for k, value in enumerate(back):
+            gx_ref[:, k * CHUNK : k * CHUNK + CHUNK] = value
+
+        def second(rows):
+            here = pl.ds(pl.multiple_of(tile * TILE + rows.start, ROWS), ROWS)
+            e, inv = norm_parts(x_ref[here, :].astype(F32))
+            grad = gx_ref[rows, :]
+            vec_acc[1] += fold8(grad * e)
+            vec_acc[2] += fold8(grad)
+            gx_ref[rows, :] = gx1_ref[here, :] + norm_back(grad, e, inv, table_ref[0:1, :])
+
+        by_rows(second)
+
+    @pl.when(step == last_step)
+    def _():
+        if fused:
+            last_out[...] = jnp.zeros_like(last_out)
+            for k in range(2):
+                last_out[k : k + 1, :] = jnp.sum(vec_acc[1 + k], axis=0, keepdims=True)
+            ends = sorted(schedule.get(last_step + 1, []))
+
+            def between():
+                for stage, chunk in ends:
+                    plans[chunk][stage]()
+
+            last_out[...] = sum_over(last_out[...], dp, fs, n_dp, n_fs, *swap, between=between)
+            for wait in sends:
+                wait()
+        else:
+            gvec_out[...] = jnp.zeros_like(gvec_out)
+            for k in range(3):
+                gvec_out[k : k + 1, :] = jnp.sum(vec_acc[k], axis=0, keepdims=True)
+            gbias_out[...] = bias_scr[...]
+
+
+def tail(mesh_size, x, h, gx1, up, down, table, others=(), grads=(), collective_id=None):
+    fused = mesh_size is not None
     frames, channels = x.shape
     hidden = up.shape[1]
-    tiles = frames // TILE
-    row = lambda width: pl.BlockSpec((TILE, width), lambda i: (i, 0))
-    big = lambda a: pltpu.VMEM(a.shape, F32)
-    shapes = [
-        jax.ShapeDtypeStruct((frames, channels), F32),
-        jax.ShapeDtypeStruct(up.shape, BF16),
-        jax.ShapeDtypeStruct(down.shape, BF16),
-        jax.ShapeDtypeStruct((8, hidden), F32),
-        jax.ShapeDtypeStruct((8, channels), F32),
+    tiles, chunks = frames // TILE, hidden // CHUNK
+    first_b, first_c = 1 + chunks, 1 + 2 * chunks
+    place = lambda i: jnp.where(
+        i < first_b, jnp.maximum(i - 1, 0), jnp.minimum(i - first_b, chunks - 1)
+    )
+    shapes = [jax.ShapeDtypeStruct((frames, channels), F32)]
+    scratch = [
+        pltpu.VMEM((channels, frames), BF16),
+        pltpu.VMEM((frames, channels), BF16),
+        pltpu.VMEM((frames, hidden), BF16),
+        pltpu.VMEM((8, 8, channels), F32),
+        pltpu.VMEM((2 * chunks, CHUNK), F32),
     ]
+    if fused:
+        devices = mesh_size[0] * mesh_size[1]
+        tails = [g.shape[1:] for g in grads]
+        own = [(hidden // devices, channels)] + [(channels // devices, hidden // 2)] * 2
+        own.append((16, 2 * CHUNK))
+        shapes.append(jax.ShapeDtypeStruct((8, channels), F32))
+        shapes += [jax.ShapeDtypeStruct(t, F32) for t in tails + own]
+        scratch += [pltpu.VMEM((devices,) + t, BF16) for t in own]
+        scratch += [pltpu.VMEM((256, channels), F32), pltpu.VMEM((8, channels), F32)]
+        scratch += scatter_scratch(*mesh_size, tails + own)
+        scratch += scatter_sems(*mesh_size, len(tails + own))
+        scratch += swap_scratch(*mesh_size, channels)
+    else:
+        shapes += [
+            jax.ShapeDtypeStruct((8, channels), F32),
+            jax.ShapeDtypeStruct((2 * chunks, CHUNK), F32),
+            jax.ShapeDtypeStruct(up.shape, BF16),
+            jax.ShapeDtypeStruct(down.shape, BF16),
+        ]
     return pl.pallas_call(
-        tail_kernel,
-        grid=(tiles,),
-        in_specs=[row(channels), row(hidden), row(channels)]
-        + [whole(a.shape) for a in (up, down, vec)],
-        out_specs=[row(channels)] + [whole(s.shape) for s in shapes[1:]],
+        partial(tail_kernel, mesh_size),
+        grid=(first_c + tiles,),
+        in_specs=[whole(x.shape), pl.BlockSpec((frames, CHUNK), lambda i: (0, place(i)))]
+        + [whole(a.shape) for a in (gx1, up, down, table) + tuple(others)]
+        + [pl.BlockSpec(memory_space=pltpu.HBM)] * len(grads),
+        out_specs=[
+            pl.BlockSpec((TILE, channels), lambda i: (jnp.maximum(i - first_c, 0), 0))
+        ]
+        + [whole(s.shape) for s in shapes[1:]],
         out_shape=shapes,
-        scratch_shapes=[
-            big(up),
-            big(down),
-            pltpu.VMEM((8, hidden), F32),
-            pltpu.VMEM((8, 8, channels), F32),
-            pltpu.VMEM((TILE, channels), BF16),
-            pltpu.VMEM((channels, TILE), BF16),
-            pltpu.VMEM((TILE, channels), BF16),
-            pltpu.VMEM((TILE, channels), F32),
+        scratch_shapes=scratch,
+        compiler_params=params(collective_id),
+        name="tail",
+    )(x, h, gx1, up, down, table, *others, *grads)
+
+
+def unpack_kernel(
+    place_ref,
+    up1_ref,
+    down1_ref,
+    convout_ref,
+    convin_ref,
+    mixout_ref,
+    mixin_ref,
+    down0_ref,
+    left_ref,
+    right_ref,
+    small_ref,
+    last_ref,
+    up_out,
+    down_out,
+    bias_out,
+    mixin_out,
+    mixout_out,
+    convin_out,
+    convout_out,
+    convbias_out,
+    rate_out,
+    map_out,
+    taps_out,
+    gains_out,
+    shifts_out,
+):
+    mine = place_ref[0]
+    half = left_ref.shape[1]
+    up_out[0, :, :half] = left_ref[...]
+    up_out[0, :, half:] = right_ref[...]
+    up_out[1] = up1_ref[...]
+    down_out[0] = down0_ref[...]
+    down_out[1] = down1_ref[...]
+    mixin_out[...] = mixin_ref[...]
+    mixout_out[...] = mixout_ref[...]
+    convin_out[...] = convin_ref[...]
+    convout_out[...] = convout_ref[...]
+    count = bias_out.shape[1]
+    row = (mine * count) // CHUNK
+    inner = mine * count - row * CHUNK
+    for layer in range(2):
+        line = small_ref[pl.ds(8 * layer + row, 1), CHUNK:]
+        line = pltpu.roll(jnp.broadcast_to(line, (8, CHUNK)), CHUNK - inner, 1)
+        bias_out[layer : layer + 1, :] = line[0:1, :count]
+    own = small_ref.shape[0]
+    channels = last_ref.shape[1]
+    first = pltpu.roll(last_ref[...], channels - mine * own, 1)[:, :128].T[:own, :]
+    small = small_ref[:, :256]
+    gains_out[...] = small[:, :6]
+    gains_out[:, 0:1] = first[:, 0:1]
+    shifts_out[...] = small[:, 6:18]
+    shifts_out[:, 0:1] = first[:, 1:2]
+    convbias_out[...] = small[:, 18:19]
+    taps_out[...] = small[:, TAP_ROW : TAP_ROW + TAPS]
+    rate_out[...] = small[:, RATE:MAP_IN]
+    map_out[0] = small[:, MAP_IN:MAP_OUT]
+    map_out[1] = small[:, MAP_OUT:TABLE]
+
+
+def unpack(mine, up1, down1, convout, convin, mixout, mixin, down0, left, right, small, last, hidden):
+    own = small.shape[0]
+    devices = last.shape[1] // own
+    f32 = lambda *shape: jax.ShapeDtypeStruct(shape, F32)
+    vmem = pl.BlockSpec(memory_space=pltpu.VMEM)
+    return pl.pallas_call(
+        unpack_kernel,
+        in_specs=[pl.BlockSpec(memory_space=pltpu.SMEM)] + [vmem] * 11,
+        out_specs=[vmem] * 13,
+        out_shape=[
+            f32(2, *up1.shape),
+            f32(2, *down1.shape),
+            f32(2, hidden // devices),
+            f32(*mixin.shape),
+            f32(*mixout.shape),
+            f32(*convin.shape),
+            f32(*convout.shape),
+            f32(own, 1),
+            f32(own, STATES),
+            f32(2, own, STATES),
+            f32(own, TAPS),
+            f32(own, 6),
+            f32(own, 12),
         ],
-        compiler_params=params(),
-        name="tail",
-    )(x, h, gx1, up, down, vec)
+        name="unpack",
+    )(mine, up1, down1, convout, convin, mixout, mixin, down0, left, right, small, last)
 
 
 def pack_table(gains, shifts, conv_bias, taps, rate, maps):
@@ -1656,17 +1989,87 @@
         scale = lax.rsqrt(pool[1:2] / (frames_dev * devices) + EPSILON)
         stat = jnp.concatenate([pool[0:1], scale, jnp.zeros((6, channels), F32)])
     h0, x1, u, v, y, gated, x2, p, hold, w, _, table, bias, decay, coupling = made[:15]
-    result, gx3, gnb, gup1, gdown1, gconvout, gbias1, gvec1 = middle(
-        x2, w, cotangent, up1, down1, convout, bias, table, stat
+    size = (n_dp, n_fs) if fused else None
+    result, gx3, gnb, gup1, gdown1, gconvout, gbias1, gvec1, stat = middle(
+        size, x2, w, cotangent, up1, down1, convout, bias, table, stat, 2 if fused else None
     )
-    sums = exchange(n_dp, n_fs, gvec1, 1, 4, total_kernel)[6:8]
-    sums = sums * (table[5:6] / (frames_dev * devices))
-    stat = jnp.concatenate([stat[0:2], sums[1:2], sums[0:1], jnp.zeros((4, channels), F32)])
-    gg, gtaps = conv_back(flags, w, gnb, p, table, stat)
-    gx1, gconvin, gmixout, gmixin, gvec2, gmap, gdecay = back(
-        flags, gg, p, x2, gx3, gated, y, v, u, x1, hold, convin, mixout, mixin, table, decay, coupling
+    if not fused:
+        sums = exchange(n_dp, n_fs, gvec1, 1, 4, total_kernel)[6:8]
+        sums = sums * (table[5:6] / (frames_dev * devices))
+        stat = jnp.concatenate([stat[0:2], sums[1:2], sums[0:1], stat[4:8]])
+    wide = lambda g: g.reshape((devices, g.shape[0] // devices, g.shape[1]))
+    grads = tuple(wide(g) for g in (gup1, gdown1, gconvout))
+    made = back(
+        size,
+        flags,
+        w,
+        gnb,
+        p,
+        x2,
+        gx3,
+        gated,
+        y,
+        v,
+        u,
+        x1,
+        hold,
+        convin,
+        mixout,
+        mixin,
+        table,
+        stat,
+        decay,
+        coupling,
+        grads if fused else (),
+        3 if fused else None,
     )
-    gx, gup0, gdown0, gbias0, gvec3 = tail(frames, h0, gx1, up0, down0, table)
+    gx1, gconvin, gmixout, gmixin, gvec2, gtaps, gmap, gdecay = made[:8]
+    if fused:
+        gx, last, *late = tail(
+            size,
+            frames,
+            h0,
+            gx1,
+            up0,
+            down0,
+            table,
+            (gvec1, gvec2, gtaps, gmap, gdecay, gbias1),
+            tuple(wide(g) for g in (gconvin, gmixout, gmixin)),
+            4,
+        )
+        (
+            up_grad,
+            down_grad,
+            bias_grad,
+            mixin_grad,
+            mixout_grad,
+            convin_grad,
+            convout_grad,
+            convbias_grad,
+            rate_grad,
+            map_grad,
+            taps_grad,
+            gains_grad,
+            shifts_grad,
+        ) = unpack(mine.reshape((1,)), *made[8:], *late, last, up0.shape[1])
+        return (
+            result,
+            gx,
+            up_grad,
+            down_grad,
+            bias_grad,
+            mixin_grad,
+            mixout_grad,
+            convin_grad,
+            convout_grad,
+            convbias_grad.reshape((-1,)),
+            rate_grad.T,
+            map_grad.transpose((0, 2, 1)),
+            taps_grad.T,
+            gains_grad.T,
+            shifts_grad.T,
+        )
+    gx, gvec3, gbias0, gup0, gdown0 = tail(None, frames, h0, gx1, up0, down0, table)
 
     def weights_of(log_rate, maps):
         log_decay = -jnp.exp(log_rate)
@@ -1676,29 +2079,17 @@
     rate, maps = unpack_table(table)[4:]
     rate_grad, map_grad = jax.vjp(weights_of, rate, maps)[1]((gdecay, gmap))
     gain_grad = jnp.stack([gvec3[1], gvec2[6], gvec2[2], gvec1[3], gvec1[0], gvec1[6]])
-    shift_grad = jnp.stack(
-        [
-            gvec3[2],
-            gvec2[7],
-            gvec2[3],
-            gvec1[4],
-            gvec1[1],
-            gvec1[7],
-            gvec3[0],
-            gvec1[2],
-            gvec2[4],
-            gvec2[0],
-            gvec2[1],
-            gvec2[5],
-        ]
+    rows = [gvec3[2], gvec2[7], gvec2[3], gvec1[4], gvec1[1], gvec1[7], gvec3[0], gvec1[2]]
+    rows += [gvec2[4], gvec2[0], gvec2[1], gvec2[5]]
+    small_grad = pack_table(
+        gain_grad, jnp.stack(rows), gvec1[5], gtaps[:TAPS], rate_grad, map_grad
     )
-    small_grad = pack_table(gain_grad, shift_grad, gvec1[5], gtaps[:TAPS], rate_grad, map_grad)
-    bias_grad = jnp.concatenate([gbias0[:1], gbias1[:1]]).reshape((16, CHUNK))
-    wide = lambda g: g.reshape((devices, g.shape[0] // devices, g.shape[1]))
+    bias_grad = jnp.concatenate([gbias0[:8], gbias1[0].reshape((8, CHUNK))])
     reduced = scatter_all(
         n_dp,
         n_fs,
-        [wide(g) for g in (gup1, gdown1, gconvout, gconvin, gmixout, gmixin, gup0, gdown0)]
+        list(grads)
+        + [wide(g) for g in (gconvin, gmixout, gmixin, gup0, gdown0)]
         + [
             wide(small_grad.astype(BF16)),
             jnp.broadcast_to(bias_grad.astype(BF16), (devices, 16, CHUNK)),

time: 461 us -> 412 us (0.89)
  local copies, waits for them, and re-layouts: 36.7 us -> 13.8 us
  Pallas kernels: 414 us -> 393 us
    pallas_call x6 -> x4, Pallas kernels: 291 us -> 269 us  [the longest x1 119 us: back(): pl.pallas_call(partial(back_kernel, mesh_size), grid=(tiles + 1,), in_spe...]
    slice x32 -> x0, local copies, waits for them, and re-layouts: 18.7 us -> none  [the longest x2 1.7 us: on_device(): bias_grad = jnp.concatenate([gbias0[:1], gbias1[:1]]).reshape((16, CHUNK))]
    unnamed x30 -> x10, local copies, waits for them, and re-layouts: 7.91 us -> 10.7 us
where the time goes in v2:
time: 412 us; the launch traced here: 411 us
  Pallas kernels  393 us (95%)
  local copies, waits for them, and re-layouts  13.8 us (3%)
    pallas_call x1, Pallas kernels, front(): pl.pallas_call(partial(front_kernel, mesh_size), grid=(2 * tiles + 1,), i...  124 us
    pallas_call x1, Pallas kernels, back(): pl.pallas_call(partial(back_kernel, mesh_size), grid=(tiles + 1,), in_spe...  119 us
    pallas_call x1, Pallas kernels, tail(): pl.pallas_call(partial(tail_kernel, mesh_size), grid=(first_c + tiles,),...  76.4 us
    pallas_call x1, Pallas kernels, middle(): pl.pallas_call(partial(middle_kernel, mesh_size), grid=(tiles,), in_specs...  70.9 us
    unnamed x10, local copies, waits for them, and re-layouts  10.7 us

profile of v2, /device:TPU:0, one launch (start us, length us, event | category | flops | bytes accessed | tf_op | source)
XLA Modules:
  0.0 411.3 jit_solution(2122663877418130462)
XLA Ops:
  1.3 0.8 convert_reduce_fusion
  2.2 0.5 broadcast_subtract_fusion.refs_0_
  2.7 0.7 copy.48
  3.4 0.8 copy.49
  4.2 0.8 copy.46
  5.0 0.8 copy.47
  5.8 0.8 dynamic_update_slice.3
  6.6 0.7 slice_bitcast_fusion
  7.3 0.8 concatenate.6
  8.1 0.6 maximum_bitcast_fusion.refs_2_
  8.7 123.7 %front.1 = (bf16[1536,2048]{1,0:T(8,128)(2,1)}, f32[1536,512]{1,0:T(8,128)}, f32[1536,512]{1,0:T(8,128)}, bf16[1536,512]{1,0:T(8,128)(2,1)}, bf16[1536,512]{1,0:...) custom-call(s32[3]{0:T(128)} %broadcast_subtract_fusion.refs_0_, ...), custom_call_target="tpu_custom_call" | custom-call | tf_op jit(solution)/shard_map/front/pallas_call | solution.py:970
  132.4 70.9 %middle.1 = (bf16[1536,512]{1,0:T(8,128)(2,1)}, f32[1536,512]{1,0:T(8,128)}, f32[1536,512]{1,0:T(8,128)}, bf16[512,2048]{1,0:T(8,128)(2,1)}, bf16[2048,512]{1,0:...) custom-call(f32[1536,512]{1,0:T(8,128)} %get-tuple-element.80.x2_ref.refs_4_,, ...), custom_call_target="tpu_custom_call" | custom-call | tf_op jit(solution)/shard_map/middle/pallas_call | solution.py:1189
  203.3 119.4 %back.1 = (f32[1536,512]{1,0:T(8,128)}, bf16[512,1024]{1,0:T(8,128)(2,1)}, bf16[512,512]{1,0:T(8,128)(2,1)}, bf16[512,1024]{1,0:T(8,128)(2,1)}, f32[8,512]{1,0:T...) custom-call(s32[3]{0:T(128)} %broadcast_subtract_fusion.refs_0_, ...), custom_call_target="tpu_custom_call" | custom-call | tf_op jit(solution)/shard_map/back/pallas_call | solution.py:1546
  322.8 76.4 %tail.1 = (f32[1536,512]{1,0:T(8,128)}, f32[8,512]{1,0:T(8,128)}, f32[16,1024]{1,0:T(8,128)}, f32[16,512]{1,0:T(8,128)}, f32[16,1024]{1,0:T(8,128)}, /*index=5*/...) custom-call(bf16[1536,512]{1,0:T(8,128)(2,1)} %refs_0_.1, ...), custom_call_target="tpu_custom_call" | custom-call | tf_op jit(solution)/shard_map/tail/pallas_call | solution.py:1794
  399.2 0.0 copy-start
  399.2 2.3 unpack.1
  401.5 1.3 reduce
  402.9 1.4 copy.51
  404.2 1.4 copy.50
  405.6 1.4 copy.52
  407.0 2.7 copy.57
  409.6 0.0 copy-done
  409.6 1.7 copy.58
  (7 shorter events, 0.0 us)
Async XLA Ops:
  399.2 10.4 %copy-start = (f32[1536,512]{1,0:T(8,128)S(1)}, f32[1536,512]{1,0:T(8,128)}, u32[]{:S(2)}) copy-start(f32[1536,512]{1,0:T(8,128)} %get-tuple-element.208) | copy-start | bytes 9437188

commit v3 on v2

--- a/solution.py
+++ b/solution.py
@@ -478,6 +478,241 @@
     )(x)
 
 
+class Place:
+    def __init__(self, dp, fs, n_dp, n_fs):
+        self.dp, self.fs, self.n_dp, self.n_fs = dp, fs, n_dp, n_fs
+        self.count = (n_dp - 1).bit_length()
+        self.bits = [lax.rem(lax.div(dp, 2**k), 2) for k in range(self.count)]
+        self.half = n_fs // 2
+
+    def peer(self, bit):
+        return (flip(self.dp, 2**bit), self.fs)
+
+    def view(self, ref, free=(), flipped=(), z=None, skip=()):
+        index = []
+        for bit in reversed(range(self.count)):
+            if bit in skip:
+                continue
+            if bit in free:
+                index.append(slice(None))
+            else:
+                index.append(1 - self.bits[bit] if bit in flipped else self.bits[bit])
+        if z is not None:
+            index.append(z)
+        return ref.at[tuple(index)] if index else ref
+
+    def part(self, which):
+        return pl.ds(which * self.half, self.half)
+
+
+def block_layout(n_dp, n_fs):
+    return (2,) * ((n_dp - 1).bit_length()) + (n_fs,)
+
+
+def hop_orders(place):
+    bits = tuple(range(1, place.count))
+    return (bits, bits[::-1])
+
+
+def copy_count(n_dp, n_fs):
+    return n_fs - 1 + 2 * ((n_dp - 1).bit_length() - 1) + 1
+
+
+def block_gather(place, sources, outs, send_sem, recv_sem, local_sem):
+    n_fs, fs = place.n_fs, place.fs
+    sends = []
+
+    def stages(chunk):
+        src, out = sources[chunk], outs[chunk]
+
+        def remote(slot, view_from, view_to, device):
+            return pltpu.make_async_remote_copy(
+                src_ref=view_from,
+                dst_ref=view_to,
+                send_sem=send_sem.at[chunk, slot],
+                recv_sem=recv_sem.at[chunk, slot],
+                device_id=device,
+                device_id_type=MESH,
+            )
+
+        def launch(make):
+            make().start()
+            sends.append(lambda: make().wait_send())
+
+        def own_copy():
+            return pltpu.make_async_copy(src, place.view(out, z=fs), local_sem.at[chunk])
+
+        def along(step):
+            to = lax.rem(fs + step, n_fs)
+            return remote(step - 1, src, place.view(out, z=fs), (place.dp, to))
+
+        def start():
+            own_copy().start()
+            for step in range(1, n_fs):
+                launch(lambda step=step: along(step))
+
+        def wait_along():
+            own_copy().wait()
+            for step in range(1, n_fs):
+                origin = lax.rem(fs + n_fs - step, n_fs)
+                remote(
+                    step - 1, src, place.view(out, z=origin), (place.dp, origin)
+                ).wait_recv()
+
+        steps, before = [start], wait_along
+        slot = n_fs - 1
+        orders = hop_orders(place)
+        for depth in range(place.count - 1):
+            plan = [(slot + part, part, order[depth], order[:depth]) for part, order in enumerate(orders)]
+            slot += 2
+
+            def hop(slot, part, bit, free, arrived):
+                view = place.view(out, free, (bit,) if arrived else (), place.part(part))
+                return remote(slot, view, view, place.peer(bit))
+
+            def go(plan=plan, before=before, hop=hop):
+                before()
+                for item in plan:
+                    launch(lambda item=item: hop(*item, False))
+
+            def arrive(plan=plan, hop=hop):
+                for item in plan:
+                    hop(*item, True).wait_recv()
+
+            steps.append(go)
+            before = arrive
+
+        def across(arrived, slot=slot):
+            free = tuple(range(1, place.count))
+            view = place.view(out, free, (0,) if arrived else ())
+            return remote(slot, view, view, place.peer(0))
+
+        def cross(before=before):
+            before()
+            launch(lambda: across(False))
+
+        return steps + [cross, lambda: across(True).wait_recv()]
+
+    return [stages(chunk) for chunk in range(len(outs))], sends
+
+
+def block_scatter(place, sources, emit, scratch, send_sem, recv_sem, local_sem):
+    n_fs, fs = place.n_fs, place.fs
+    sends = []
+    per = 3 + place.count - 1
+
+    def add_into(kept, other):
+        shape = kept.shape[:-3]
+        for index in itertools.product(*[range(n) for n in shape]):
+            kept[index] = (kept[index].astype(F32) + other[index].astype(F32)).astype(BF16)
+
+    def stages(chunk):
+        src = sources[chunk]
+        own, cross_in, last, *later = scratch[per * chunk : per * chunk + per]
+
+        def remote(slot, view_from, view_to, device):
+            return pltpu.make_async_remote_copy(
+                src_ref=view_from,
+                dst_ref=view_to,
+                send_sem=send_sem.at[chunk, slot],
+                recv_sem=recv_sem.at[chunk, slot],
+                device_id=device,
+                device_id_type=MESH,
+            )
+
+        def launch(make):
+            make().start()
+            sends.append(lambda: make().wait_send())
+
+        every = tuple(range(1, place.count))
+
+        def load():
+            return pltpu.make_async_copy(place.view(src, every), own, local_sem.at[chunk])
+
+        def across():
+            return remote(0, place.view(src, every, (0,)), cross_in, place.peer(0))
+
+        def start():
+            launch(across)
+            load().start()
+
+        def fold_cross():
+            load().wait()
+            across().wait_recv()
+            add_into(own, cross_in)
+
+        steps, before = [start], fold_cross
+        slot = 1
+        orders = [order[::-1] for order in hop_orders(place)]
+        for depth in range(place.count - 1):
+            plan = []
+            for part, order in enumerate(orders):
+                free = tuple(order[depth + 1 :])
+                plan.append((slot + part, part, order[depth], free, later[depth]))
+            slot += 2
+
+            def hop(slot, part, bit, free, buffer):
+                view = place.view(own, free, (bit,), place.part(part), skip=(0,))
+                return remote(slot, view, buffer.at[part], place.peer(bit))
+
+            def go(plan=plan, before=before, hop=hop):
+                before()
+                for item in plan:
+                    launch(lambda item=item: hop(*item))
+
+            def fold(plan=plan, hop=hop):
+                for item in plan:
+                    hop(*item).wait_recv()
+                    _, part, _, free, buffer = item
+                    kept = place.view(own, free, (), place.part(part), skip=(0,))
+                    add_into(kept, buffer.at[part])
+
+            steps.append(go)
+            before = fold
+
+        def along(step, slot=slot):
+            to = lax.rem(fs + step, n_fs)
+            view = place.view(own, z=to, skip=(0,))
+            return remote(slot + step - 1, view, last.at[step - 1], (place.dp, to))
+
+        def spread(before=before):
+            before()
+            for step in range(1, n_fs):
+                launch(lambda step=step: along(step))
+
+        def finish():
+            total = place.view(own, z=fs, skip=(0,))[...].astype(F32)
+            for step in range(1, n_fs):
+                along(step).wait_recv()
+                total = total + last[step - 1].astype(F32)
+            emit(chunk, total)
+
+        return steps + [spread, finish]
+
+    return [stages(chunk) for chunk in range(len(sources))], sends
+
+
+def block_scratch(n_dp, n_fs, blocks, tail):
+    hops = (n_dp - 1).bit_length() - 1
+    out = []
+    for count in blocks:
+        entry = (count,) + tail
+        zone = (2,) * hops + (n_fs,) + entry
+        out += [pltpu.VMEM(zone, BF16), pltpu.VMEM(zone, BF16), pltpu.VMEM((n_fs - 1,) + entry, BF16)]
+        for depth in range(hops):
+            out.append(pltpu.VMEM((2,) + (2,) * (hops - 1 - depth) + (n_fs // 2,) + entry, BF16))
+    return out
+
+
+def block_sems(n_dp, n_fs, chunks):
+    count = copy_count(n_dp, n_fs)
+    return [
+        pltpu.SemaphoreType.DMA((chunks, count)),
+        pltpu.SemaphoreType.DMA((chunks, count)),
+        pltpu.SemaphoreType.DMA((chunks,)),
+    ]
+
+
 TILE = 512
 STATES = 32
 TAPS = 15
@@ -558,7 +793,7 @@
     return jnp.sum(v.reshape((STATES // 8, 8, v.shape[1])), axis=0)
 
 
-def fill_halo(padded, flags_ref, tiles):
+def fill_halo(padded, flags, tiles):
     pitch = TILE + 2 * REACH
     for at in range(tiles):
         base = at * pitch
@@ -568,7 +803,7 @@
             end = base + REACH + TILE
             padded[:, end : end + REACH, :] = jnp.zeros_like(padded[:, end : end + REACH, :])
         else:
-            keep = flags_ref[at + 1].astype(F32)
+            keep = flags[at + 1]
             end = base + REACH + TILE
             padded[:, end : end + REACH, :] = (
                 padded[:, base + pitch + REACH : base + pitch + 2 * REACH, :] * keep
@@ -625,19 +860,105 @@
     return ref.reshape((ref.shape[0] * ref.shape[1], ref.shape[2]))
 
 
-WEIGHTS = 6
+PIECE = 16
+WIDTH = 512
+
+
+def cols_of(ref, first, at):
+    per = WIDTH // CHUNK
+    part = ref[:, first + lax.div(at, per), :, columns(lax.rem(at, per))]
+    return part.reshape((ref.shape[0] * PIECE, CHUNK))
+
+
+def rows_of(ref, first, at):
+    groups = CHUNK // (4 * PIECE)
+    part = ref[pl.ds(at * groups, groups), first : first + 4]
+    return part.reshape((CHUNK, WIDTH))
+
+
+def square_of(ref, at):
+    return ref[:, at].reshape((ref.shape[0] * PIECE, WIDTH))
+
+
+def store_wide(out, first, acc):
+    def run(group, _):
+        rows = pl.ds(pl.multiple_of(group * PIECE, PIECE), PIECE)
+        for k in range(acc.shape[1] // WIDTH):
+            out[group, first + k] = acc[rows, k * WIDTH : k * WIDTH + WIDTH].astype(BF16)
+        return 0
+
+    lax.fori_loop(0, acc.shape[0] // PIECE, run, 0)
+
+
+def store_tall(out, first, acc):
+    def run(group, _):
+        rows = pl.ds(pl.multiple_of(group * 4 * PIECE, 4 * PIECE), 4 * PIECE)
+        out[group, first : first + 4] = acc[rows, :].astype(BF16).reshape((4, PIECE, WIDTH))
+        return 0
+
+    lax.fori_loop(0, acc.shape[0] // (4 * PIECE), run, 0)
+
+
+def flat_groups(ref):
+    count = 1
+    for n in ref.shape[:-3]:
+        count *= n
+    return ref.reshape((count,) + ref.shape[-3:])
+
+
+def carries(offsets_ref, counts_ref, tiles):
+    out = []
+    for tile in range(tiles):
+        begins = jnp.int32(0)
+        for slot in range(offsets_ref.shape[1]):
+            here = (offsets_ref[0, slot] == tile * TILE) & (slot < counts_ref[0])
+            begins = jnp.maximum(begins, here.astype(jnp.int32))
+        out.append((1 - begins).astype(F32))
+    return out
+
+
+def pick(values, at):
+    total = values[0] * (at == 0).astype(F32)
+    for k in range(1, len(values)):
+        total = total + values[k] * (at == k).astype(F32)
+    return total
+
+
+def pack_small(out, scr, place, bias_ref, gains, shifts, conv_bias, taps, rate, maps):
+    own = gains.shape[1]
+    scr[...] = jnp.zeros_like(scr)
+    scr[0:6, :own] = gains[...].astype(F32)
+    scr[6:18, :own] = shifts[...].astype(F32)
+    scr[18:19, :own] = conv_bias[...].astype(F32)
+    scr[TAP_ROW : TAP_ROW + TAPS, :own] = taps[...].astype(F32)
+    out[:, :CHUNK] = scr[...].T[:own, :].astype(BF16)
+    out[:, RATE:MAP_IN] = rate[...]
+    out[:, MAP_IN:MAP_OUT] = maps[0]
+    out[:, MAP_OUT:TABLE] = maps[1]
+    count = bias_ref.shape[1]
+    row = lax.div(place * count, CHUNK)
+    inner = place * count - row * CHUNK
+    at_row = lax.broadcasted_iota(jnp.int32, (PIECE, CHUNK), 0)
+    wide = jnp.zeros((PIECE, CHUNK), F32)
+    for layer in range(2):
+        line = jnp.broadcast_to(bias_ref[layer : layer + 1, :].astype(F32), (8, count))
+        line = jnp.concatenate([line, jnp.zeros((8, CHUNK - count), F32)], axis=1)
+        line = pltpu.roll(line, inner, 1)
+        wide = wide + jnp.where(at_row == 8 * layer + row, jnp.broadcast_to(line[0:1], wide.shape), 0.0)
+    out[:, CHUNK:] = wide.astype(BF16)
 
 
 def front_kernel(mesh_size, *refs):
     fused = mesh_size is not None
     refs = list(refs)
     take = lambda count: [refs.pop(0) for _ in range(count)]
-    flags_ref, x_ref = take(2)
+    offsets_ref, counts_ref, x_ref = take(3)
     if fused:
         n_dp, n_fs = mesh_size
-        shards = take(7)
+        small_in = take(7)
+        up_s, down_s, mixin_s, mixout_s, convin_s, convout_s = take(6)
     else:
-        up_ref, down_ref, mixin_ref, mixout_ref, convin_ref, table_in, bias_in = take(7)
+        first_v, second_v, third_v, table_in, bias_in = take(5)
     (
         h_out,
         x1_out,
@@ -655,7 +976,7 @@
         decay_ref,
         map_ref,
     ) = take(15)
-    gathered = take(9) if fused else []
+    gathered = take(4) if fused else []
     x1_scr, low_all, low_scr, sum_scr, state_scr, padded = take(6)
     step = pl.program_id(0)
     channels = x_ref.shape[1]
@@ -665,73 +986,65 @@
     gain = lambda k: table_ref[k : k + 1, :]
     shift = lambda k: table_ref[6 + k : 7 + k, :]
     here = lambda rows, tile: pl.ds(pl.multiple_of(tile * TILE + rows.start, ROWS), ROWS)
+    flags = carries(offsets_ref, counts_ref, tiles)
     if fused:
-        small_v, up_v, down_v, mixin_v, mixout_v, convin_v = take(WEIGHTS)
-        send_sem, recv_sem, local_sem, load_sem = take(4)
+        first_c, second_c, third_c = take(3)
+        sources = take(4)
+        turn_scr = refs.pop(0)
+        sems = take(3)
+        load_sem = refs.pop(0)
         swap = take(4)
         dp, fs = lax.axis_index("dp"), lax.axis_index("fsdp")
-        small_s, up_s, down_s, mixin_s, mixout_s, convin_s, convout_s = shards
-        sources = [
-            small_s.at[0],
-            up_s.at[0],
-            down_s.at[0],
-            mixin_s.at[0],
-            mixout_s.at[0],
-            convin_s.at[0],
-            convout_s.at[0],
-            up_s.at[1],
-            down_s.at[1],
-        ]
-        plans, sends = gather_plan(
-            dp, fs, n_dp, n_fs, sources, gathered, send_sem, recv_sem, local_sem
-        )
-        order = waves(plans)
-        ready = len(plans[0]) + 2
-        held = (small_v, up_v, down_v, mixin_v, mixout_v, convin_v)
-
-        def load(chunk):
-            return pltpu.make_async_copy(gathered[chunk], held[chunk], load_sem.at[chunk])
-
-        up_ref, down_ref, mixin_ref, mixout_ref, convin_ref = [ref_rows(r) for r in held[1:]]
+        place = Place(dp, fs, n_dp, n_fs)
+        landing = [first_c, second_c, third_c, gathered[3]]
+        plans, sends = block_gather(place, sources, landing, *sems)
+        first_v, second_v, third_v = [flat_groups(r) for r in landing[:3]]
+
+        def keep_copy(chunk):
+            return pltpu.make_async_copy(landing[chunk], gathered[chunk], load_sem.at[chunk])
+
+        def run(*stages):
+            for chunk, stage in stages:
+                plans[chunk][stage]()
 
         @pl.when(step == 0)
         def _():
+            pack_small(sources[0].at[0], turn_scr, dp * n_fs + fs, *small_in)
+            for k in range(4):
+                cols = slice(k * WIDTH, k * WIDTH + WIDTH)
+                sources[0][1 + k] = up_s[0, :, cols]
+                sources[3][1 + k] = up_s[1, :, cols]
+                rows = slice(k * PIECE, k * PIECE + PIECE)
+                sources[1][k] = down_s[0, rows, :]
+                sources[3][5 + k] = down_s[1, rows, :]
+            for k in range(2):
+                cols = slice(k * WIDTH, k * WIDTH + WIDTH)
+                sources[2][k] = mixin_s[:, cols]
+                sources[2][3 + k] = convin_s[:, cols]
+            sources[2][2] = mixout_s[...]
+            sources[3][0] = convout_s[...]
             greet(dp, fs, n_dp, n_fs)
-            for wave in order[:ready]:
-                for stage in wave:
-                    stage()
-            for chunk in range(3):
-                load(chunk).start()
-            load(0).wait()
-            table_ref[...] = ref_rows(small_v)[:, :256].astype(F32).T[: table_ref.shape[0], :]
-            total = small_v[0, :, 256:].astype(F32)
+            run((0, 0), (1, 0), (0, 1), (1, 1), (2, 0), (0, 2), (1, 2), (0, 3), (2, 1), (1, 3), (0, 4))
+            table_ref[...] = first_v[:, 0, :, :CHUNK].reshape((channels, CHUNK)).astype(F32).T[:TABLE, :]
+            total = first_v[0, 0, :, CHUNK:].astype(F32)
             for k in range(1, n_dp * n_fs):
-                total = total + small_v[k, :, 256:].astype(F32)
+                total = total + first_v[k, 0, :, CHUNK:].astype(F32)
             bias_ref[...] = total
-            load(1).wait()
-            load(2).wait()
-
-        for k in range(1, tiles + 1):
-
-            @pl.when(step == k)
-            def _(k=k):
-                for stage in order[ready + k - 1]:
-                    stage()
-                if k == tiles:
-                    for chunk in range(3, 6):
-                        load(chunk).start()
-                    for chunk in range(3, 6):
-                        load(chunk).wait()
-
-        rest = order[ready + tiles :]
-        for k in range(tiles):
-
-            @pl.when(step == tiles + 1 + k)
-            def _(k=k):
-                for wave in rest[k :: tiles] if k < tiles - 1 else rest[k:]:
-                    for stage in wave:
-                        stage()
-                if k == tiles - 1:
+            run((1, 4))
+
+        rest = {1: [(2, 2), (3, 0)], 2: [(2, 3)], tiles: [(2, 4), (3, 1)]}
+        rest.update({tiles + 1: [(3, 2)], tiles + 2: [(3, 3)], 2 * tiles: [(3, 4)]})
+        for at, stages in rest.items():
+
+            @pl.when(step == at)
+            def _(at=at, stages=stages):
+                run(*stages)
+                if at == tiles:
+                    for chunk in range(3):
+                        keep_copy(chunk).start()
+                if at == 2 * tiles:
+                    for chunk in range(3):
+                        keep_copy(chunk).wait()
                     for wait in sends:
                         wait()
 
@@ -760,13 +1073,13 @@
 
         def hidden(c, _):
             cols = columns(c)
-            h = dot_nn(low_scr[...], up_ref[:, cols]) + bias_ref[pl.ds(c, 1), :]
+            h = dot_nn(low_scr[...], cols_of(first_v, 1, c)) + bias_ref[pl.ds(c, 1), :]
             h_out[:, cols] = h.astype(BF16)
             active = (h * sigmoid(h)).astype(BF16)
-            sum_scr[...] += dot_nn(active, down_ref[cols, :])
+            sum_scr[...] += dot_nn(active, rows_of(second_v, 0, c))
             return 0
 
-        lax.fori_loop(0, up_ref.shape[1] // CHUNK, hidden, 0)
+        lax.fori_loop(0, h_out.shape[1] // CHUNK, hidden, 0)
 
         def second(rows):
             x1 = x_ref[rows, :].astype(F32) + 0.5 * (sum_scr[rows, :] + shift(6))
@@ -784,14 +1097,14 @@
 
         def project(c, _):
             cols = columns(c)
-            right = columns(c + channels // CHUNK)
-            u_out[:, cols] = dot_nn(low_all[whole_tile, :], mixin_ref[:, cols])
-            v_out[:, cols] = dot_nn(low_all[whole_tile, :], mixin_ref[:, right]).astype(BF16)
+            low = low_all[whole_tile, :]
+            u_out[:, cols] = dot_nn(low, cols_of(third_v, 0, c))
+            v_out[:, cols] = dot_nn(low, cols_of(third_v, 1, c)).astype(BF16)
             return 0
 
         lax.fori_loop(0, channels // CHUNK, project, 0)
         low_half = half_masks(128)
-        state_scr[...] = state_scr[...] * flags_ref[at].astype(F32)
+        state_scr[...] = state_scr[...] * pick(flags, at)
 
         def scan_span(span, _):
             hold_out[span] = state_scr[...]
@@ -824,7 +1137,7 @@
             gated_out[rows, :] = (y * (v * sigmoid(v))).astype(BF16)
 
         by_rows(gate)
-        sum_scr[...] = dot_nn(gated_out[...], mixout_ref[...])
+        sum_scr[...] = dot_nn(gated_out[...], square_of(third_v, 2))
 
         def third(rows):
             x2 = x1_scr[here(rows, at), :] + (sum_scr[rows, :] + shift(8))
@@ -838,8 +1151,8 @@
         def widen(c, _):
             cols = columns(c)
             right = columns(c + channels // CHUNK)
-            left_part = dot_nn(low_scr[...], convin_ref[:, cols]) + table_ref[15:16, cols]
-            right_part = dot_nn(low_scr[...], convin_ref[:, right]) + table_ref[16:17, cols]
+            left_part = dot_nn(low_scr[...], cols_of(third_v, 3, c)) + table_ref[15:16, cols]
+            right_part = dot_nn(low_scr[...], cols_of(third_v, 4, c)) + table_ref[16:17, cols]
             p_out[:, cols] = left_part.astype(BF16)
             p_out[:, right] = right_part.astype(BF16)
             g = left_part * sigmoid(right_part)
@@ -852,7 +1165,7 @@
 
     @pl.when(step == 2 * tiles)
     def _():
-        fill_halo(padded, flags_ref, tiles)
+        fill_halo(padded, flags, tiles)
 
         def store(lane, row, base, total):
             w_out[pl.ds(pl.multiple_of(row, 64), 64), lane * 128 : lane * 128 + 128] = total
@@ -903,10 +1216,13 @@
     )
 
 
-def front(mesh_size, flags, x, weights, collective_id=None):
+SMEM_SPEC = pl.BlockSpec(memory_space=pltpu.SMEM)
+HBM_SPEC = pl.BlockSpec(memory_space=pltpu.HBM)
+
+
+def front(mesh_size, offsets, counts, x, small, weights, hidden, collective_id=None):
     fused = mesh_size is not None
     frames, channels = x.shape
-    hidden = weights[1].shape[-1] if fused else weights[0].shape[1]
     tiles = frames // TILE
     early = lambda width: pl.BlockSpec((TILE, width), lambda i: (jnp.minimum(i, tiles - 1), 0))
     place = lambda i: jnp.clip(i - tiles, 0, tiles - 1)
@@ -946,63 +1262,28 @@
         pltpu.VMEM((STATES, channels), F32),
         pltpu.VMEM((channels // 128, tiles * (TILE + 2 * REACH), 128), F32),
     ]
-    in_specs = [pl.BlockSpec(memory_space=pltpu.SMEM), early(channels)]
+    operands = (weights if not fused else small + weights) + (small if not fused else [])
     if fused:
-        n_dp, n_fs = mesh_size
-        hbm = pl.BlockSpec(memory_space=pltpu.HBM)
-        in_specs += [hbm] * len(weights)
-        chunks = []
-        for at in (0, 1, 2, 3, 4, 5, 6, 1, 2):
-            chunks.append(jax.ShapeDtypeStruct((n_dp * n_fs,) + weights[at].shape[1:], BF16))
+        layout = block_layout(*mesh_size)
+        blocks = (5, 4, 5, 9)
+        chunks = [jax.ShapeDtypeStruct(layout + (k, PIECE, WIDTH), BF16) for k in blocks]
         out_shape += chunks
-        out_specs += [hbm] * len(chunks)
-        scratch += [pltpu.VMEM(c.shape, BF16) for c in chunks[:WEIGHTS]]
-        count = slot_count(n_dp, n_fs)
-        scratch += [
-            pltpu.SemaphoreType.DMA((len(chunks), count)),
-            pltpu.SemaphoreType.DMA((len(chunks), count)),
-            pltpu.SemaphoreType.DMA((len(chunks),)),
-            pltpu.SemaphoreType.DMA((WEIGHTS,)),
-        ]
-        scratch += swap_scratch(n_dp, n_fs, channels)
-    else:
-        in_specs += [whole(a.shape) for a in weights]
+        out_specs += [HBM_SPEC] * len(chunks)
+        scratch += [pltpu.VMEM(c.shape, BF16) for c in chunks[:3]]
+        scratch += [pltpu.VMEM((k, PIECE, WIDTH), BF16) for k in blocks]
+        scratch += [pltpu.VMEM((CHUNK, 128), F32)]
+        scratch += block_sems(*mesh_size, len(chunks)) + [pltpu.SemaphoreType.DMA((3,))]
+        scratch += swap_scratch(*mesh_size, channels)
     return pl.pallas_call(
         partial(front_kernel, mesh_size),
         grid=(2 * tiles + 1,),
-        in_specs=in_specs,
+        in_specs=[SMEM_SPEC, SMEM_SPEC, early(channels)] + [whole(a.shape) for a in operands],
         out_specs=out_specs,
         out_shape=out_shape,
         scratch_shapes=scratch,
         compiler_params=params(collective_id),
         name="front",
-    )(flags, x, *weights)
-
-
-def ffn_back(low_t, grad_t, grad_ref, h_load, up_ref, down_ref, up_acc, down_acc, bias_acc, back_scr, hidden):
-    def chunk(c, _):
-        cols = columns(c)
-        h = h_load(cols)
-        sig = sigmoid(h)
-        active = h * sig
-        gate = dot_nt(grad_ref[...], down_ref[cols, :])
-        grad_h = (gate * (sig * (1.0 + h - active))).astype(BF16)
-        bias_acc[:, cols] += fold8(grad_h.astype(F32))
-        down_acc[cols, :] += dot_tn(active.astype(BF16), grad_ref[...])
-        up_acc[:, cols] += dot_nn(low_t[...], grad_h)
-        back_scr[...] += dot_nt(grad_h, up_ref[:, cols])
-        return 0
-
-    lax.fori_loop(0, hidden // CHUNK, chunk, 0)
-
-
-def convert_rows(out, acc, step=64):
-    def run(at, _):
-        rows = pl.ds(pl.multiple_of(at * step, step), step)
-        out[rows, :] = acc[rows, :].astype(BF16)
-        return 0
-
-    lax.fori_loop(0, acc.shape[0] // step, run, 0)
+    )(offsets, counts, x, *operands)
 
 
 def middle_kernel(
@@ -1010,18 +1291,14 @@
     x2_ref,
     w_ref,
     cot_ref,
-    up_ref,
-    down_ref,
-    convout_ref,
+    blocks_ref,
     bias_ref,
     vec_ref,
     stat_ref,
     out_ref,
     gx3_ref,
     gnb_ref,
-    gup_out,
-    gdown_out,
-    gconvout_out,
+    gblocks_out,
     gbias_out,
     gvec_out,
     stat_out,
@@ -1050,7 +1327,7 @@
         def _():
             greet(dp, fs, n_dp, n_fs)
 
-    hidden = up_ref.shape[1]
+    hidden = up_acc.shape[1]
     gain = lambda k: vec_ref[k : k + 1, :]
     shift = lambda k: vec_ref[6 + k : 7 + k, :]
     center, scale = stat_ref[0:1, :], stat_ref[1:2, :]
@@ -1069,7 +1346,7 @@
         act_scr[rows, :] = (nb * sigmoid(nb)).astype(BF16)
 
     by_rows(first)
-    sum_scr[...] = dot_nn(act_scr[...], convout_ref[...])
+    sum_scr[...] = dot_nn(act_scr[...], square_of(blocks_ref, 0))
 
     def second(rows):
         x3 = x2_ref[rows, :] + (sum_scr[rows, :] + vec_ref[18:19, :])
@@ -1082,10 +1359,10 @@
 
     def forward(c, _):
         cols = columns(c)
-        h = dot_nn(low_scr[...], up_ref[:, cols]) + bias_ref[pl.ds(8 + c, 1), :]
+        h = dot_nn(low_scr[...], cols_of(blocks_ref, 1, c)) + bias_ref[pl.ds(8 + c, 1), :]
         h_scr[:, cols] = h
         active = (h * sigmoid(h)).astype(BF16)
-        sum_scr[...] += dot_nn(active, down_ref[cols, :])
+        sum_scr[...] += dot_nn(active, rows_of(blocks_ref, 5, c))
         return 0
 
     lax.fori_loop(0, hidden // CHUNK, forward, 0)
@@ -1106,19 +1383,21 @@
         sum_scr[rows, :] = jnp.zeros((ROWS, channels), F32)
 
     by_rows(last)
-    ffn_back(
-        turn_scr,
-        None,
-        grad_scr,
-        lambda cols: h_scr[:, cols],
-        up_ref,
-        down_ref,
-        up_acc,
-        down_acc,
-        bias_acc,
-        sum_scr,
-        hidden,
-    )
+
+    def backward(c, _):
+        cols = columns(c)
+        h = h_scr[:, cols]
+        sig = sigmoid(h)
+        active = h * sig
+        gate = dot_nt(grad_scr[...], rows_of(blocks_ref, 5, c))
+        grad_h = (gate * (sig * (1.0 + h - active))).astype(BF16)
+        bias_acc[:, cols] += fold8(grad_h.astype(F32))
+        down_acc[cols, :] += dot_tn(active.astype(BF16), grad_scr[...])
+        up_acc[:, cols] += dot_nn(turn_scr[...], grad_h)
+        sum_scr[...] += dot_nt(grad_h, cols_of(blocks_ref, 1, c))
+        return 0
+
+    lax.fori_loop(0, hidden // CHUNK, backward, 0)
 
     def fourth(rows):
         e, inv = norm_parts(x3_scr[rows, :])
@@ -1133,7 +1412,7 @@
 
     by_rows(fourth)
     convout_acc[...] += dot_tn(act_scr[...], grad_scr[...])
-    sum_scr[...] = dot_nt(grad_scr[...], convout_ref[...])
+    sum_scr[...] = dot_nt(grad_scr[...], square_of(blocks_ref, 0))
 
     def fifth(rows):
         e, nb = normed(rows)
@@ -1151,9 +1430,9 @@
             gvec_out[k : k + 1, :] = jnp.sum(vec_acc[k], axis=0, keepdims=True)
 
         def convert():
-            convert_rows(gup_out, up_acc)
-            convert_rows(gdown_out, down_acc)
-            convert_rows(gconvout_out, convout_acc)
+            store_wide(gblocks_out, 0, convout_acc)
+            store_wide(gblocks_out, 1, up_acc)
+            store_tall(gblocks_out, 5, down_acc)
             gbias_out[...] = jnp.broadcast_to(
                 jnp.sum(bias_acc[...], axis=0, keepdims=True), gbias_out.shape
             )
@@ -1168,19 +1447,15 @@
             stat_out[3:4, :] = total[6:7, :] * share
 
 
-def middle(mesh_size, x2, w, cot, up, down, convout, bias, vec, stat, collective_id=None):
+def middle(mesh_size, x2, w, cot, blocks, bias, vec, stat, hidden, collective_id=None):
     frames, channels = x2.shape
-    hidden = up.shape[1]
     tiles = frames // TILE
     row = lambda width: pl.BlockSpec((TILE, width), lambda i: (i, 0))
-    big = lambda a: pltpu.VMEM(a.shape, F32)
     shapes = [
         jax.ShapeDtypeStruct((frames, channels), BF16),
         jax.ShapeDtypeStruct((frames, channels), F32),
         jax.ShapeDtypeStruct((frames, channels), F32),
-        jax.ShapeDtypeStruct(up.shape, BF16),
-        jax.ShapeDtypeStruct(down.shape, BF16),
-        jax.ShapeDtypeStruct(convout.shape, BF16),
+        jax.ShapeDtypeStruct(blocks.shape, BF16),
         jax.ShapeDtypeStruct((8, hidden), F32),
         jax.ShapeDtypeStruct((8, channels), F32),
         jax.ShapeDtypeStruct((8, channels), F32),
@@ -1190,13 +1465,13 @@
         partial(middle_kernel, mesh_size),
         grid=(tiles,),
         in_specs=[row(channels)] * 3
-        + [whole(a.shape) for a in (up, down, convout, bias, vec, stat)],
+        + [whole(a.shape) for a in (blocks, bias, vec, stat)],
         out_specs=[row(channels)] * 3 + [whole(s.shape) for s in shapes[3:]],
         out_shape=shapes,
         scratch_shapes=[
-            big(up),
-            big(down),
-            big(convout),
+            pltpu.VMEM((channels, hidden), F32),
+            pltpu.VMEM((hidden, channels), F32),
+            pltpu.VMEM((channels, channels), F32),
             pltpu.VMEM((8, hidden), F32),
             pltpu.VMEM((8, 8, channels), F32),
             pltpu.VMEM((TILE, hidden), F32),
@@ -1210,7 +1485,7 @@
         + swap,
         compiler_params=params(collective_id),
         name="middle",
-    )(x2, w, cot, up, down, convout, bias, vec, stat)
+    )(x2, w, cot, blocks, bias, vec, stat)
 
 
 def back_kernel(mesh_size, *refs):
@@ -1218,7 +1493,8 @@
     refs = list(refs)
     take = lambda count: [refs.pop(0) for _ in range(count)]
     (
-        flags_ref,
+        offsets_ref,
+        counts_ref,
         w_ref,
         gnb_ref,
         p_all,
@@ -1230,26 +1506,22 @@
         u_ref,
         x1_ref,
         hold_ref,
-        convin_ref,
-        mixout_ref,
-        mixin_ref,
+        blocks_ref,
         vec_ref,
         stat_ref,
         decay_ref,
         map_ref,
-    ) = take(19)
-    sources = take(3) if fused else []
+    ) = take(18)
+    sources = take(1) if fused else []
     (
         gx1_ref,
-        gconvin_out,
-        gmixout_out,
-        gmixin_out,
+        gblocks_out,
         gvec_out,
         gtaps_ref,
         gmap_out,
         gdecay_out,
-    ) = take(8)
-    reduced = take(3) if fused else []
+    ) = take(6)
+    reduced = take(1) if fused else []
     (
         convin_acc,
         mixout_acc,
@@ -1275,18 +1547,18 @@
     gain = lambda k: vec_ref[k : k + 1, :]
     shift = lambda k: vec_ref[6 + k : 7 + k, :]
     left, right = slice(0, channels), slice(channels, 2 * channels)
+    flags = carries(offsets_ref, counts_ref, tiles)
     if fused:
         n_dp, n_fs = mesh_size
-        scratch = take(12)
-        dp, fs = lax.axis_index("dp"), lax.axis_index("fsdp")
+        place = Place(lax.axis_index("dp"), lax.axis_index("fsdp"), n_dp, n_fs)
+        scratch = take(2 + place.count)
 
         def emit(chunk, total):
             reduced[chunk][...] = total
 
-        plans, sends = scatter_plan(dp, fs, n_dp, n_fs, sources, emit, scratch, *take(3))
+        plans, sends = block_scatter(place, sources, emit, scratch, *take(3))
         order = waves(plans)
-        points = [(0, 0), (0, 1), (0, 2), (1, 0), (1, 3), (1, 4), (2, 0), (2, 3), (2, 4)]
-        points += [(tiles, 4)] * (len(order) - len(points))
+        points = [(0, 0), (0, 2), (1, 0), (1, 3), (2, 0)]
 
     def progress(point):
         if not fused:
@@ -1304,7 +1576,7 @@
         for ref in (convin_acc, mixout_acc, mixin_acc, vec_acc, map_acc, decay_acc, adj_scr):
             ref[...] = jnp.zeros_like(ref)
         if fused:
-            greet(dp, fs, n_dp, n_fs)
+            greet(place.dp, place.fs, n_dp, n_fs)
 
     progress(0)
 
@@ -1329,8 +1601,8 @@
             return 0
 
         lax.fori_loop(0, tiles * per, fill, 0)
-        fill_halo(padded, flags_ref, tiles)
-        fill_halo(gpad, flags_ref, tiles)
+        fill_halo(padded, flags, tiles)
+        fill_halo(gpad, flags, tiles)
 
     progress(1)
 
@@ -1380,7 +1652,9 @@
         by_rows(first)
         turned = low_scr[...].T
         convin_acc[...] += dot_nn(turned, wide_scr[...])
-        sum_scr[...] = dot_nt(wide_scr[...], convin_ref[...])
+        sum_scr[...] = dot_nt(wide_scr[:, left], square_of(blocks_ref, 3)) + dot_nt(
+            wide_scr[:, right], square_of(blocks_ref, 4)
+        )
 
         def second(rows):
             e, inv = norm_parts(x2_ref[rows, :])
@@ -1396,7 +1670,7 @@
         by_rows(second)
         progress(3)
         mixout_acc[...] += dot_tn(gated_ref[...], low_scr[...])
-        sum_scr[...] = dot_nt(low_scr[...], mixout_ref[...])
+        sum_scr[...] = dot_nt(low_scr[...], square_of(blocks_ref, 2))
 
         def third(rows):
             grad = sum_scr[rows, :]
@@ -1414,7 +1688,7 @@
         progress(4)
         low_half = half_masks(128)
         later = jnp.minimum(at + 1, tiles - 1)
-        adj_scr[...] = adj_scr[...] * flags_ref[later].astype(F32)
+        adj_scr[...] = adj_scr[...] * pick(flags, later)
 
         def span_back(index, _):
             span = TILE // SPAN - 1 - index
@@ -1470,7 +1744,9 @@
         by_rows(fourth)
         turned = low_scr[...].T
         mixin_acc[...] += dot_nn(turned, wide_scr[...])
-        sum_scr[...] = dot_nt(wide_scr[...], mixin_ref[...])
+        sum_scr[...] = dot_nt(wide_scr[:, left], square_of(blocks_ref, 0)) + dot_nt(
+            wide_scr[:, right], square_of(blocks_ref, 1)
+        )
 
         def fifth(rows):
             e, inv = norm_parts(x1_ref[rows, :])
@@ -1483,9 +1759,9 @@
 
         @pl.when(step == tiles)
         def _():
-            convert_rows(gconvin_out, convin_acc)
-            convert_rows(gmixout_out, mixout_acc)
-            convert_rows(gmixin_out, mixin_acc)
+            store_wide(gblocks_out, 0, mixin_acc)
+            store_wide(gblocks_out, 2, mixout_acc)
+            store_wide(gblocks_out, 3, convin_acc)
             for k in range(8):
                 gvec_out[k : k + 1, :] = jnp.sum(vec_acc[k], axis=0, keepdims=True)
             gmap_out[...] = map_acc[...]
@@ -1503,20 +1779,17 @@
                 wait()
 
 
-def back(mesh_size, flags, w, gnb, p, x2, gx3, gated, y, v, u, x1, hold, convin, mixout, mixin, vec, stat, decay, maps, grads=(), collective_id=None):
+def back(mesh_size, offsets, counts, wholes, tiled, hold, blocks, vec, stat, decay, maps, grads=(), collective_id=None):
     fused = mesh_size is not None
-    frames, channels = x2.shape
+    frames, channels = wholes[0].shape
     tiles = frames // TILE
     place = lambda i: tiles - jnp.maximum(i, 1)
     row = lambda width: pl.BlockSpec((TILE, width), lambda i: (place(i), 0))
     spans = TILE // SPAN
-    big = lambda a: pltpu.VMEM(a.shape, F32)
     state = jax.ShapeDtypeStruct((STATES, channels), F32)
     shapes = [
         jax.ShapeDtypeStruct((frames, channels), F32),
-        jax.ShapeDtypeStruct(convin.shape, BF16),
-        jax.ShapeDtypeStruct(mixout.shape, BF16),
-        jax.ShapeDtypeStruct(mixin.shape, BF16),
+        jax.ShapeDtypeStruct(blocks.shape, BF16),
         jax.ShapeDtypeStruct((8, channels), F32),
         jax.ShapeDtypeStruct((16, channels), F32),
         state,
@@ -1524,9 +1797,9 @@
     ]
     pad = pltpu.VMEM((channels // 128, tiles * (TILE + 2 * REACH), 128), F32)
     scratch = [
-        big(convin),
-        big(mixout),
-        big(mixin),
+        pltpu.VMEM((channels, 2 * channels), F32),
+        pltpu.VMEM((channels, channels), F32),
+        pltpu.VMEM((channels, 2 * channels), F32),
         pltpu.VMEM((8, 8, channels), F32),
         pltpu.VMEM((STATES, channels), F32),
         pltpu.VMEM((STATES, channels), F32),
@@ -1540,24 +1813,25 @@
         pad,
     ]
     if fused:
-        tails = [g.shape[1:] for g in grads]
-        shapes += [jax.ShapeDtypeStruct(t, F32) for t in tails]
-        scratch += scatter_scratch(*mesh_size, tails) + scatter_sems(*mesh_size, len(tails))
+        counts_of = [g.shape[-3] for g in grads]
+        shapes += [jax.ShapeDtypeStruct((k, PIECE, WIDTH), F32) for k in counts_of]
+        scratch += block_scratch(*mesh_size, counts_of, (PIECE, WIDTH))
+        scratch += block_sems(*mesh_size, len(grads))
     return pl.pallas_call(
         partial(back_kernel, mesh_size),
         grid=(tiles + 1,),
-        in_specs=[pl.BlockSpec(memory_space=pltpu.SMEM)]
-        + [whole(a.shape) for a in (w, gnb, p)]
-        + [row(channels)] * 7
+        in_specs=[SMEM_SPEC, SMEM_SPEC]
+        + [whole(a.shape) for a in wholes]
+        + [row(channels)] * len(tiled)
         + [pl.BlockSpec((spans, STATES, channels), lambda i: (place(i), 0, 0))]
-        + [whole(a.shape) for a in (convin, mixout, mixin, vec, stat, decay, maps)]
-        + [pl.BlockSpec(memory_space=pltpu.HBM)] * len(grads),
+        + [whole(a.shape) for a in (blocks, vec, stat, decay, maps)]
+        + [HBM_SPEC] * len(grads),
         out_specs=[row(channels)] + [whole(s.shape) for s in shapes[1:]],
         out_shape=shapes,
         scratch_shapes=scratch,
         compiler_params=params(collective_id),
         name="back",
-    )(flags, w, gnb, p, x2, gx3, gated, y, v, u, x1, hold, convin, mixout, mixin, vec, stat, decay, maps, *grads)
+    )(offsets, counts, *wholes, *tiled, hold, blocks, vec, stat, decay, maps, *grads)
 
 
 def small_gradients(out, gvec1, gvec2, gvec3, gtaps, gmap, gdecay, table_ref):
@@ -1581,22 +1855,28 @@
     )
 
 
+def store_cols(out, at, value):
+    per = WIDTH // CHUNK
+    groups = value.shape[0] // PIECE
+    out[:, lax.div(at, per), :, columns(lax.rem(at, per))] = value.reshape((groups, PIECE, CHUNK))
+
+
 def tail_kernel(mesh_size, *refs):
     fused = mesh_size is not None
     refs = list(refs)
     take = lambda count: [refs.pop(0) for _ in range(count)]
     x_ref, h_ref, gx1_ref, up_ref, down_ref, table_ref = take(6)
+    hidden = 4 * WIDTH
     if fused:
         gvec1, gvec2, gtaps, gmap, gdecay, gbias1 = take(6)
-        sources = take(3)
+        sources = take(1)
         gx_ref, last_out = take(2)
-        reduced = take(7)
+        reduced = take(5)
     else:
         gx_ref, gvec_out, gbias_out, up_out, down_out = take(5)
     turn_scr, grad_scr, gh_scr, vec_acc, bias_scr = take(5)
     step = pl.program_id(0)
     frames, channels = x_ref.shape
-    hidden = up_ref.shape[1]
     chunks = hidden // CHUNK
     tiles = frames // TILE
     first_b, first_c = 1 + chunks, 1 + 2 * chunks
@@ -1604,32 +1884,30 @@
     if fused:
         n_dp, n_fs = mesh_size
         down_src, left_src, right_src, small_src, small_scr, gvec3 = take(6)
-        scratch = take(28)
+        dp, fs = lax.axis_index("dp"), lax.axis_index("fsdp")
+        place = Place(dp, fs, n_dp, n_fs)
+        scratch = take(5 * (2 + place.count))
         sems = take(3)
         swap = take(4)
-        dp, fs = lax.axis_index("dp"), lax.axis_index("fsdp")
-        down_out = ref_rows(down_src)
-        halves = (ref_rows(left_src), ref_rows(right_src))
+        down_out = flat_groups(down_src)
+        halves = (flat_groups(left_src), flat_groups(right_src))
 
         def emit(chunk, total):
             reduced[chunk][...] = total
 
-        plans, sends = scatter_plan(
-            dp,
-            fs,
-            n_dp,
-            n_fs,
-            sources + [down_src, left_src, right_src, small_src],
-            emit,
-            scratch,
-            *sems,
+        plans, sends = block_scatter(
+            place, sources + [down_src, left_src, right_src, small_src], emit, scratch, *sems
         )
-        depth = len(plans[0])
-        starts = [0, 0, 0, first_b, first_b + chunks // 2, first_c, first_c]
-        for chunk, begin in enumerate(starts):
-            for stage in range(depth):
-                at = begin + 2 * stage if chunk < 5 else begin + stage
-                schedule.setdefault(min(at, first_c + tiles), []).append((stage, chunk))
+        begins = [
+            (0, 3, 5, 7, 9),
+            (first_b, first_b + 2, first_b + 4, first_b + 6, first_c),
+            (first_b + 4, first_b + 6, first_c, first_c + 1, first_c + 2),
+            (first_c, first_c + 1, first_c + 2, first_c + tiles, first_c + tiles),
+            (first_c, first_c + 1, first_c + 2, first_c + tiles, first_c + tiles),
+        ]
+        for chunk, steps in enumerate(begins):
+            for stage, at in enumerate(steps):
+                schedule.setdefault(at, []).append((stage, chunk))
     last_step = first_c + tiles - 1
 
     def progress(at):
@@ -1665,13 +1943,15 @@
     def _():
         h = h_ref[...].astype(F32)
         active = (h * sigmoid(h)).astype(BF16)
-        down_out[columns(step - 1), :] = dot_tn(active, grad_scr[...]).astype(BF16)
+        value = dot_tn(active, grad_scr[...]).astype(BF16)
+        groups = CHUNK // (4 * PIECE)
+        down_out[pl.ds((step - 1) * groups, groups)] = value.reshape((groups, 4, PIECE, WIDTH))
 
     def second_half(c, store):
         cols = columns(c)
         h = h_ref[...].astype(F32)
         sig = sigmoid(h)
-        gate = dot_nt(grad_scr[...], down_ref[cols, :])
+        gate = dot_nt(grad_scr[...], rows_of(down_ref, 0, c))
         grad_h = (gate * (sig * (1.0 + h * (1.0 - sig)))).astype(BF16)
         gh_scr[:, cols] = grad_h
         bias_scr[pl.ds(c, 1), :] = jnp.sum(fold8(grad_h.astype(F32)), axis=0, keepdims=True)
@@ -1684,7 +1964,7 @@
             @pl.when((step >= begin) & (step < begin + chunks // 2))
             def _(half=half, begin=begin):
                 def store(value):
-                    halves[half][:, columns(step - begin)] = value
+                    store_cols(halves[half], step - begin, value)
 
                 second_half(step - first_b, store)
 
@@ -1693,7 +1973,7 @@
         @pl.when((step >= first_b) & (step < first_c))
         def _():
             def store(value):
-                up_out[:, columns(step - first_b)] = value
+                store_cols(up_out, step - first_b, value)
 
             second_half(step - first_b, store)
 
@@ -1704,24 +1984,24 @@
             gvec3[0:1, :] = jnp.sum(vec_acc[0], axis=0, keepdims=True)
             small_gradients(small_scr, gvec1, gvec2, gvec3, gtaps, gmap, gdecay, table_ref)
             narrow = small_scr[...].T.astype(BF16)
-            devices = small_src.shape[0]
-            small_src[:, :, :256] = narrow.reshape((devices, 16, 256))
+            devices = n_dp * n_fs
+            small_out = flat_groups(small_src)
+            small_out[:, 0, :, :CHUNK] = narrow.reshape((devices, PIECE, CHUNK))
             for c in range(chunks):
                 bias_scr[chunks + c : chunks + c + 1, :] = gbias1[0:1, c * CHUNK : c * CHUNK + CHUNK]
             bias = bias_scr[...].astype(BF16)
-            small_src[:, :, 256:] = jnp.broadcast_to(bias[None], (devices, 16, CHUNK))
+            small_out[:, 0, :, CHUNK:] = jnp.broadcast_to(bias[None], (devices, PIECE, CHUNK))
             progress(first_c)
 
     @pl.when(step >= first_c)
     def _():
         tile = step - first_c
         whole_tile = pl.ds(pl.multiple_of(tile * TILE, TILE), TILE)
-        back = [
-            dot_nt(gh_scr[whole_tile, :], up_ref[k * CHUNK : k * CHUNK + CHUNK, :])
-            for k in range(channels // CHUNK)
-        ]
-        for k, value in enumerate(back):
-            gx_ref[:, k * CHUNK : k * CHUNK + CHUNK] = value
+        total = dot_nt(gh_scr[whole_tile, :WIDTH], square_of(up_ref, 1))
+        for k in range(1, hidden // WIDTH):
+            cols = slice(k * WIDTH, k * WIDTH + WIDTH)
+            total = total + dot_nt(gh_scr[whole_tile, cols], square_of(up_ref, 1 + k))
+        gx_ref[...] = total
 
         def second(rows):
             here = pl.ds(pl.multiple_of(tile * TILE + rows.start, ROWS), ROWS)
@@ -1758,7 +2038,7 @@
 def tail(mesh_size, x, h, gx1, up, down, table, others=(), grads=(), collective_id=None):
     fused = mesh_size is not None
     frames, channels = x.shape
-    hidden = up.shape[1]
+    hidden = h.shape[1]
     tiles, chunks = frames // TILE, hidden // CHUNK
     first_b, first_c = 1 + chunks, 1 + 2 * chunks
     place = lambda i: jnp.where(
@@ -1773,23 +2053,22 @@
         pltpu.VMEM((2 * chunks, CHUNK), F32),
     ]
     if fused:
-        devices = mesh_size[0] * mesh_size[1]
-        tails = [g.shape[1:] for g in grads]
-        own = [(hidden // devices, channels)] + [(channels // devices, hidden // 2)] * 2
-        own.append((16, 2 * CHUNK))
+        own = [4, 2, 2, 1]
+        counts = [g.shape[-3] for g in grads] + own
         shapes.append(jax.ShapeDtypeStruct((8, channels), F32))
-        shapes += [jax.ShapeDtypeStruct(t, F32) for t in tails + own]
-        scratch += [pltpu.VMEM((devices,) + t, BF16) for t in own]
+        shapes += [jax.ShapeDtypeStruct((k, PIECE, WIDTH), F32) for k in counts]
+        layout = block_layout(*mesh_size)
+        scratch += [pltpu.VMEM(layout + (k, PIECE, WIDTH), BF16) for k in own]
         scratch += [pltpu.VMEM((256, channels), F32), pltpu.VMEM((8, channels), F32)]
-        scratch += scatter_scratch(*mesh_size, tails + own)
-        scratch += scatter_sems(*mesh_size, len(tails + own))
+        scratch += block_scratch(*mesh_size, counts, (PIECE, WIDTH))
+        scratch += block_sems(*mesh_size, len(counts))
         scratch += swap_scratch(*mesh_size, channels)
     else:
         shapes += [
             jax.ShapeDtypeStruct((8, channels), F32),
             jax.ShapeDtypeStruct((2 * chunks, CHUNK), F32),
-            jax.ShapeDtypeStruct(up.shape, BF16),
-            jax.ShapeDtypeStruct(down.shape, BF16),
+            jax.ShapeDtypeStruct((channels // PIECE, 4, PIECE, WIDTH), BF16),
+            jax.ShapeDtypeStruct((channels // PIECE, 4, PIECE, WIDTH), BF16),
         ]
     return pl.pallas_call(
         partial(tail_kernel, mesh_size),
@@ -1810,13 +2089,9 @@
 
 def unpack_kernel(
     place_ref,
-    up1_ref,
-    down1_ref,
-    convout_ref,
-    convin_ref,
-    mixout_ref,
-    mixin_ref,
-    down0_ref,
+    second_ref,
+    mixer_ref,
+    down_ref,
     left_ref,
     right_ref,
     small_ref,
@@ -1836,64 +2111,67 @@
     shifts_out,
 ):
     mine = place_ref[0]
-    half = left_ref.shape[1]
-    up_out[0, :, :half] = left_ref[...]
-    up_out[0, :, half:] = right_ref[...]
-    up_out[1] = up1_ref[...]
-    down_out[0] = down0_ref[...]
-    down_out[1] = down1_ref[...]
-    mixin_out[...] = mixin_ref[...]
-    mixout_out[...] = mixout_ref[...]
-    convin_out[...] = convin_ref[...]
-    convout_out[...] = convout_ref[...]
+    for k in range(4):
+        cols = slice(k * WIDTH, k * WIDTH + WIDTH)
+        rows = slice(k * PIECE, k * PIECE + PIECE)
+        up_out[0, :, cols] = (left_ref if k < 2 else right_ref)[k % 2]
+        up_out[1, :, cols] = second_ref[1 + k]
+        down_out[0, rows, :] = down_ref[k]
+        down_out[1, rows, :] = second_ref[5 + k]
+    convout_out[...] = second_ref[0]
+    mixout_out[...] = mixer_ref[2]
+    for k in range(2):
+        cols = slice(k * WIDTH, k * WIDTH + WIDTH)
+        mixin_out[:, cols] = mixer_ref[k]
+        convin_out[:, cols] = mixer_ref[3 + k]
     count = bias_out.shape[1]
     row = (mine * count) // CHUNK
     inner = mine * count - row * CHUNK
     for layer in range(2):
-        line = small_ref[pl.ds(8 * layer + row, 1), CHUNK:]
+        line = small_ref[0, pl.ds(8 * layer + row, 1), CHUNK:]
         line = pltpu.roll(jnp.broadcast_to(line, (8, CHUNK)), CHUNK - inner, 1)
         bias_out[layer : layer + 1, :] = line[0:1, :count]
-    own = small_ref.shape[0]
     channels = last_ref.shape[1]
-    first = pltpu.roll(last_ref[...], channels - mine * own, 1)[:, :128].T[:own, :]
-    small = small_ref[:, :256]
-    gains_out[...] = small[:, :6]
-    gains_out[:, 0:1] = first[:, 0:1]
-    shifts_out[...] = small[:, 6:18]
-    shifts_out[:, 0:1] = first[:, 1:2]
-    convbias_out[...] = small[:, 18:19]
-    taps_out[...] = small[:, TAP_ROW : TAP_ROW + TAPS]
+    first = pltpu.roll(last_ref[...], channels - mine * PIECE, 1)[:, :PIECE]
+    small = small_ref[0, :, :CHUNK]
+    turned = small.T
+    gains_out[...] = turned[0:6, :]
+    gains_out[0:1, :] = first[0:1, :]
+    shifts_out[...] = turned[6:18, :]
+    shifts_out[0:1, :] = first[1:2, :]
+    convbias_out[...] = turned[18:19, :]
+    taps_out[...] = turned[TAP_ROW : TAP_ROW + TAPS, :]
     rate_out[...] = small[:, RATE:MAP_IN]
     map_out[0] = small[:, MAP_IN:MAP_OUT]
     map_out[1] = small[:, MAP_OUT:TABLE]
 
 
-def unpack(mine, up1, down1, convout, convin, mixout, mixin, down0, left, right, small, last, hidden):
-    own = small.shape[0]
-    devices = last.shape[1] // own
+def unpack(mine, arrays, hidden):
+    channels = arrays[-1].shape[1]
+    devices = channels // PIECE
     f32 = lambda *shape: jax.ShapeDtypeStruct(shape, F32)
     vmem = pl.BlockSpec(memory_space=pltpu.VMEM)
     return pl.pallas_call(
         unpack_kernel,
-        in_specs=[pl.BlockSpec(memory_space=pltpu.SMEM)] + [vmem] * 11,
+        in_specs=[SMEM_SPEC] + [vmem] * len(arrays),
         out_specs=[vmem] * 13,
         out_shape=[
-            f32(2, *up1.shape),
-            f32(2, *down1.shape),
+            f32(2, PIECE, hidden),
+            f32(2, hidden // devices, channels),
             f32(2, hidden // devices),
-            f32(*mixin.shape),
-            f32(*mixout.shape),
-            f32(*convin.shape),
-            f32(*convout.shape),
-            f32(own, 1),
-            f32(own, STATES),
-            f32(2, own, STATES),
-            f32(own, TAPS),
-            f32(own, 6),
-            f32(own, 12),
+            f32(PIECE, 2 * WIDTH),
+            f32(PIECE, WIDTH),
+            f32(PIECE, 2 * WIDTH),
+            f32(PIECE, WIDTH),
+            f32(1, PIECE),
+            f32(PIECE, STATES),
+            f32(2, PIECE, STATES),
+            f32(TAPS, PIECE),
+            f32(6, PIECE),
+            f32(12, PIECE),
         ],
         name="unpack",
-    )(mine, up1, down1, convout, convin, mixout, mixin, down0, left, right, small, last)
+    )(mine, *arrays)
 
 
 def pack_table(gains, shifts, conv_bias, taps, rate, maps):
@@ -1949,127 +2227,108 @@
     devices = n_dp * n_fs
     mine = lax.axis_index("dp") * n_fs + lax.axis_index("fsdp")
     frames_dev, channels = frames.shape
-    tiles = frames_dev // TILE
-    slot = jnp.arange(seq_offsets.shape[1], dtype=jnp.int32)
-    begins = (seq_offsets[0][None, :] == TILE * jnp.arange(tiles, dtype=jnp.int32)[:, None]) & (
-        slot < seq_counts[0]
+    hidden = ffn_up.shape[2]
+    if channels // devices == PIECE:
+        size = (n_dp, n_fs)
+        small = [
+            ffn_bias_up,
+            gains,
+            shifts,
+            conv_out_bias[None],
+            conv_kernel,
+            ssm_rate.T,
+            ssm_map.transpose((0, 2, 1)),
+        ]
+        weights = [ffn_up, ffn_down, mix_in, mix_out, conv_in, conv_out]
+        made = front(size, seq_offsets, seq_counts, frames, small, weights, hidden, 1)
+        h0, x1, u, v, y, gated, x2, p, hold, w, stat, table, bias, decay, coupling = made[:15]
+        groups = lambda g: g.reshape((devices,) + g.shape[-3:])
+        places = lambda g: g.reshape(block_layout(n_dp, n_fs) + g.shape[1:])
+        first, second, third, fourth = [groups(g) for g in made[15:]]
+        result, gx3, gnb, grads, gbias1, gvec1, stat = middle(
+            size, x2, w, cotangent, fourth, bias, table, stat, hidden, 2
+        )
+        gx1, grads2, gvec2, gtaps, gmap, gdecay, reduced = back(
+            size,
+            seq_offsets,
+            seq_counts,
+            [w, gnb, p],
+            [x2, gx3, gated, y, v, u, x1],
+            hold,
+            third,
+            table,
+            stat,
+            decay,
+            coupling,
+            (places(grads),),
+            3,
+        )
+        others = (gvec1, gvec2, gtaps, gmap, gdecay, gbias1)
+        gx, last, *late = tail(
+            size, frames, h0, gx1, first, second, table, others, (places(grads2),), 4
+        )
+        made = unpack(mine.reshape((1,)), [reduced] + late + [last], hidden)
+        made = list(made)
+        made[7] = made[7].reshape((-1,))
+        made[8] = made[8].T
+        made[9] = made[9].transpose((0, 2, 1))
+        return (result, gx) + tuple(made)
+
+    small = pack_table(gains, shifts, conv_out_bias, conv_kernel, ssm_rate, ssm_map)
+    got = gather_all(
+        n_dp,
+        n_fs,
+        [
+            small[None],
+            pack_bias(ffn_bias_up, mine)[None],
+            ffn_up,
+            ffn_down,
+            mix_in[None],
+            mix_out[None],
+            conv_in[None],
+            conv_out[None],
+        ],
+        1,
     )
-    flags = 1 - jnp.max(begins.astype(jnp.int32), axis=1)
-    small = pack_table(gains, shifts, conv_out_bias, conv_kernel, ssm_rate, ssm_map)
-    bias = pack_bias(ffn_bias_up, mine)
-    fused = small.shape[0] % 16 == 0
-    shards = [ffn_up, ffn_down, mix_in[None], mix_out[None], conv_in[None], conv_out[None]]
-    if fused:
-        small = jnp.concatenate([small, bias], axis=1)
-        made = front((n_dp, n_fs), flags, frames, [small[None]] + shards, 1)
-        _, up0, down0, mixin, mixout, convin, convout, up1, down1 = [
-            g.reshape((-1, g.shape[-1])) for g in made[15:]
-        ]
-        stat = made[10]
-    else:
-        got = gather_all(n_dp, n_fs, [small[None], bias[None]] + shards, 1)
-        small, _, up0, up1, down0, down1, mixin, mixout, convin, convout = [
-            g.reshape((-1, g.shape[-1])) for g in got
-        ]
-        made = front(
-            None,
-            flags,
-            frames,
-            [
-                up0,
-                down0,
-                mixin,
-                mixout,
-                convin,
-                small.astype(F32).T[:TABLE],
-                jnp.sum(got[1].astype(F32), axis=0),
-            ],
-        )
-        pool = exchange(n_dp, n_fs, made[10], frames_dev, 2, pool_kernel)
-        scale = lax.rsqrt(pool[1:2] / (frames_dev * devices) + EPSILON)
-        stat = jnp.concatenate([pool[0:1], scale, jnp.zeros((6, channels), F32)])
-    h0, x1, u, v, y, gated, x2, p, hold, w, _, table, bias, decay, coupling = made[:15]
-    size = (n_dp, n_fs) if fused else None
-    result, gx3, gnb, gup1, gdown1, gconvout, gbias1, gvec1, stat = middle(
-        size, x2, w, cotangent, up1, down1, convout, bias, table, stat, 2 if fused else None
+    matrix = lambda g: g.reshape((-1, g.shape[-1]))
+    table, _, up0, up1, down0, down1, mixin, mixout, convin, convout = [matrix(g) for g in got]
+    table = table.astype(F32).T[:TABLE]
+    bias = jnp.sum(got[1].astype(F32), axis=0)
+    group_count = channels // PIECE
+    cut = lambda g: g.reshape((group_count, PIECE, -1, WIDTH)).transpose((0, 2, 1, 3))
+    tall = lambda g: g.reshape((group_count, -1, PIECE, WIDTH))
+    join = lambda g: g.transpose((0, 2, 1, 3)).reshape((channels, -1))
+    blank = jnp.zeros((group_count, 1, PIECE, WIDTH), BF16)
+    first = jnp.concatenate([blank, cut(up0)], axis=1)
+    third = jnp.concatenate([cut(mixin), cut(mixout), cut(convin)], axis=1)
+    fourth = jnp.concatenate([cut(convout), cut(up1), tall(down1)], axis=1)
+    made = front(
+        None, seq_offsets, seq_counts, frames, [table, bias], [first, tall(down0), third], hidden
     )
-    if not fused:
-        sums = exchange(n_dp, n_fs, gvec1, 1, 4, total_kernel)[6:8]
-        sums = sums * (table[5:6] / (frames_dev * devices))
-        stat = jnp.concatenate([stat[0:2], sums[1:2], sums[0:1], stat[4:8]])
-    wide = lambda g: g.reshape((devices, g.shape[0] // devices, g.shape[1]))
-    grads = tuple(wide(g) for g in (gup1, gdown1, gconvout))
-    made = back(
-        size,
-        flags,
-        w,
-        gnb,
-        p,
-        x2,
-        gx3,
-        gated,
-        y,
-        v,
-        u,
-        x1,
+    h0, x1, u, v, y, gated, x2, p, hold, w, stat, table, bias, decay, coupling = made
+    pool = exchange(n_dp, n_fs, stat, frames_dev, 2, pool_kernel)
+    scale = lax.rsqrt(pool[1:2] / (frames_dev * devices) + EPSILON)
+    stat = jnp.concatenate([pool[0:1], scale, jnp.zeros((6, channels), F32)])
+    result, gx3, gnb, grads, gbias1, gvec1, stat = middle(
+        None, x2, w, cotangent, fourth, bias, table, stat, hidden
+    )
+    sums = exchange(n_dp, n_fs, gvec1, 1, 4, total_kernel)[6:8]
+    sums = sums * (table[5:6] / (frames_dev * devices))
+    stat = jnp.concatenate([stat[0:2], sums[1:2], sums[0:1], stat[4:8]])
+    gx1, grads2, gvec2, gtaps, gmap, gdecay = back(
+        None,
+        seq_offsets,
+        seq_counts,
+        [w, gnb, p],
+        [x2, gx3, gated, y, v, u, x1],
         hold,
-        convin,
-        mixout,
-        mixin,
+        third,
         table,
         stat,
         decay,
         coupling,
-        grads if fused else (),
-        3 if fused else None,
     )
-    gx1, gconvin, gmixout, gmixin, gvec2, gtaps, gmap, gdecay = made[:8]
-    if fused:
-        gx, last, *late = tail(
-            size,
-            frames,
-            h0,
-            gx1,
-            up0,
-            down0,
-            table,
-            (gvec1, gvec2, gtaps, gmap, gdecay, gbias1),
-            tuple(wide(g) for g in (gconvin, gmixout, gmixin)),
-            4,
-        )
-        (
-            up_grad,
-            down_grad,
-            bias_grad,
-            mixin_grad,
-            mixout_grad,
-            convin_grad,
-            convout_grad,
-            convbias_grad,
-            rate_grad,
-            map_grad,
-            taps_grad,
-            gains_grad,
-            shifts_grad,
-        ) = unpack(mine.reshape((1,)), *made[8:], *late, last, up0.shape[1])
-        return (
-            result,
-            gx,
-            up_grad,
-            down_grad,
-            bias_grad,
-            mixin_grad,
-            mixout_grad,
-            convin_grad,
-            convout_grad,
-            convbias_grad.reshape((-1,)),
-            rate_grad.T,
-            map_grad.transpose((0, 2, 1)),
-            taps_grad.T,
-            gains_grad.T,
-            shifts_grad.T,
-        )
-    gx, gvec3, gbias0, gup0, gdown0 = tail(None, frames, h0, gx1, up0, down0, table)
+    gx, gvec3, gbias0, gup0, gdown0 = tail(None, frames, h0, gx1, first, tall(down0), table)
 
     def weights_of(log_rate, maps):
         log_decay = -jnp.exp(log_rate)
@@ -2085,14 +2344,21 @@
         gain_grad, jnp.stack(rows), gvec1[5], gtaps[:TAPS], rate_grad, map_grad
     )
     bias_grad = jnp.concatenate([gbias0[:8], gbias1[0].reshape((8, CHUNK))])
+    wide = lambda g: g.reshape((devices, g.shape[0] // devices, g.shape[1]))
     reduced = scatter_all(
         n_dp,
         n_fs,
-        list(grads)
-        + [wide(g) for g in (gconvin, gmixout, gmixin, gup0, gdown0)]
-        + [
+        [
+            wide(join(grads[:, 1:5])),
+            wide(matrix(grads[:, 5:9])),
+            wide(join(grads[:, 0:1])),
+            wide(join(grads2[:, 3:5])),
+            wide(join(grads2[:, 2:3])),
+            wide(join(grads2[:, 0:2])),
+            wide(join(gup0)),
+            wide(matrix(gdown0)),
             wide(small_grad.astype(BF16)),
-            jnp.broadcast_to(bias_grad.astype(BF16), (devices, 16, CHUNK)),
+            jnp.broadcast_to(bias_grad.astype(BF16), (devices, PIECE, CHUNK)),
         ],
         5,
     )

time: 412 us -> 393 us (0.954)
  local copies, waits for them, and re-layouts: 13.8 us -> 4.32 us
  Pallas kernels: 393 us -> 387 us
    pallas_call x1, Pallas kernels: 124 us -> 117 us  [front(): pl.pallas_call(partial(front_kernel, mesh_size), grid=(2 * tiles + 1,), i...]
    unnamed x10 -> x4, local copies, waits for them, and re-layouts: 10.7 us -> 4.32 us
where the time goes in v3:
time: 393 us
  Pallas kernels  387 us (98%)
  local copies, waits for them, and re-layouts  4.32 us (1%)
    pallas_call x1, Pallas kernels, back(): pl.pallas_call(partial(back_kernel, mesh_size), grid=(tiles + 1,), in_spe...  120 us
    pallas_call x1, Pallas kernels, front(): pl.pallas_call(partial(front_kernel, mesh_size), grid=(2 * tiles + 1,), i...  117 us
    pallas_call x1, Pallas kernels, tail(): pl.pallas_call(partial(tail_kernel, mesh_size), grid=(first_c + tiles,),...  77.2 us
    pallas_call x1, Pallas kernels, middle(): pl.pallas_call(partial(middle_kernel, mesh_size), grid=(tiles,), in_specs...  70.8 us

profile of v3, /device:TPU:0, one launch (start us, length us, event | category | flops | bytes accessed | tf_op | source)
XLA Modules:
  0.0 392.7 jit_solution(4609575031136100024)
XLA Ops:
  1.3 117.2 %front.1 = (bf16[1536,2048]{1,0:T(8,128)(2,1)}, f32[1536,512]{1,0:T(8,128)}, f32[1536,512]{1,0:T(8,128)}, bf16[1536,512]{1,0:T(8,128)(2,1)}, bf16[1536,512]{1,0:...) custom-call(s32[1,3]{1,0:T(1,128)} %refs_0_.4, ...), custom_call_target="tpu_custom_call" | custom-call | tf_op jit(solution)/shard_map/front/pallas_call | solution.py:1277
  118.5 70.8 %middle.1 = (bf16[1536,512]{1,0:T(8,128)(2,1)}, f32[1536,512]{1,0:T(8,128)}, f32[1536,512]{1,0:T(8,128)}, bf16[32,9,16,512]{3,2,1,0:T(8,128)(2,1)}, f32[8,2048]{...) custom-call(f32[1536,512]{1,0:T(8,128)} %get-tuple-element.68.x2_ref.refs_5_, ...), custom_call_target="tpu_custom_call" | custom-call | tf_op jit(solution)/shard_map/middle/pallas_call | solution.py:1464
  189.3 119.7 %back.1 = (f32[1536,512]{1,0:T(8,128)}, bf16[32,5,16,512]{3,2,1,0:T(8,128)(2,1)}, f32[8,512]{1,0:T(8,128)}, f32[16,512]{1,0:T(8,128)}, f32[32,512]{1,0:T(8,128)}...) custom-call(s32[1,3]{1,0:T(1,128)} %refs_0_.4, s32[1]{0:T(128)S(6)} %copy.34.refs_1_, ...), custom_call_target="tpu_custom_call" | custom-call | tf_op jit(solution)/shard_map/back/pallas_call | solution.py:1820
  309.0 77.2 %tail.1 = (f32[1536,512]{1,0:T(8,128)}, f32[8,512]{1,0:T(8,128)}, f32[5,16,512]{2,1,0:T(8,128)}, f32[4,16,512]{2,1,0:T(8,128)}, f32[2,16,512]{2,1,0:T(8,128)}, /...) custom-call(bf16[1536,512]{1,0:T(8,128)(2,1)} %refs_0_.5, bf16[1536,2048]{1,0:T(8,128)(2,1)} %get-tuple-element.75.refs_1_, ...), custom_call_target="tpu_custom_call" | custom-call | tf_op jit(solution)/shard_map/tail/pallas_call | solution.py:2073
  386.2 0.0 copy-start
  386.2 2.2 unpack.1
  388.4 2.7 copy.35
  391.0 0.0 copy-done
  391.0 1.7 copy.36
Async XLA Ops:
  386.2 4.8 %copy-start = (f32[1536,512]{1,0:T(8,128)S(1)}, f32[1536,512]{1,0:T(8,128)}, u32[]{:S(2)}) copy-start(f32[1536,512]{1,0:T(8,128)} %get-tuple-element.137) | copy-start | bytes 9437188

commit v4 on v3

--- a/solution.py
+++ b/solution.py
@@ -720,7 +720,6 @@
 EPSILON = 1e-05
 CHUNK = 256
 ROWS = 128
-SPAN = 32
 VMEM_LIMIT = 60 << 20
 TAP_ROW = 24
 RATE = 40
@@ -772,25 +771,6 @@
 
 def columns(at, width=CHUNK):
     return pl.ds(pl.multiple_of(at * width, width), width)
-
-
-def merge_rows(parts, low_half):
-    for distance in (1, 2, 4):
-        low = low_half[distance]
-        parts = [
-            jnp.where(low, a, b) + pltpu.roll(jnp.where(low, b, a), distance, 0)
-            for a, b in zip(parts[0::2], parts[1::2])
-        ]
-    return parts[0]
-
-
-def half_masks(width):
-    row = lax.broadcasted_iota(jnp.int32, (8, width), 0)
-    return {d: (row // d) % 2 == 0 for d in (4, 2, 1)}
-
-
-def fold_states(v):
-    return jnp.sum(v.reshape((STATES // 8, 8, v.shape[1])), axis=0)
 
 
 def fill_halo(padded, flags, tiles):
@@ -871,9 +851,14 @@
 
 
 def rows_of(ref, first, at):
-    groups = CHUNK // (4 * PIECE)
+    groups = WIDTH // (4 * PIECE)
     part = ref[pl.ds(at * groups, groups), first : first + 4]
-    return part.reshape((CHUNK, WIDTH))
+    return part.reshape((WIDTH, WIDTH))
+
+
+def bias_of(ref, layer, at):
+    row = 8 * layer + 2 * at
+    return jnp.concatenate([ref[pl.ds(row, 1), :], ref[pl.ds(row + 1, 1), :]], axis=1)
 
 
 def square_of(ref, at):
@@ -917,11 +902,313 @@
     return out
 
 
-def pick(values, at):
-    total = values[0] * (at == 0).astype(F32)
-    for k in range(1, len(values)):
-        total = total + values[k] * (at == k).astype(F32)
-    return total
+STRETCH = 16
+SPREAD = PIECE * STATES
+
+
+def same_channel(rows, width, per, first=0):
+    shape = (rows, width)
+    row = lax.rem(lax.broadcasted_iota(jnp.int32, shape, 0), PIECE)
+    col = lax.broadcasted_iota(jnp.int32, shape, 1)
+    if per == 1:
+        return row == lax.rem(col, PIECE)
+    return row == lax.div(col, per)
+
+
+def split_low(v):
+    high = v.astype(BF16)
+    return high, (v - high.astype(F32)).astype(BF16)
+
+
+def spread_states(part):
+    rows = part.shape[0]
+    state = lax.broadcasted_iota(jnp.int32, (STATES, SPREAD), 0)
+    col = lax.broadcasted_iota(jnp.int32, (STATES, SPREAD), 1)
+    pick_state = (state == lax.rem(col, STATES)).astype(F32).astype(BF16)
+    wide = dot_nn(part, pick_state)
+    wide = jnp.where(same_channel(rows, SPREAD, STATES), wide, 0.0)
+    return jnp.sum(wide.reshape((rows // PIECE, PIECE, SPREAD)), axis=1)
+
+
+def gather_states(wide):
+    groups = wide.shape[0]
+    full = jnp.broadcast_to(wide[:, None, :], (groups, PIECE, SPREAD)).reshape((groups * PIECE, SPREAD))
+    full = jnp.where(same_channel(groups * PIECE, SPREAD, STATES), full, 0.0)
+    state = lax.broadcasted_iota(jnp.int32, (SPREAD, 128), 1)
+    row = lax.broadcasted_iota(jnp.int32, (SPREAD, 128), 0)
+    pick_state = (state == lax.rem(row, STATES)).astype(F32).astype(BF16)
+    high, low = split_low(full)
+    return (dot_nn(high, pick_state) + dot_nn(low, pick_state)).T[:STATES, :]
+
+
+def prepare_states(small, power, shifted, weight):
+    groups = small.shape[0]
+    entries = lambda first: small[:, :, first : first + STATES].reshape((groups * PIECE, STATES))
+    log_decay = -jnp.exp(spread_states(entries(RATE)))
+    root = jnp.sqrt(-2.0 * log_decay * small_expm1_over(2.0 * log_decay))
+    both = spread_states(entries(MAP_IN)) * root * spread_states(entries(MAP_OUT))
+    weight[...] = both
+    col = lax.broadcasted_iota(jnp.int32, (SPREAD, 128), 1)
+    row = lax.broadcasted_iota(jnp.int32, (SPREAD, 128), 0)
+    add_states = (col == lax.div(row, STATES)).astype(F32).astype(BF16)
+    power[0] = jnp.ones_like(both)
+    decay = small_exp(log_decay)
+    for m in range(1, STRETCH):
+        power[m] = power[m - 1] * decay
+    halves = []
+    for half in range(2):
+        total = jnp.zeros((groups, 128), F32)
+        for k in range(8):
+            high, low = split_low(power[half * 8 + k] * both)
+            lag = dot_nn(high, add_states) + dot_nn(low, add_states)
+            total = total + (pltpu.roll(lag, k * PIECE, 1) if k else lag)
+        halves.append(total)
+    blank = jnp.zeros((groups, 256), F32)
+    padded = jnp.concatenate([blank] + halves, axis=1)
+    for m in range(STRETCH):
+        shifted[m] = pltpu.roll(padded, 512 - (m + 1) * PIECE, 1)[:, :256]
+
+
+def group_weights(power, shifted, group, decay_w, lag_w):
+    mask = same_channel(PIECE, SPREAD, STATES)
+    lag_mask = same_channel(PIECE, 256, 1)
+    for m in range(STRETCH):
+        rows = slice(m * PIECE, m * PIECE + PIECE)
+        line = jnp.broadcast_to(power[m, pl.ds(group, 1), :], (PIECE, SPREAD))
+        decay_w[rows, :] = jnp.where(mask, line, 0.0).astype(BF16)
+        line = jnp.broadcast_to(shifted[m, pl.ds(group, 1), :], (PIECE, 256))
+        lag_w[rows, :] = jnp.where(lag_mask, line, 0.0).astype(BF16)
+
+
+def swap_blocks(parts):
+    col = lax.div(lax.broadcasted_iota(jnp.int32, parts[0].shape, 1), PIECE)
+    parts = list(parts)
+    for distance in (1, 2, 4):
+        low = lax.rem(lax.div(col, distance), 2) == 0
+        shift = distance * PIECE
+        for a in range(8):
+            if a & distance:
+                continue
+            first, second = parts[a], parts[a + distance]
+            parts[a] = jnp.where(low, first, pltpu.roll(second, shift, 1))
+            parts[a + distance] = jnp.where(low, pltpu.roll(first, 128 - shift, 1), second)
+    return parts
+
+
+SLAB = 32
+TOGETHER = 4
+
+
+def to_blocks(load, out, blocks, backward):
+    for slab in range(blocks // SLAB):
+        rows = slice(slab * SLAB, slab * SLAB + SLAB)
+        for half in range(2):
+            parts = []
+            for k in range(8):
+                frame = half * 8 + k
+                frame = STRETCH - 1 - frame if backward else frame
+                parts.append(load(slab * SLAB * STRETCH + frame))
+            for group, part in enumerate(swap_blocks(parts)):
+                out[group, rows, half * 128 : half * 128 + 128] = part.astype(out.dtype)
+
+
+def from_blocks(store, ref, blocks, backward):
+    for slab in range(blocks // SLAB):
+        rows = slice(slab * SLAB, slab * SLAB + SLAB)
+        for half in range(2):
+            parts = [ref[group, rows, half * 128 : half * 128 + 128] for group in range(8)]
+            for k, part in enumerate(swap_blocks(parts)):
+                frame = half * 8 + k
+                frame = STRETCH - 1 - frame if backward else frame
+                store(slab * SLAB * STRETCH + frame, part)
+
+
+def block_powers(decay):
+    q2 = decay * decay
+    q4 = q2 * q2
+    q8 = q4 * q4
+    one = q8 * q8
+    two = one * one
+    four = two * two
+    return one, two, four
+
+
+def row_powers(one, count=8):
+    rows = [one]
+    for _ in range(count - 1):
+        rows.append(rows[-1] * one)
+    return rows
+
+
+def scan_blocks(source, into, decay, keeps, per, reverse):
+    blocks, width = source.shape
+    one, two, four = block_powers(decay)
+    row = lax.broadcasted_iota(jnp.int32, (8, width), 0)
+    if reverse:
+        row = 7 - row
+    factors = []
+    for distance, power in ((1, one), (2, two), (4, four)):
+        line = jnp.broadcast_to(power, (8, width))
+        factors.append((8 - distance if reverse else distance, jnp.where(row >= distance, line, 0.0)))
+    entering = jnp.ones((8, width), F32)
+    for bit, power in ((1, one), (2, two), (4, four)):
+        line = jnp.broadcast_to(power, (8, width))
+        entering = jnp.where(lax.rem(lax.div(row, bit), 2) == 1, entering * line, entering)
+    eight = jnp.broadcast_to(four * four, (8, width))
+    carry = jnp.zeros((8, width), F32)
+    tiles = blocks // 8
+    for k in range(tiles):
+        tile = tiles - 1 - k if reverse else k
+        edge = (tile + 1) * 8 if reverse else tile * 8
+        if k and edge % per == 0:
+            carry = carry * keeps[edge // per]
+        x = source[tile * 8 : tile * 8 + 8, :]
+        for shift, factor in factors:
+            x = x + factor * pltpu.roll(x, shift, 0)
+        moved = pltpu.roll(x, 7 if reverse else 1, 0)
+        into[tile * 8 : tile * 8 + 8, :] = jnp.where(row >= 1, moved, 0.0) + entering * carry
+        end = x[0:1, :] if reverse else x[7:8, :]
+        carry = jnp.broadcast_to(end, (8, width)) + eight * carry
+
+
+def mix_forward(u_ref, y_ref, power, shifted, weight, keeps, ub_out, state_out, blk_in, blk_out, decay_w, lag_w, t_scr, h_scr):
+    lanes, frames, _ = u_ref.shape
+    blocks = frames // STRETCH
+    count = decay_w.shape[0]
+    several = range(count)
+
+    def lane_tile(lane, _):
+        to_blocks(lambda at: u_ref[lane, pl.ds(at, SLAB, stride=STRETCH), :], blk_in, blocks, True)
+
+        def some_groups(k, _):
+            place = [k * count + n for n in several]
+            groups = [lane * 8 + at for at in place]
+            for n in several:
+                group_weights(power, shifted, groups[n], decay_w.at[n], lag_w.at[n])
+            for n in several:
+                ub_out[groups[n]] = blk_in[place[n]]
+                t_scr[n] = dot_nn(blk_in[place[n]], decay_w[n])
+            for n in several:
+                decay = power[1, pl.ds(groups[n], 1), :]
+                scan_blocks(t_scr.at[n], h_scr.at[n], decay, keeps, TILE // STRETCH, False)
+            for n in several:
+                decay = power[1, pl.ds(groups[n], 1), :]
+                state = h_scr[n]
+                state_out[groups[n]] = state.astype(BF16)
+                out = (state * (weight[pl.ds(groups[n], 1), :] * decay)).astype(BF16)
+                blk_out[place[n]] = dot_nn(blk_in[place[n]], lag_w[n]) + dot_nt(out, decay_w[n])
+            return 0
+
+        lax.fori_loop(0, 8 // count, some_groups, 0)
+
+        def store(at, values):
+            y_ref[lane, pl.ds(at, SLAB, stride=STRETCH), :] = values
+
+        from_blocks(store, blk_out, blocks, False)
+        return 0
+
+    lax.fori_loop(0, lanes, lane_tile, 0)
+
+
+def mix_backward(
+    lane, u_ref, grad, skip, u_tile, u_sem, power, shifted, weight, keeps, ub_ref, state_ref, lags, sums,
+    frames_scr, blk_in, blk_out, decay_w, lag_w, stack_scr, e_scr, r_scr,
+):
+    blocks = frames_scr.shape[2]
+    count = decay_w.shape[0]
+    several = range(count)
+    lanes = u_ref.shape[0]
+    copy = lambda at: pltpu.make_async_copy(u_ref.at[at], u_tile, u_sem)
+    copy(lane).wait()
+    for at in range(STRETCH):
+        for slab in range(blocks // SLAB):
+            rows = slice(slab * SLAB, slab * SLAB + SLAB)
+            first = pl.ds(slab * SLAB * STRETCH + at, SLAB, stride=STRETCH)
+            frames_scr[0, at, rows, :] = u_tile[first, :]
+            frames_scr[1, at, rows, :] = grad[lane, first, :]
+
+    @pl.when(lane + 1 < lanes)
+    def _():
+        copy(lane + 1).start()
+
+    def one_lag(lag, _):
+        def one_frame(at, total):
+            for slab in range(blocks // SLAB):
+                rows = slice(slab * SLAB, slab * SLAB + SLAB)
+                total = total + frames_scr[1, at, rows, :] * frames_scr[0, at - lag, rows, :]
+            return total
+
+        total = lax.fori_loop(lag, STRETCH, one_frame, jnp.zeros((SLAB, 128), F32))
+        lags[lane, pl.ds(lag, 1), :] = jnp.sum(total, axis=0, keepdims=True)
+        return 0
+
+    lax.fori_loop(0, STRETCH, one_lag, 0)
+    for slab in range(blocks // SLAB):
+        rows = slice(slab * SLAB, slab * SLAB + SLAB)
+        for half in range(2):
+            parts = [frames_scr[1, half * 8 + k, rows, :] for k in range(8)]
+            for group, part in enumerate(swap_blocks(parts)):
+                blk_in[group, rows, half * 128 : half * 128 + 128] = part.astype(BF16)
+    position = lax.div(lax.broadcasted_iota(jnp.int32, (1, 256), 1), PIECE).astype(F32)
+
+    def some_groups(k, _):
+        place = [k * count + n for n in several]
+        groups = [lane * 8 + at for at in place]
+        for n in several:
+            group_weights(power, shifted, groups[n], decay_w.at[n], lag_w.at[n])
+        for n in several:
+            gy = blk_in[place[n]]
+            stack_scr[n, 0:blocks, :] = gy
+            stack_scr[n, blocks : 2 * blocks, :] = (gy.astype(F32) * (position + 1.0)).astype(BF16)
+            stack_scr[n, 2 * blocks :, :] = (ub_ref[groups[n]].astype(F32) * position).astype(BF16)
+        for n in several:
+            e_scr[n] = dot_nn(stack_scr[n], decay_w[n])
+        for n in several:
+            decay = power[1, pl.ds(groups[n], 1), :]
+            own = e_scr.at[n, pl.ds(0, blocks)]
+            own[...] = own[...] * decay
+            scan_blocks(own, r_scr.at[n], decay, keeps, TILE // STRETCH, True)
+        for n in several:
+            group = groups[n]
+            inverse = 1.0 / power[1, pl.ds(group, 1), :]
+            last = 16.0 * power[15, pl.ds(group, 1), :]
+            first, second = jnp.zeros((8, SPREAD), F32), jnp.zeros((8, SPREAD), F32)
+            for at in range(blocks // 8):
+                rows = slice(at * 8, at * 8 + 8)
+                state = state_ref[group, rows, :].astype(F32)
+                turn = e_scr[n, 2 * blocks + at * 8 : 2 * blocks + at * 8 + 8, :]
+                first = first + state * e_scr[n, rows, :]
+                second = second + state * e_scr[n, blocks + at * 8 : blocks + at * 8 + 8, :]
+                second = second + r_scr[n, rows, :] * (turn * inverse + last * state)
+            sums[0, pl.ds(group, 1), :] = jnp.sum(first, axis=0, keepdims=True)
+            sums[1, pl.ds(group, 1), :] = jnp.sum(second, axis=0, keepdims=True)
+            out = (r_scr[n] * weight[pl.ds(group, 1), :]).astype(BF16)
+            blk_out[place[n]] = dot_nt(blk_in[place[n]], lag_w[n]) + dot_nt(out, decay_w[n])
+        return 0
+
+    lax.fori_loop(0, 8 // count, some_groups, 0)
+
+    def store(at, values):
+        slab, frame = at // (SLAB * STRETCH), at % STRETCH
+        through = frames_scr[1, frame, slab * SLAB : slab * SLAB + SLAB, :]
+        grad[lane, pl.ds(at, SLAB, stride=STRETCH), :] = values + skip[pl.ds(lane, 1), :] * through
+
+    from_blocks(store, blk_out, blocks, True)
+
+
+def mix_gradients(lags, sums, table_ref):
+    _, decay, root, maps_in, maps_out = state_terms(table_ref)
+    coupling = maps_in * root * maps_out
+    gmap = gather_states(sums[0])
+    gdecay = gather_states(sums[1])
+    power = jnp.ones_like(decay)
+    for lag in range(STRETCH):
+        line = jnp.concatenate([lags[k, lag : lag + 1, :] for k in range(lags.shape[0])], axis=1)
+        if lag:
+            gdecay = gdecay + float(lag) * power * line
+            power = power * decay
+        gmap = gmap + power * line
+    return gmap, gdecay * coupling
 
 
 def pack_small(out, scr, place, bias_ref, gains, shifts, conv_bias, taps, rate, maps):
@@ -962,22 +1249,25 @@
     (
         h_out,
         x1_out,
-        u_out,
         v_out,
         y_out,
         gated_out,
         x2_out,
         p_out,
-        hold_out,
+        u_out,
         w_out,
         stat_out,
         table_ref,
         bias_ref,
-        decay_ref,
-        map_ref,
-    ) = take(15)
+        ub_out,
+        state_out,
+        power,
+        shifted,
+        weight,
+    ) = take(17)
     gathered = take(4) if fused else []
-    x1_scr, low_all, low_scr, sum_scr, state_scr, padded = take(6)
+    x1_scr, low_all, low_scr, sum_scr, y_all, padded = take(6)
+    mix_scr = take(6)
     step = pl.program_id(0)
     channels = x_ref.shape[1]
     frames = w_out.shape[0]
@@ -1033,7 +1323,7 @@
             run((1, 4))
 
         rest = {1: [(2, 2), (3, 0)], 2: [(2, 3)], tiles: [(2, 4), (3, 1)]}
-        rest.update({tiles + 1: [(3, 2)], tiles + 2: [(3, 3)], 2 * tiles: [(3, 4)]})
+        rest.update({tiles + 1: [(3, 2)], tiles + 2: [(3, 3)], 2 * tiles + 1: [(3, 4)]})
         for at, stages in rest.items():
 
             @pl.when(step == at)
@@ -1042,7 +1332,7 @@
                 if at == tiles:
                     for chunk in range(3):
                         keep_copy(chunk).start()
-                if at == 2 * tiles:
+                if at == 2 * tiles + 1:
                     for chunk in range(3):
                         keep_copy(chunk).wait()
                     for wait in sends:
@@ -1054,13 +1344,6 @@
         def _():
             table_ref[...] = table_in[...]
             bias_ref[...] = bias_in[...]
-
-    @pl.when(step == 0)
-    def _():
-        _, decay, root, maps_in, maps_out = state_terms(table_ref)
-        decay_ref[...] = decay
-        map_ref[...] = maps_in * root * maps_out
-        state_scr[...] = jnp.zeros_like(state_scr)
 
     @pl.when(step < tiles)
     def _():
@@ -1072,14 +1355,14 @@
         by_rows(first)
 
         def hidden(c, _):
-            cols = columns(c)
-            h = dot_nn(low_scr[...], cols_of(first_v, 1, c)) + bias_ref[pl.ds(c, 1), :]
+            cols = columns(c, WIDTH)
+            h = dot_nn(low_scr[...], square_of(first_v, 1 + c)) + bias_of(bias_ref, 0, c)
             h_out[:, cols] = h.astype(BF16)
             active = (h * sigmoid(h)).astype(BF16)
             sum_scr[...] += dot_nn(active, rows_of(second_v, 0, c))
             return 0
 
-        lax.fori_loop(0, h_out.shape[1] // CHUNK, hidden, 0)
+        lax.fori_loop(0, h_out.shape[1] // WIDTH, hidden, 0)
 
         def second(rows):
             x1 = x_ref[rows, :].astype(F32) + 0.5 * (sum_scr[rows, :] + shift(6))
@@ -1090,48 +1373,29 @@
 
         by_rows(second)
 
-    @pl.when((step >= tiles) & (step < 2 * tiles))
+    @pl.when(step == tiles)
     def _():
-        at = step - tiles
+        prepare_states(first_v[:, 0, :, :CHUNK], power, shifted, weight)
+
+        def project(tile, _):
+            rows = pl.ds(pl.multiple_of(tile * TILE, TILE), TILE)
+            u = dot_nn(low_all[rows, :], square_of(third_v, 0))
+            for lane in range(lanes):
+                u_out[lane, rows, :] = u[:, lane * 128 : lane * 128 + 128]
+            return 0
+
+        lax.fori_loop(0, tiles, project, 0)
+        mix_forward(u_out, y_all, power, shifted, weight, flags, ub_out, state_out, *mix_scr)
+
+    @pl.when((step > tiles) & (step <= 2 * tiles))
+    def _():
+        at = step - tiles - 1
         whole_tile = pl.ds(pl.multiple_of(at * TILE, TILE), TILE)
-
-        def project(c, _):
-            cols = columns(c)
-            low = low_all[whole_tile, :]
-            u_out[:, cols] = dot_nn(low, cols_of(third_v, 0, c))
-            v_out[:, cols] = dot_nn(low, cols_of(third_v, 1, c)).astype(BF16)
-            return 0
-
-        lax.fori_loop(0, channels // CHUNK, project, 0)
-        low_half = half_masks(128)
-        state_scr[...] = state_scr[...] * pick(flags, at)
-
-        def scan_span(span, _):
-            hold_out[span] = state_scr[...]
-
-            def scan(block, _):
-                start = pl.multiple_of(span * SPAN + block * 8, 8)
-                for lane in range(lanes):
-                    cols = slice(lane * 128, lane * 128 + 128)
-                    state = state_scr[:, cols]
-                    decay = decay_ref[:, cols]
-                    maps = map_ref[:, cols]
-                    drive = u_out[pl.ds(start, 8), cols]
-                    parts = []
-                    for j in range(8):
-                        state = decay * state + jnp.broadcast_to(drive[j : j + 1, :], (STATES, 128))
-                        parts.append(fold_states(maps * state))
-                    state_scr[:, cols] = state
-                    sum_scr[pl.ds(start, 8), cols] = merge_rows(parts, low_half)
-                return 0
-
-            lax.fori_loop(0, SPAN // 8, scan, 0)
-            return 0
-
-        lax.fori_loop(0, TILE // SPAN, scan_span, 0)
+        v_out[...] = dot_nn(low_all[whole_tile, :], square_of(third_v, 1)).astype(BF16)
 
         def gate(rows):
-            y = sum_scr[rows, :] + shift(11) * u_out[rows, :]
+            join = lambda ref: jnp.concatenate([ref[lane, here(rows, at), :] for lane in range(lanes)], axis=1)
+            y = join(y_all) + shift(11) * join(u_out)
             v = v_out[rows, :].astype(F32)
             y_out[rows, :] = y.astype(BF16)
             gated_out[rows, :] = (y * (v * sigmoid(v))).astype(BF16)
@@ -1163,7 +1427,7 @@
 
         lax.fori_loop(0, channels // CHUNK, widen, 0)
 
-    @pl.when(step == 2 * tiles)
+    @pl.when(step == 2 * tiles + 1)
     def _():
         fill_halo(padded, flags, tiles)
 
@@ -1225,42 +1489,44 @@
     frames, channels = x.shape
     tiles = frames // TILE
     early = lambda width: pl.BlockSpec((TILE, width), lambda i: (jnp.minimum(i, tiles - 1), 0))
-    place = lambda i: jnp.clip(i - tiles, 0, tiles - 1)
+    place = lambda i: jnp.clip(i - tiles - 1, 0, tiles - 1)
     late = lambda width: pl.BlockSpec((TILE, width), lambda i: (place(i), 0))
     shape = lambda width, kind: jax.ShapeDtypeStruct((frames, width), kind)
-    spans = TILE // SPAN
-    state = jax.ShapeDtypeStruct((STATES, channels), F32)
+    groups, blocks = channels // PIECE, frames // STRETCH
     out_shape = [
         shape(hidden, BF16),
-        shape(channels, F32),
         shape(channels, F32),
         shape(channels, BF16),
         shape(channels, BF16),
         shape(channels, BF16),
         shape(channels, F32),
         shape(2 * channels, BF16),
-        jax.ShapeDtypeStruct((frames // SPAN, STATES, channels), F32),
+        jax.ShapeDtypeStruct((channels // 128, frames, 128), F32),
         shape(channels, F32),
         jax.ShapeDtypeStruct((8, channels), F32),
         jax.ShapeDtypeStruct((TABLE, channels), F32),
         jax.ShapeDtypeStruct((16, CHUNK), F32),
-        state,
-        state,
+        jax.ShapeDtypeStruct((groups, blocks, STRETCH * PIECE), BF16),
+        jax.ShapeDtypeStruct((groups, blocks, SPREAD), BF16),
+        jax.ShapeDtypeStruct((STRETCH, groups, SPREAD), F32),
+        jax.ShapeDtypeStruct((STRETCH, groups, STRETCH * PIECE), F32),
+        jax.ShapeDtypeStruct((groups, SPREAD), F32),
     ]
-    out_specs = [early(hidden), early(channels)]
-    out_specs += [late(channels)] * 5
-    out_specs += [
-        late(2 * channels),
-        pl.BlockSpec((spans, STATES, channels), lambda i: (place(i), 0, 0)),
-    ]
-    out_specs += [whole(s.shape) for s in out_shape[9:]]
+    out_specs = [early(hidden), early(channels)] + [late(channels)] * 4 + [late(2 * channels)]
+    out_specs += [whole(s.shape) for s in out_shape[7:]]
     scratch = [
         pltpu.VMEM((frames, channels), F32),
         pltpu.VMEM((frames, channels), BF16),
         pltpu.VMEM((TILE, channels), BF16),
         pltpu.VMEM((TILE, channels), F32),
-        pltpu.VMEM((STATES, channels), F32),
+        pltpu.VMEM((channels // 128, frames, 128), F32),
         pltpu.VMEM((channels // 128, tiles * (TILE + 2 * REACH), 128), F32),
+        pltpu.VMEM((8, blocks, STRETCH * PIECE), BF16),
+        pltpu.VMEM((8, blocks, STRETCH * PIECE), F32),
+        pltpu.VMEM((TOGETHER, STRETCH * PIECE, SPREAD), BF16),
+        pltpu.VMEM((TOGETHER, STRETCH * PIECE, STRETCH * PIECE), BF16),
+        pltpu.VMEM((TOGETHER, blocks, SPREAD), F32),
+        pltpu.VMEM((TOGETHER, blocks, SPREAD), F32),
     ]
     operands = (weights if not fused else small + weights) + (small if not fused else [])
     if fused:
@@ -1276,7 +1542,7 @@
         scratch += swap_scratch(*mesh_size, channels)
     return pl.pallas_call(
         partial(front_kernel, mesh_size),
-        grid=(2 * tiles + 1,),
+        grid=(2 * tiles + 2,),
         in_specs=[SMEM_SPEC, SMEM_SPEC, early(channels)] + [whole(a.shape) for a in operands],
         out_specs=out_specs,
         out_shape=out_shape,
@@ -1358,14 +1624,14 @@
     by_rows(second)
 
     def forward(c, _):
-        cols = columns(c)
-        h = dot_nn(low_scr[...], cols_of(blocks_ref, 1, c)) + bias_ref[pl.ds(8 + c, 1), :]
+        cols = columns(c, WIDTH)
+        h = dot_nn(low_scr[...], square_of(blocks_ref, 1 + c)) + bias_of(bias_ref, 1, c)
         h_scr[:, cols] = h
         active = (h * sigmoid(h)).astype(BF16)
         sum_scr[...] += dot_nn(active, rows_of(blocks_ref, 5, c))
         return 0
 
-    lax.fori_loop(0, hidden // CHUNK, forward, 0)
+    lax.fori_loop(0, hidden // WIDTH, forward, 0)
     turn_scr[...] = low_scr[...].T
 
     def last(rows):
@@ -1385,7 +1651,7 @@
     by_rows(last)
 
     def backward(c, _):
-        cols = columns(c)
+        cols = columns(c, WIDTH)
         h = h_scr[:, cols]
         sig = sigmoid(h)
         active = h * sig
@@ -1394,10 +1660,10 @@
         bias_acc[:, cols] += fold8(grad_h.astype(F32))
         down_acc[cols, :] += dot_tn(active.astype(BF16), grad_scr[...])
         up_acc[:, cols] += dot_nn(turn_scr[...], grad_h)
-        sum_scr[...] += dot_nt(grad_h, cols_of(blocks_ref, 1, c))
+        sum_scr[...] += dot_nt(grad_h, square_of(blocks_ref, 1 + c))
         return 0
 
-    lax.fori_loop(0, hidden // CHUNK, backward, 0)
+    lax.fori_loop(0, hidden // WIDTH, backward, 0)
 
     def fourth(rows):
         e, inv = norm_parts(x3_scr[rows, :])
@@ -1492,122 +1758,87 @@
     fused = mesh_size is not None
     refs = list(refs)
     take = lambda count: [refs.pop(0) for _ in range(count)]
-    (
-        offsets_ref,
-        counts_ref,
-        w_ref,
-        gnb_ref,
-        p_all,
-        x2_ref,
-        gx3_ref,
-        gated_ref,
-        y_ref,
-        v_ref,
-        u_ref,
-        x1_ref,
-        hold_ref,
-        blocks_ref,
-        vec_ref,
-        stat_ref,
-        decay_ref,
-        map_ref,
-    ) = take(18)
+    offsets_ref, counts_ref, w_ref, gnb_ref, p_ref = take(5)
+    x2_ref, gx3_ref, gated_ref, y_ref, v_ref, x1_ref = take(6)
+    u_ref, ub_ref, state_ref, power, shifted, weight, blocks_ref, vec_ref, stat_ref = take(9)
     sources = take(1) if fused else []
-    (
-        gx1_ref,
-        gblocks_out,
-        gvec_out,
-        gtaps_ref,
-        gmap_out,
-        gdecay_out,
-    ) = take(6)
-    reduced = take(1) if fused else []
-    (
-        convin_acc,
-        mixout_acc,
-        mixin_acc,
-        vec_acc,
-        map_acc,
-        decay_acc,
-        adj_scr,
-        track,
-        low_scr,
-        wide_scr,
-        sum_scr,
-        gy_scr,
-        padded,
-        gpad,
-    ) = take(14)
+    gx1_ref, gin_out, gvec_out, gtaps_ref, gmap_out, gdecay_out = take(6)
+    reduced = take(2) if fused else []
+    mid_ref = None if fused else refs.pop(0)
+    wide_acc, mixout_acc, vec_acc, low_scr, wide_scr, sum_scr = take(6)
+    padded, gpad, gv_all, lags, sums, skip, u_tile, u_sem = take(8)
+    mix_scr = take(8)
     step = pl.program_id(0)
-    tiles = pl.num_programs(0) - 1
-    at = tiles - jnp.maximum(step, 1)
     channels = x2_ref.shape[1]
+    frames = u_ref.shape[1]
+    tiles = frames // TILE
     lanes = channels // 128
     pitch = TILE + 2 * REACH
+    conv_at, mix_at = tiles, 2 * tiles + 1
+    last_step = 3 * tiles + 1
     gain = lambda k: vec_ref[k : k + 1, :]
     shift = lambda k: vec_ref[6 + k : 7 + k, :]
     left, right = slice(0, channels), slice(channels, 2 * channels)
     flags = carries(offsets_ref, counts_ref, tiles)
+    schedule = {}
     if fused:
         n_dp, n_fs = mesh_size
         place = Place(lax.axis_index("dp"), lax.axis_index("fsdp"), n_dp, n_fs)
-        scratch = take(2 + place.count)
+        mid_src = refs.pop(0)
+        mid_ref = flat_groups(mid_src)
+        scratch = take(2 * (2 + place.count))
 
         def emit(chunk, total):
             reduced[chunk][...] = total
 
-        plans, sends = block_scatter(place, sources, emit, scratch, *take(3))
-        order = waves(plans)
-        points = [(0, 0), (0, 2), (1, 0), (1, 3), (2, 0)]
-
-    def progress(point):
-        if not fused:
-            return
-        for wave, place in zip(order, points):
-            if place[1] == point:
-
-                @pl.when(step == place[0])
-                def _(wave=wave):
-                    for stage in wave:
-                        stage()
+        plans, sends = block_scatter(place, sources + [mid_src], emit, scratch, *take(3))
+        first = [(0, 0), (conv_at, 1), (conv_at + 2, 0), (conv_at + 3, 0), (mix_at, 1)]
+        second = [(mix_at, 0), (mix_at, 1), (mix_at + 1, 0), (mix_at + 2, 0), (last_step, 1)]
+        for chunk, points in enumerate((first, second)):
+            for stage, point in enumerate(points):
+                schedule.setdefault(point, []).append((stage, chunk))
+
+    def progress(at, part):
+        for stage, chunk in sorted(schedule.get((at, part), [])):
+            plans[chunk][stage]()
 
     @pl.when(step == 0)
     def _():
-        for ref in (convin_acc, mixout_acc, mixin_acc, vec_acc, map_acc, decay_acc, adj_scr):
+        for ref in (wide_acc, mixout_acc, vec_acc):
             ref[...] = jnp.zeros_like(ref)
         if fused:
             greet(place.dp, place.fs, n_dp, n_fs)
 
-    progress(0)
-
-    @pl.when(step == 0)
+    for at in sorted({key[0] for key in schedule if key[1] == 0 and key[0] != mix_at}):
+
+        @pl.when(step == at)
+        def _(at=at):
+            progress(at, 0)
+
+    @pl.when(step < tiles)
     def _():
         center, scale = stat_ref[0:1, :], stat_ref[1:2, :]
         plain, cross = stat_ref[2:3, :], stat_ref[3:4, :]
-        per = TILE // 64
 
         def fill(index, _):
-            tile, inner = index // per, index % per
             rows = pl.ds(pl.multiple_of(index * 64, 64), 64)
-            place = pl.ds(pl.multiple_of(tile * pitch + REACH + inner * 64, 8), 64)
+            spot = pl.ds(pl.multiple_of(step * pitch + REACH + index * 64, 8), 64)
             e = (w_ref[rows, :] - center) * scale
             d = gnb_ref[rows, :] * gain(5)
             gw = scale * (d - plain - e * cross)
-            g = p_all[rows, left].astype(F32) * sigmoid(p_all[rows, right].astype(F32))
+            g = p_ref[rows, left].astype(F32) * sigmoid(p_ref[rows, right].astype(F32))
             for lane in range(lanes):
                 cols = slice(lane * 128, lane * 128 + 128)
-                padded[lane, place, :] = gw[:, cols]
-                gpad[lane, place, :] = g[:, cols]
+                padded[lane, spot, :] = gw[:, cols]
+                gpad[lane, spot, :] = g[:, cols]
             return 0
 
-        lax.fori_loop(0, tiles * per, fill, 0)
+        lax.fori_loop(0, TILE // 64, fill, 0)
+
+    @pl.when(step == conv_at)
+    def _():
         fill_halo(padded, flags, tiles)
         fill_halo(gpad, flags, tiles)
-
-    progress(1)
-
-    @pl.when(step == 0)
-    def _():
         block = 64
         per = TILE // block
         gtaps_ref[...] = jnp.zeros_like(gtaps_ref)
@@ -1621,27 +1852,28 @@
                     for k, s in enumerate(sums)
                 )
 
-            sums = lax.fori_loop(0, tiles * per, corr, (jnp.zeros((8, 128), F32),) * TAPS)
+            found = lax.fori_loop(0, tiles * per, corr, (jnp.zeros((8, 128), F32),) * TAPS)
             for k in range(TAPS):
                 gtaps_ref[k : k + 1, lane * 128 : lane * 128 + 128] = jnp.sum(
-                    sums[k], axis=0, keepdims=True
+                    found[k], axis=0, keepdims=True
                 )
+        progress(conv_at, 1)
 
         def store(lane, row, base, total):
             gpad[lane, pl.ds(pl.multiple_of(base + REACH, 8), 64), :] = total
 
         taps_over(padded, vec_ref, store, tiles, True)
 
-    progress(2)
-
-    def back_tile():
+    @pl.when((step > conv_at) & (step < mix_at))
+    def _():
+        at = step - conv_at - 1
+
         def first(rows):
-            place = pl.ds(pl.multiple_of(at * pitch + REACH + rows.start, 8), ROWS)
-            here = pl.ds(pl.multiple_of(at * TILE + rows.start, ROWS), ROWS)
-            grad = jnp.concatenate([gpad[lane, place, :] for lane in range(lanes)], axis=1)
-            sig = sigmoid(p_all[here, right].astype(F32))
+            spot = pl.ds(pl.multiple_of(at * pitch + REACH + rows.start, 8), ROWS)
+            grad = jnp.concatenate([gpad[lane, spot, :] for lane in range(lanes)], axis=1)
+            sig = sigmoid(p_ref[rows, right].astype(F32))
             gl = (grad * sig).astype(BF16)
-            gr = (grad * p_all[here, left].astype(F32) * (sig * (1.0 - sig))).astype(BF16)
+            gr = (grad * p_ref[rows, left].astype(F32) * (sig * (1.0 - sig))).astype(BF16)
             wide_scr[rows, left] = gl
             wide_scr[rows, right] = gr
             vec_acc[0] += fold8(gl.astype(F32))
@@ -1651,99 +1883,83 @@
 
         by_rows(first)
         turned = low_scr[...].T
-        convin_acc[...] += dot_nn(turned, wide_scr[...])
+        wide_acc[...] += dot_nn(turned, wide_scr[...])
         sum_scr[...] = dot_nt(wide_scr[:, left], square_of(blocks_ref, 3)) + dot_nt(
             wide_scr[:, right], square_of(blocks_ref, 4)
         )
 
         def second(rows):
+            here = pl.ds(pl.multiple_of(at * TILE + rows.start, ROWS), ROWS)
             e, inv = norm_parts(x2_ref[rows, :])
             grad = sum_scr[rows, :]
             vec_acc[2] += fold8(grad * e)
             vec_acc[3] += fold8(grad)
             gx2 = gx3_ref[rows, :] + norm_back(grad, e, inv, gain(2))
-            gx1_ref[rows, :] = gx2
+            spot = pl.ds(pl.multiple_of(at * pitch + REACH + rows.start, 8), ROWS)
+            for lane in range(lanes):
+                gpad[lane, spot, :] = gx2[:, lane * 128 : lane * 128 + 128]
             low = gx2.astype(BF16)
             low_scr[rows, :] = low
             vec_acc[4] += fold8(low.astype(F32))
 
         by_rows(second)
-        progress(3)
         mixout_acc[...] += dot_tn(gated_ref[...], low_scr[...])
         sum_scr[...] = dot_nt(low_scr[...], square_of(blocks_ref, 2))
 
         def third(rows):
+            here = pl.ds(pl.multiple_of(at * TILE + rows.start, ROWS), ROWS)
             grad = sum_scr[rows, :]
             v = v_ref[rows, :].astype(F32)
             sig = sigmoid(v)
             swish = v * sig
             gy = grad * swish
-            gy_scr[rows, :] = gy
-            wide_scr[rows, right] = (
+            for lane in range(lanes):
+                padded[lane, here, :] = gy[:, lane * 128 : lane * 128 + 128]
+            gv_all[here, :] = (
                 grad * y_ref[rows, :].astype(F32) * (sig * (1.0 + v - swish))
             ).astype(BF16)
-            vec_acc[5] += fold8(gy * u_ref[rows, :])
+
 
         by_rows(third)
-        progress(4)
-        low_half = half_masks(128)
-        later = jnp.minimum(at + 1, tiles - 1)
-        adj_scr[...] = adj_scr[...] * pick(flags, later)
-
-        def span_back(index, _):
-            span = TILE // SPAN - 1 - index
-            base = pl.multiple_of(span * SPAN, SPAN)
-            for lane in range(lanes):
-                cols = slice(lane * 128, lane * 128 + 128)
-                decay = decay_ref[:, cols]
-
-                def forward(block, state):
-                    drive = u_ref[pl.ds(pl.multiple_of(base + block * 8, 8), 8), cols]
-                    for j in range(8):
-                        track[block * 8 + j, :, cols] = state
-                        state = decay * state + jnp.broadcast_to(drive[j : j + 1, :], (STATES, 128))
-                    return state
-
-                lax.fori_loop(0, SPAN // 8, forward, hold_ref[span, :, cols])
-
-            def backward(index, _):
-                block = SPAN // 8 - 1 - index
-                start = pl.multiple_of(base + block * 8, 8)
-                for lane in range(lanes):
-                    cols = slice(lane * 128, lane * 128 + 128)
-                    decay = decay_ref[:, cols]
-                    maps = map_ref[:, cols]
-                    adj = adj_scr[:, cols]
-                    drive = u_ref[pl.ds(start, 8), cols]
-                    grad = gy_scr[pl.ds(start, 8), cols]
-                    gmap = map_acc[:, cols]
-                    gdecay = decay_acc[:, cols]
-                    parts = [None] * 8
-                    for j in range(7, -1, -1):
-                        adj = decay * adj + jnp.broadcast_to(grad[j : j + 1, :], (STATES, 128))
-                        parts[j] = fold_states(maps * adj)
-                        gmap = gmap + adj * jnp.broadcast_to(drive[j : j + 1, :], (STATES, 128))
-                        gdecay = gdecay + adj * track[block * 8 + j, :, cols]
-                    adj_scr[:, cols] = adj
-                    map_acc[:, cols] = gmap
-                    decay_acc[:, cols] = gdecay
-                    sum_scr[pl.ds(start, 8), cols] = merge_rows(parts, low_half)
-                return 0
-
-            lax.fori_loop(0, SPAN // 8, backward, 0)
+
+    @pl.when(step == mix_at)
+    def _():
+        pltpu.make_async_copy(u_ref.at[0], u_tile, u_sem).start()
+        store_wide(mid_ref, 0, mixout_acc)
+        store_wide(mid_ref, 1, wide_acc)
+        wide_acc[...] = jnp.zeros_like(wide_acc)
+        for lane in range(lanes):
+            skip[lane : lane + 1, :] = vec_ref[17:18, lane * 128 : lane * 128 + 128]
+        progress(mix_at, 0)
+
+        def one(lane, _):
+            mix_backward(
+                lane, u_ref, padded, skip, u_tile, u_sem, power, shifted, weight, flags, ub_ref, state_ref, lags, sums, *mix_scr
+            )
             return 0
 
-        lax.fori_loop(0, TILE // SPAN, span_back, 0)
+        lax.fori_loop(0, lanes // 2, one, 0)
+        progress(mix_at, 1)
+        lax.fori_loop(lanes // 2, lanes, one, 0)
+        gmap, gdecay = mix_gradients(lags, sums, vec_ref)
+        gmap_out[...] = gmap
+        gdecay_out[...] = gdecay
+
+    @pl.when(step > mix_at)
+    def _():
+        at = step - mix_at - 1
 
         def fourth(rows):
-            gu = sum_scr[rows, :] + shift(11) * gy_scr[rows, :]
+            here = pl.ds(pl.multiple_of(at * TILE + rows.start, ROWS), ROWS)
+            gu = jnp.concatenate([padded[lane, here, :] for lane in range(lanes)], axis=1)
             wide_scr[rows, left] = gu.astype(BF16)
+            wide_scr[rows, right] = gv_all[here, :]
             e, _ = norm_parts(x1_ref[rows, :])
             low_scr[rows, :] = (e * gain(1) + shift(1)).astype(BF16)
 
         by_rows(fourth)
         turned = low_scr[...].T
-        mixin_acc[...] += dot_nn(turned, wide_scr[...])
+        wide_acc[...] += dot_nn(turned, wide_scr[...])
         sum_scr[...] = dot_nt(wide_scr[:, left], square_of(blocks_ref, 0)) + dot_nt(
             wide_scr[:, right], square_of(blocks_ref, 1)
         )
@@ -1753,43 +1969,40 @@
             grad = sum_scr[rows, :]
             vec_acc[6] += fold8(grad * e)
             vec_acc[7] += fold8(grad)
-            gx1_ref[rows, :] = gx1_ref[rows, :] + norm_back(grad, e, inv, gain(1))
+            spot = pl.ds(pl.multiple_of(at * pitch + REACH + rows.start, 8), ROWS)
+            gx2 = jnp.concatenate([gpad[lane, spot, :] for lane in range(lanes)], axis=1)
+            gx1_ref[rows, :] = gx2 + norm_back(grad, e, inv, gain(1))
 
         by_rows(fifth)
 
-        @pl.when(step == tiles)
-        def _():
-            store_wide(gblocks_out, 0, mixin_acc)
-            store_wide(gblocks_out, 2, mixout_acc)
-            store_wide(gblocks_out, 3, convin_acc)
-            for k in range(8):
-                gvec_out[k : k + 1, :] = jnp.sum(vec_acc[k], axis=0, keepdims=True)
-            gmap_out[...] = map_acc[...]
-            gdecay_out[...] = decay_acc[...] * map_ref[...]
-
-    @pl.when(step > 0)
+    @pl.when(step == last_step)
     def _():
-        back_tile()
-
-    if fused:
-
-        @pl.when(step == tiles)
-        def _():
+        store_wide(gin_out, 0, wide_acc)
+        for k in range(8):
+            gvec_out[k : k + 1, :] = jnp.sum(vec_acc[k], axis=0, keepdims=True)
+        gvec_out[5:6, :] = jnp.concatenate([lags[k, 0:1, :] for k in range(lanes)], axis=1)
+        if fused:
+            progress(last_step, 1)
             for wait in sends:
                 wait()
 
 
-def back(mesh_size, offsets, counts, wholes, tiled, hold, blocks, vec, stat, decay, maps, grads=(), collective_id=None):
+def back(mesh_size, offsets, counts, tiled, wholes, grads=(), collective_id=None):
     fused = mesh_size is not None
-    frames, channels = wholes[0].shape
+    frames, channels = tiled[0].shape
     tiles = frames // TILE
-    place = lambda i: tiles - jnp.maximum(i, 1)
-    row = lambda width: pl.BlockSpec((TILE, width), lambda i: (place(i), 0))
-    spans = TILE // SPAN
+    groups, blocks = channels // PIECE, frames // STRETCH
+    late = lambda i, first: jnp.clip(i - first, 0, tiles - 1)
+    filling = lambda i: (late(i, 0), 0)
+    twice = lambda i: (jnp.where(i < tiles, i, late(i, tiles + 1)), 0)
+    mixing = lambda i: (late(i, tiles + 1), 0)
+    ending = lambda i: (late(i, 2 * tiles + 2), 0)
+    maps = [filling, filling, twice] + [mixing] * 5 + [ending]
     state = jax.ShapeDtypeStruct((STATES, channels), F32)
+    bf16 = lambda *shape: jax.ShapeDtypeStruct(shape, BF16)
     shapes = [
         jax.ShapeDtypeStruct((frames, channels), F32),
-        jax.ShapeDtypeStruct(blocks.shape, BF16),
+        bf16(groups, 2, PIECE, WIDTH),
         jax.ShapeDtypeStruct((8, channels), F32),
         jax.ShapeDtypeStruct((16, channels), F32),
         state,
@@ -1799,39 +2012,49 @@
     scratch = [
         pltpu.VMEM((channels, 2 * channels), F32),
         pltpu.VMEM((channels, channels), F32),
-        pltpu.VMEM((channels, 2 * channels), F32),
         pltpu.VMEM((8, 8, channels), F32),
-        pltpu.VMEM((STATES, channels), F32),
-        pltpu.VMEM((STATES, channels), F32),
-        pltpu.VMEM((STATES, channels), F32),
-        pltpu.VMEM((SPAN, STATES, channels), F32),
         pltpu.VMEM((TILE, channels), BF16),
         pltpu.VMEM((TILE, 2 * channels), BF16),
         pltpu.VMEM((TILE, channels), F32),
-        pltpu.VMEM((TILE, channels), F32),
         pad,
         pad,
+        pltpu.VMEM((frames, channels), BF16),
+        pltpu.VMEM((channels // 128, STRETCH, 128), F32),
+        pltpu.VMEM((2, groups, SPREAD), F32),
+        pltpu.VMEM((8, 128), F32),
+        pltpu.VMEM((frames, 128), F32),
+        pltpu.SemaphoreType.DMA(()),
+        pltpu.VMEM((2, STRETCH, blocks, 128), F32),
+        pltpu.VMEM((8, blocks, STRETCH * PIECE), BF16),
+        pltpu.VMEM((8, blocks, STRETCH * PIECE), F32),
+        pltpu.VMEM((2, STRETCH * PIECE, SPREAD), BF16),
+        pltpu.VMEM((2, STRETCH * PIECE, STRETCH * PIECE), BF16),
+        pltpu.VMEM((2, 3 * blocks, STRETCH * PIECE), BF16),
+        pltpu.VMEM((2, 3 * blocks, SPREAD), F32),
+        pltpu.VMEM((2, blocks, SPREAD), F32),
     ]
     if fused:
-        counts_of = [g.shape[-3] for g in grads]
+        counts_of = [grads[0].shape[-3], 3]
         shapes += [jax.ShapeDtypeStruct((k, PIECE, WIDTH), F32) for k in counts_of]
+        scratch += [pltpu.VMEM(block_layout(*mesh_size) + (3, PIECE, WIDTH), BF16)]
         scratch += block_scratch(*mesh_size, counts_of, (PIECE, WIDTH))
-        scratch += block_sems(*mesh_size, len(grads))
+        scratch += block_sems(*mesh_size, 2)
+    else:
+        shapes.append(bf16(groups, 3, PIECE, WIDTH))
     return pl.pallas_call(
         partial(back_kernel, mesh_size),
-        grid=(tiles + 1,),
+        grid=(3 * tiles + 2,),
         in_specs=[SMEM_SPEC, SMEM_SPEC]
-        + [whole(a.shape) for a in wholes]
-        + [row(channels)] * len(tiled)
-        + [pl.BlockSpec((spans, STATES, channels), lambda i: (place(i), 0, 0))]
-        + [whole(a.shape) for a in (blocks, vec, stat, decay, maps)]
+        + [pl.BlockSpec((TILE, a.shape[1]), index) for a, index in zip(tiled, maps)]
+        + [HBM_SPEC]
+        + [whole(a.shape) for a in wholes[1:]]
         + [HBM_SPEC] * len(grads),
-        out_specs=[row(channels)] + [whole(s.shape) for s in shapes[1:]],
+        out_specs=[pl.BlockSpec((TILE, channels), ending)] + [whole(s.shape) for s in shapes[1:]],
         out_shape=shapes,
         scratch_shapes=scratch,
         compiler_params=params(collective_id),
         name="back",
-    )(offsets, counts, *wholes, *tiled, hold, blocks, vec, stat, decay, maps, *grads)
+    )(offsets, counts, *tiled, *wholes, *grads)
 
 
 def small_gradients(out, gvec1, gvec2, gvec3, gtaps, gmap, gdecay, table_ref):
@@ -1856,9 +2079,8 @@
 
 
 def store_cols(out, at, value):
-    per = WIDTH // CHUNK
     groups = value.shape[0] // PIECE
-    out[:, lax.div(at, per), :, columns(lax.rem(at, per))] = value.reshape((groups, PIECE, CHUNK))
+    out[:, at] = value.reshape((groups, PIECE, WIDTH))
 
 
 def tail_kernel(mesh_size, *refs):
@@ -1877,7 +2099,7 @@
     turn_scr, grad_scr, gh_scr, vec_acc, bias_scr = take(5)
     step = pl.program_id(0)
     frames, channels = x_ref.shape
-    chunks = hidden // CHUNK
+    chunks = hidden // WIDTH
     tiles = frames // TILE
     first_b, first_c = 1 + chunks, 1 + 2 * chunks
     schedule = {}
@@ -1899,9 +2121,9 @@
             place, sources + [down_src, left_src, right_src, small_src], emit, scratch, *sems
         )
         begins = [
-            (0, 3, 5, 7, 9),
-            (first_b, first_b + 2, first_b + 4, first_b + 6, first_c),
-            (first_b + 4, first_b + 6, first_c, first_c + 1, first_c + 2),
+            (0, 1, 2, 4, 6),
+            (first_b, first_b + 1, first_b + 2, first_b + 3, first_c),
+            (first_b + 2, first_b + 3, first_c, first_c + 1, first_c + 2),
             (first_c, first_c + 1, first_c + 2, first_c + tiles, first_c + tiles),
             (first_c, first_c + 1, first_c + 2, first_c + tiles, first_c + tiles),
         ]
@@ -1944,17 +2166,19 @@
         h = h_ref[...].astype(F32)
         active = (h * sigmoid(h)).astype(BF16)
         value = dot_tn(active, grad_scr[...]).astype(BF16)
-        groups = CHUNK // (4 * PIECE)
+        groups = WIDTH // (4 * PIECE)
         down_out[pl.ds((step - 1) * groups, groups)] = value.reshape((groups, 4, PIECE, WIDTH))
 
     def second_half(c, store):
-        cols = columns(c)
+        cols = columns(c, WIDTH)
         h = h_ref[...].astype(F32)
         sig = sigmoid(h)
         gate = dot_nt(grad_scr[...], rows_of(down_ref, 0, c))
         grad_h = (gate * (sig * (1.0 + h * (1.0 - sig)))).astype(BF16)
         gh_scr[:, cols] = grad_h
-        bias_scr[pl.ds(c, 1), :] = jnp.sum(fold8(grad_h.astype(F32)), axis=0, keepdims=True)
+        sums = jnp.sum(fold8(grad_h.astype(F32)), axis=0, keepdims=True)
+        bias_scr[pl.ds(2 * c, 1), :] = sums[:, :CHUNK]
+        bias_scr[pl.ds(2 * c + 1, 1), :] = sums[:, CHUNK:]
         store(dot_nn(turn_scr[...], grad_h).astype(BF16))
 
     if fused:
@@ -1987,8 +2211,8 @@
             devices = n_dp * n_fs
             small_out = flat_groups(small_src)
             small_out[:, 0, :, :CHUNK] = narrow.reshape((devices, PIECE, CHUNK))
-            for c in range(chunks):
-                bias_scr[chunks + c : chunks + c + 1, :] = gbias1[0:1, c * CHUNK : c * CHUNK + CHUNK]
+            for c in range(8):
+                bias_scr[8 + c : 9 + c, :] = gbias1[0:1, c * CHUNK : c * CHUNK + CHUNK]
             bias = bias_scr[...].astype(BF16)
             small_out[:, 0, :, CHUNK:] = jnp.broadcast_to(bias[None], (devices, PIECE, CHUNK))
             progress(first_c)
@@ -2039,7 +2263,7 @@
     fused = mesh_size is not None
     frames, channels = x.shape
     hidden = h.shape[1]
-    tiles, chunks = frames // TILE, hidden // CHUNK
+    tiles, chunks = frames // TILE, hidden // WIDTH
     first_b, first_c = 1 + chunks, 1 + 2 * chunks
     place = lambda i: jnp.where(
         i < first_b, jnp.maximum(i - 1, 0), jnp.minimum(i - first_b, chunks - 1)
@@ -2050,7 +2274,7 @@
         pltpu.VMEM((frames, channels), BF16),
         pltpu.VMEM((frames, hidden), BF16),
         pltpu.VMEM((8, 8, channels), F32),
-        pltpu.VMEM((2 * chunks, CHUNK), F32),
+        pltpu.VMEM((16, CHUNK), F32),
     ]
     if fused:
         own = [4, 2, 2, 1]
@@ -2066,14 +2290,14 @@
     else:
         shapes += [
             jax.ShapeDtypeStruct((8, channels), F32),
-            jax.ShapeDtypeStruct((2 * chunks, CHUNK), F32),
+            jax.ShapeDtypeStruct((16, CHUNK), F32),
             jax.ShapeDtypeStruct((channels // PIECE, 4, PIECE, WIDTH), BF16),
             jax.ShapeDtypeStruct((channels // PIECE, 4, PIECE, WIDTH), BF16),
         ]
     return pl.pallas_call(
         partial(tail_kernel, mesh_size),
         grid=(first_c + tiles,),
-        in_specs=[whole(x.shape), pl.BlockSpec((frames, CHUNK), lambda i: (0, place(i)))]
+        in_specs=[whole(x.shape), pl.BlockSpec((frames, WIDTH), lambda i: (0, place(i)))]
         + [whole(a.shape) for a in (gx1, up, down, table) + tuple(others)]
         + [pl.BlockSpec(memory_space=pltpu.HBM)] * len(grads),
         out_specs=[
@@ -2090,7 +2314,8 @@
 def unpack_kernel(
     place_ref,
     second_ref,
-    mixer_ref,
+    middle_ref,
+    mixin_ref,
     down_ref,
     left_ref,
     right_ref,
@@ -2119,11 +2344,11 @@
         down_out[0, rows, :] = down_ref[k]
         down_out[1, rows, :] = second_ref[5 + k]
     convout_out[...] = second_ref[0]
-    mixout_out[...] = mixer_ref[2]
+    mixout_out[...] = middle_ref[0]
     for k in range(2):
         cols = slice(k * WIDTH, k * WIDTH + WIDTH)
-        mixin_out[:, cols] = mixer_ref[k]
-        convin_out[:, cols] = mixer_ref[3 + k]
+        mixin_out[:, cols] = mixin_ref[k]
+        convin_out[:, cols] = middle_ref[1 + k]
     count = bias_out.shape[1]
     row = (mine * count) // CHUNK
     inner = mine * count - row * CHUNK
@@ -2241,25 +2466,19 @@
         ]
         weights = [ffn_up, ffn_down, mix_in, mix_out, conv_in, conv_out]
         made = front(size, seq_offsets, seq_counts, frames, small, weights, hidden, 1)
-        h0, x1, u, v, y, gated, x2, p, hold, w, stat, table, bias, decay, coupling = made[:15]
+        h0, x1, v, y, gated, x2, p, u, w, stat, table, bias, *mixing = made[:17]
         groups = lambda g: g.reshape((devices,) + g.shape[-3:])
         places = lambda g: g.reshape(block_layout(n_dp, n_fs) + g.shape[1:])
-        first, second, third, fourth = [groups(g) for g in made[15:]]
+        first, second, third, fourth = [groups(g) for g in made[17:]]
         result, gx3, gnb, grads, gbias1, gvec1, stat = middle(
             size, x2, w, cotangent, fourth, bias, table, stat, hidden, 2
         )
-        gx1, grads2, gvec2, gtaps, gmap, gdecay, reduced = back(
+        gx1, grads2, gvec2, gtaps, gmap, gdecay, reduced, reduced2 = back(
             size,
             seq_offsets,
             seq_counts,
-            [w, gnb, p],
-            [x2, gx3, gated, y, v, u, x1],
-            hold,
-            third,
-            table,
-            stat,
-            decay,
-            coupling,
+            [w, gnb, p, x2, gx3, gated, y, v, x1],
+            [u] + mixing + [third, table, stat],
             (places(grads),),
             3,
         )
@@ -2267,7 +2486,7 @@
         gx, last, *late = tail(
             size, frames, h0, gx1, first, second, table, others, (places(grads2),), 4
         )
-        made = unpack(mine.reshape((1,)), [reduced] + late + [last], hidden)
+        made = unpack(mine.reshape((1,)), [reduced, reduced2] + late + [last], hidden)
         made = list(made)
         made[7] = made[7].reshape((-1,))
         made[8] = made[8].T
@@ -2298,14 +2517,14 @@
     cut = lambda g: g.reshape((group_count, PIECE, -1, WIDTH)).transpose((0, 2, 1, 3))
     tall = lambda g: g.reshape((group_count, -1, PIECE, WIDTH))
     join = lambda g: g.transpose((0, 2, 1, 3)).reshape((channels, -1))
-    blank = jnp.zeros((group_count, 1, PIECE, WIDTH), BF16)
+    blank = jnp.pad(matrix(got[0]), ((0, 0), (0, WIDTH - 256))).reshape((group_count, 1, PIECE, WIDTH))
     first = jnp.concatenate([blank, cut(up0)], axis=1)
     third = jnp.concatenate([cut(mixin), cut(mixout), cut(convin)], axis=1)
     fourth = jnp.concatenate([cut(convout), cut(up1), tall(down1)], axis=1)
     made = front(
         None, seq_offsets, seq_counts, frames, [table, bias], [first, tall(down0), third], hidden
     )
-    h0, x1, u, v, y, gated, x2, p, hold, w, stat, table, bias, decay, coupling = made
+    h0, x1, v, y, gated, x2, p, u, w, stat, table, bias, *mixing = made
     pool = exchange(n_dp, n_fs, stat, frames_dev, 2, pool_kernel)
     scale = lax.rsqrt(pool[1:2] / (frames_dev * devices) + EPSILON)
     stat = jnp.concatenate([pool[0:1], scale, jnp.zeros((6, channels), F32)])
@@ -2315,18 +2534,12 @@
     sums = exchange(n_dp, n_fs, gvec1, 1, 4, total_kernel)[6:8]
     sums = sums * (table[5:6] / (frames_dev * devices))
     stat = jnp.concatenate([stat[0:2], sums[1:2], sums[0:1], stat[4:8]])
-    gx1, grads2, gvec2, gtaps, gmap, gdecay = back(
+    gx1, grads2, gvec2, gtaps, gmap, gdecay, grads3 = back(
         None,
         seq_offsets,
         seq_counts,
-        [w, gnb, p],
-        [x2, gx3, gated, y, v, u, x1],
-        hold,
-        third,
-        table,
-        stat,
-        decay,
-        coupling,
+        [w, gnb, p, x2, gx3, gated, y, v, x1],
+        [u] + mixing + [third, table, stat],
     )
     gx, gvec3, gbias0, gup0, gdown0 = tail(None, frames, h0, gx1, first, tall(down0), table)
 
@@ -2352,8 +2565,8 @@
             wide(join(grads[:, 1:5])),
             wide(matrix(grads[:, 5:9])),
             wide(join(grads[:, 0:1])),
-            wide(join(grads2[:, 3:5])),
-            wide(join(grads2[:, 2:3])),
+            wide(join(grads3[:, 1:3])),
+            wide(join(grads3[:, 0:1])),
             wide(join(grads2[:, 0:2])),
             wide(join(gup0)),
             wide(matrix(gdown0)),

time: 393 us -> 346 us (0.88)
  Pallas kernels: 387 us -> 340 us
    pallas_call x2, Pallas kernels: 237 us -> 213 us  [the longest x1 122 us: front(): pl.pallas_call(partial(front_kernel, mesh_size), grid=(2 * tiles + 2,), i...]
    pallas_call x1, Pallas kernels: 77.2 us -> 62.1 us  [tail(): pl.pallas_call(partial(tail_kernel, mesh_size), grid=(first_c + tiles,),...]
    pallas_call x1, Pallas kernels: 70.8 us -> 62.1 us  [middle(): pl.pallas_call(partial(middle_kernel, mesh_size), grid=(tiles,), in_specs...]
where the time goes in v4:
time: 346 us; the launch traced here: 345 us
  Pallas kernels  340 us (98%)
  local copies, waits for them, and re-layouts  4.32 us (1%)
    pallas_call x1, Pallas kernels, front(): pl.pallas_call(partial(front_kernel, mesh_size), grid=(2 * tiles + 2,), i...  122 us
    pallas_call x1, Pallas kernels, back(): pl.pallas_call(partial(back_kernel, mesh_size), grid=(3 * tiles + 2,), in...  91.2 us
    pallas_call x1, Pallas kernels, middle(): pl.pallas_call(partial(middle_kernel, mesh_size), grid=(tiles,), in_specs...  62.1 us
    pallas_call x1, Pallas kernels, tail(): pl.pallas_call(partial(tail_kernel, mesh_size), grid=(first_c + tiles,),...  62.1 us

profile of v4, /device:TPU:0, one launch (start us, length us, event | category | flops | bytes accessed | tf_op | source)
XLA Modules:
  0.0 345.5 jit_solution(8760790492522268336)
XLA Ops:
  1.3 122.3 %front.1 = (bf16[1536,2048]{1,0:T(8,128)(2,1)}, f32[1536,512]{1,0:T(8,128)}, bf16[1536,512]{1,0:T(8,128)(2,1)}, bf16[1536,512]{1,0:T(8,128)(2,1)}, bf16[1536,512...) custom-call(s32[1,3]{1,0:T(1,128)} %refs_0_.4, ...), custom_call_target="tpu_custom_call" | custom-call | tf_op jit(solution)/shard_map/front/pallas_call | solution.py:1543
  123.6 62.1 %middle.1 = (bf16[1536,512]{1,0:T(8,128)(2,1)}, f32[1536,512]{1,0:T(8,128)}, f32[1536,512]{1,0:T(8,128)}, bf16[32,9,16,512]{3,2,1,0:T(8,128)(2,1)}, f32[8,2048]{...) custom-call(f32[1536,512]{1,0:T(8,128)} %get-tuple-element.71.x2_ref.refs_5_, ...), custom_call_target="tpu_custom_call" | custom-call | tf_op jit(solution)/shard_map/middle/pallas_call | solution.py:1730
  185.7 91.2 %back.1 = (f32[1536,512]{1,0:T(8,128)}, bf16[32,2,16,512]{3,2,1,0:T(8,128)(2,1)}, f32[8,512]{1,0:T(8,128)}, f32[16,512]{1,0:T(8,128)}, f32[32,512]{1,0:T(8,128)}...) custom-call(s32[1,3]{1,0:T(1,128)} %refs_0_.4, s32[1]{0:T(128)S(6)} %copy.34.refs_1_, ...), custom_call_target="tpu_custom_call" | custom-call | tf_op jit(solution)/shard_map/back/pallas_call | solution.py:2044
  276.9 62.1 %tail.1 = (f32[1536,512]{1,0:T(8,128)}, f32[8,512]{1,0:T(8,128)}, f32[2,16,512]{2,1,0:T(8,128)}, f32[4,16,512]{2,1,0:T(8,128)}, f32[2,16,512]{2,1,0:T(8,128)}, /...) custom-call(bf16[1536,512]{1,0:T(8,128)(2,1)} %refs_0_.5, bf16[1536,2048]{1,0:T(8,128)(2,1)} %get-tuple-element.78.refs_1_, ...), custom_call_target="tpu_custom_call" | custom-call | tf_op jit(solution)/shard_map/tail/pallas_call | solution.py:2297
  339.0 0.0 copy-start
  339.0 2.2 unpack.1
  341.2 2.7 copy.35
  343.8 0.0 copy-done
  343.8 1.7 copy.36
Async XLA Ops:
  339.0 4.8 %copy-start = (f32[1536,512]{1,0:T(8,128)S(1)}, f32[1536,512]{1,0:T(8,128)}, u32[]{:S(2)}) copy-start(f32[1536,512]{1,0:T(8,128)} %get-tuple-element.143) | copy-start | bytes 9437188

commit v5 on v4

--- a/solution.py
+++ b/solution.py
@@ -1245,7 +1245,7 @@
         small_in = take(7)
         up_s, down_s, mixin_s, mixout_s, convin_s, convout_s = take(6)
     else:
-        first_v, second_v, third_v, table_in, bias_in = take(5)
+        first_v, extra_v, second_v, third_v, table_in, bias_in = take(6)
     (
         h_out,
         x1_out,
@@ -1265,8 +1265,8 @@
         shifted,
         weight,
     ) = take(17)
-    gathered = take(4) if fused else []
-    x1_scr, low_all, low_scr, sum_scr, y_all, padded = take(6)
+    gathered = take(5) if fused else []
+    x1_scr, low_all, low_scr, sum_scr, y_all, padded, act_all = take(7)
     mix_scr = take(6)
     step = pl.program_id(0)
     channels = x_ref.shape[1]
@@ -1277,18 +1277,19 @@
     shift = lambda k: table_ref[6 + k : 7 + k, :]
     here = lambda rows, tile: pl.ds(pl.multiple_of(tile * TILE + rows.start, ROWS), ROWS)
     flags = carries(offsets_ref, counts_ref, tiles)
+    mix_at, last_step = 3 * tiles, 4 * tiles + 1
     if fused:
-        first_c, second_c, third_c = take(3)
-        sources = take(4)
+        landing = take(4)
+        sources = take(5)
         turn_scr = refs.pop(0)
         sems = take(3)
         load_sem = refs.pop(0)
         swap = take(4)
         dp, fs = lax.axis_index("dp"), lax.axis_index("fsdp")
         place = Place(dp, fs, n_dp, n_fs)
-        landing = [first_c, second_c, third_c, gathered[3]]
+        landing.append(gathered[4])
         plans, sends = block_gather(place, sources, landing, *sems)
-        first_v, second_v, third_v = [flat_groups(r) for r in landing[:3]]
+        first_v, extra_v, second_v, third_v = [flat_groups(r) for r in landing[:4]]
 
         def keep_copy(chunk):
             return pltpu.make_async_copy(landing[chunk], gathered[chunk], load_sem.at[chunk])
@@ -1302,38 +1303,42 @@
             pack_small(sources[0].at[0], turn_scr, dp * n_fs + fs, *small_in)
             for k in range(4):
                 cols = slice(k * WIDTH, k * WIDTH + WIDTH)
-                sources[0][1 + k] = up_s[0, :, cols]
-                sources[3][1 + k] = up_s[1, :, cols]
+                if k < 2:
+                    sources[0][1 + k] = up_s[0, :, cols]
+                else:
+                    sources[1][k - 2] = up_s[0, :, cols]
+                sources[4][1 + k] = up_s[1, :, cols]
                 rows = slice(k * PIECE, k * PIECE + PIECE)
-                sources[1][k] = down_s[0, rows, :]
-                sources[3][5 + k] = down_s[1, rows, :]
+                sources[2][k] = down_s[0, rows, :]
+                sources[4][5 + k] = down_s[1, rows, :]
             for k in range(2):
                 cols = slice(k * WIDTH, k * WIDTH + WIDTH)
-                sources[2][k] = mixin_s[:, cols]
-                sources[2][3 + k] = convin_s[:, cols]
-            sources[2][2] = mixout_s[...]
-            sources[3][0] = convout_s[...]
+                sources[3][k] = mixin_s[:, cols]
+                sources[3][3 + k] = convin_s[:, cols]
+            sources[3][2] = mixout_s[...]
+            sources[4][0] = convout_s[...]
             greet(dp, fs, n_dp, n_fs)
-            run((0, 0), (1, 0), (0, 1), (1, 1), (2, 0), (0, 2), (1, 2), (0, 3), (2, 1), (1, 3), (0, 4))
+            run((0, 0), (1, 0), (0, 1), (2, 0), (1, 1), (0, 2), (1, 2), (0, 3), (2, 1), (0, 4))
             table_ref[...] = first_v[:, 0, :, :CHUNK].reshape((channels, CHUNK)).astype(F32).T[:TABLE, :]
             total = first_v[0, 0, :, CHUNK:].astype(F32)
             for k in range(1, n_dp * n_fs):
                 total = total + first_v[k, 0, :, CHUNK:].astype(F32)
             bias_ref[...] = total
-            run((1, 4))
-
-        rest = {1: [(2, 2), (3, 0)], 2: [(2, 3)], tiles: [(2, 4), (3, 1)]}
-        rest.update({tiles + 1: [(3, 2)], tiles + 2: [(3, 3)], 2 * tiles + 1: [(3, 4)]})
+
+        rest = {1: [(1, 3), (3, 0)], 2: [(2, 2)], tiles: [(1, 4), (4, 0)], tiles + 1: [(2, 3), (3, 1)]}
+        rest.update({2 * tiles: [(2, 4), (3, 2)], 2 * tiles + 1: [(3, 3)]})
+        rest.update({mix_at: [(3, 4), (4, 1)], mix_at + 1: [(4, 2)], mix_at + 2: [(4, 3)]})
+        rest[last_step] = [(4, 4)]
         for at, stages in rest.items():
 
             @pl.when(step == at)
             def _(at=at, stages=stages):
                 run(*stages)
-                if at == tiles:
-                    for chunk in range(3):
+                if at == mix_at:
+                    for chunk in range(4):
                         keep_copy(chunk).start()
-                if at == 2 * tiles + 1:
-                    for chunk in range(3):
+                if at == last_step:
+                    for chunk in range(4):
                         keep_copy(chunk).wait()
                     for wait in sends:
                         wait()
@@ -1349,31 +1354,43 @@
     def _():
         def first(rows):
             e, _ = norm_parts(x_ref[rows, :].astype(F32))
-            low_scr[rows, :] = (e * gain(0) + shift(0)).astype(BF16)
-            sum_scr[rows, :] = jnp.zeros((ROWS, channels), F32)
+            low_all[here(rows, step), :] = (e * gain(0) + shift(0)).astype(BF16)
 
         by_rows(first)
 
-        def hidden(c, _):
-            cols = columns(c, WIDTH)
-            h = dot_nn(low_scr[...], square_of(first_v, 1 + c)) + bias_of(bias_ref, 0, c)
-            h_out[:, cols] = h.astype(BF16)
-            active = (h * sigmoid(h)).astype(BF16)
-            sum_scr[...] += dot_nn(active, rows_of(second_v, 0, c))
-            return 0
-
-        lax.fori_loop(0, h_out.shape[1] // WIDTH, hidden, 0)
+    for half, part in enumerate((first_v, extra_v)):
+
+        @pl.when((step >= half * tiles) & (step < half * tiles + tiles))
+        def _(half=half, part=part):
+            tile_rows = pl.ds(pl.multiple_of((step - half * tiles) * TILE, TILE), TILE)
+            for k in range(2):
+                c = 2 * half + k
+                h = dot_nn(low_all[tile_rows, :], square_of(part, 1 - half + k))
+                h = h + bias_of(bias_ref, 0, c)
+                h_out[:, k * WIDTH : k * WIDTH + WIDTH] = h.astype(BF16)
+                active = (h * sigmoid(h)).astype(BF16)
+                act_all[tile_rows, c * WIDTH : c * WIDTH + WIDTH] = active
+
+    @pl.when((step >= 2 * tiles) & (step < mix_at))
+    def _():
+        at = step - 2 * tiles
+        tile_rows = pl.ds(pl.multiple_of(at * TILE, TILE), TILE)
+        total = dot_nn(act_all[tile_rows, :WIDTH], rows_of(second_v, 0, 0))
+        for c in range(1, 4):
+            cols = slice(c * WIDTH, c * WIDTH + WIDTH)
+            total = total + dot_nn(act_all[tile_rows, cols], rows_of(second_v, 0, c))
+        sum_scr[...] = total
 
         def second(rows):
             x1 = x_ref[rows, :].astype(F32) + 0.5 * (sum_scr[rows, :] + shift(6))
             x1_out[rows, :] = x1
-            x1_scr[here(rows, step), :] = x1
+            x1_scr[here(rows, at), :] = x1
             e, _ = norm_parts(x1)
-            low_all[here(rows, step), :] = (e * gain(1) + shift(1)).astype(BF16)
+            low_all[here(rows, at), :] = (e * gain(1) + shift(1)).astype(BF16)
 
         by_rows(second)
 
-    @pl.when(step == tiles)
+    @pl.when(step == mix_at)
     def _():
         prepare_states(first_v[:, 0, :, :CHUNK], power, shifted, weight)
 
@@ -1387,9 +1404,9 @@
         lax.fori_loop(0, tiles, project, 0)
         mix_forward(u_out, y_all, power, shifted, weight, flags, ub_out, state_out, *mix_scr)
 
-    @pl.when((step > tiles) & (step <= 2 * tiles))
+    @pl.when((step > mix_at) & (step < last_step))
     def _():
-        at = step - tiles - 1
+        at = step - mix_at - 1
         whole_tile = pl.ds(pl.multiple_of(at * TILE, TILE), TILE)
         v_out[...] = dot_nn(low_all[whole_tile, :], square_of(third_v, 1)).astype(BF16)
 
@@ -1427,7 +1444,7 @@
 
         lax.fori_loop(0, channels // CHUNK, widen, 0)
 
-    @pl.when(step == 2 * tiles + 1)
+    @pl.when(step == last_step)
     def _():
         fill_halo(padded, flags, tiles)
 
@@ -1488,8 +1505,10 @@
     fused = mesh_size is not None
     frames, channels = x.shape
     tiles = frames // TILE
-    early = lambda width: pl.BlockSpec((TILE, width), lambda i: (jnp.minimum(i, tiles - 1), 0))
-    place = lambda i: jnp.clip(i - tiles - 1, 0, tiles - 1)
+    clip = lambda i, first: jnp.clip(i - first, 0, tiles - 1)
+    twice = lambda i: (jnp.where(i < tiles, i, jnp.where(i < 2 * tiles, tiles - 1, clip(i, 2 * tiles))), 0)
+    halves = lambda i: (jnp.where(i < tiles, i, clip(i, tiles)), jnp.where(i < tiles, 0, 1))
+    place = lambda i: clip(i, 3 * tiles + 1)
     late = lambda width: pl.BlockSpec((TILE, width), lambda i: (place(i), 0))
     shape = lambda width, kind: jax.ShapeDtypeStruct((frames, width), kind)
     groups, blocks = channels // PIECE, frames // STRETCH
@@ -1512,7 +1531,11 @@
         jax.ShapeDtypeStruct((STRETCH, groups, STRETCH * PIECE), F32),
         jax.ShapeDtypeStruct((groups, SPREAD), F32),
     ]
-    out_specs = [early(hidden), early(channels)] + [late(channels)] * 4 + [late(2 * channels)]
+    out_specs = [
+        pl.BlockSpec((TILE, hidden // 2), halves),
+        pl.BlockSpec((TILE, channels), lambda i: (clip(i, 2 * tiles), 0)),
+    ]
+    out_specs += [late(channels)] * 4 + [late(2 * channels)]
     out_specs += [whole(s.shape) for s in out_shape[7:]]
     scratch = [
         pltpu.VMEM((frames, channels), F32),
@@ -1521,6 +1544,7 @@
         pltpu.VMEM((TILE, channels), F32),
         pltpu.VMEM((channels // 128, frames, 128), F32),
         pltpu.VMEM((channels // 128, tiles * (TILE + 2 * REACH), 128), F32),
+        pltpu.VMEM((frames, hidden), BF16),
         pltpu.VMEM((8, blocks, STRETCH * PIECE), BF16),
         pltpu.VMEM((8, blocks, STRETCH * PIECE), F32),
         pltpu.VMEM((TOGETHER, STRETCH * PIECE, SPREAD), BF16),
@@ -1531,19 +1555,19 @@
     operands = (weights if not fused else small + weights) + (small if not fused else [])
     if fused:
         layout = block_layout(*mesh_size)
-        blocks = (5, 4, 5, 9)
+        blocks = (3, 2, 4, 5, 9)
         chunks = [jax.ShapeDtypeStruct(layout + (k, PIECE, WIDTH), BF16) for k in blocks]
         out_shape += chunks
         out_specs += [HBM_SPEC] * len(chunks)
-        scratch += [pltpu.VMEM(c.shape, BF16) for c in chunks[:3]]
+        scratch += [pltpu.VMEM(c.shape, BF16) for c in chunks[:4]]
         scratch += [pltpu.VMEM((k, PIECE, WIDTH), BF16) for k in blocks]
         scratch += [pltpu.VMEM((CHUNK, 128), F32)]
-        scratch += block_sems(*mesh_size, len(chunks)) + [pltpu.SemaphoreType.DMA((3,))]
+        scratch += block_sems(*mesh_size, len(chunks)) + [pltpu.SemaphoreType.DMA((4,))]
         scratch += swap_scratch(*mesh_size, channels)
     return pl.pallas_call(
         partial(front_kernel, mesh_size),
-        grid=(2 * tiles + 2,),
-        in_specs=[SMEM_SPEC, SMEM_SPEC, early(channels)] + [whole(a.shape) for a in operands],
+        grid=(4 * tiles + 2,),
+        in_specs=[SMEM_SPEC, SMEM_SPEC, pl.BlockSpec((TILE, channels), twice)] + [whole(a.shape) for a in operands],
         out_specs=out_specs,
         out_shape=out_shape,
         scratch_shapes=scratch,
@@ -2087,7 +2111,7 @@
     fused = mesh_size is not None
     refs = list(refs)
     take = lambda count: [refs.pop(0) for _ in range(count)]
-    x_ref, h_ref, gx1_ref, up_ref, down_ref, table_ref = take(6)
+    x_ref, h_ref, gx1_ref, up_ref, up2_ref, down_ref, table_ref = take(7)
     hidden = 4 * WIDTH
     if fused:
         gvec1, gvec2, gtaps, gmap, gdecay, gbias1 = take(6)
@@ -2121,9 +2145,9 @@
             place, sources + [down_src, left_src, right_src, small_src], emit, scratch, *sems
         )
         begins = [
-            (0, 1, 2, 4, 6),
-            (first_b, first_b + 1, first_b + 2, first_b + 3, first_c),
-            (first_b + 2, first_b + 3, first_c, first_c + 1, first_c + 2),
+            (0, 2, 4, 6, 8),
+            (first_b, first_b + 2, first_c, first_c + 2, first_c + tiles),
+            (first_b + 2, first_b + 3, first_c + 1, first_c + 2, first_c + tiles),
             (first_c, first_c + 1, first_c + 2, first_c + tiles, first_c + tiles),
             (first_c, first_c + 1, first_c + 2, first_c + tiles, first_c + tiles),
         ]
@@ -2222,9 +2246,10 @@
         tile = step - first_c
         whole_tile = pl.ds(pl.multiple_of(tile * TILE, TILE), TILE)
         total = dot_nt(gh_scr[whole_tile, :WIDTH], square_of(up_ref, 1))
+        later = [square_of(up_ref, 2), square_of(up2_ref, 0), square_of(up2_ref, 1)]
         for k in range(1, hidden // WIDTH):
             cols = slice(k * WIDTH, k * WIDTH + WIDTH)
-            total = total + dot_nt(gh_scr[whole_tile, cols], square_of(up_ref, 1 + k))
+            total = total + dot_nt(gh_scr[whole_tile, cols], later[k - 1])
         gx_ref[...] = total
 
         def second(rows):
@@ -2259,7 +2284,7 @@
             gbias_out[...] = bias_scr[...]
 
 
-def tail(mesh_size, x, h, gx1, up, down, table, others=(), grads=(), collective_id=None):
+def tail(mesh_size, x, h, gx1, up, up2, down, table, others=(), grads=(), collective_id=None):
     fused = mesh_size is not None
     frames, channels = x.shape
     hidden = h.shape[1]
@@ -2298,7 +2323,7 @@
         partial(tail_kernel, mesh_size),
         grid=(first_c + tiles,),
         in_specs=[whole(x.shape), pl.BlockSpec((frames, WIDTH), lambda i: (0, place(i)))]
-        + [whole(a.shape) for a in (gx1, up, down, table) + tuple(others)]
+        + [whole(a.shape) for a in (gx1, up, up2, down, table) + tuple(others)]
         + [pl.BlockSpec(memory_space=pltpu.HBM)] * len(grads),
         out_specs=[
             pl.BlockSpec((TILE, channels), lambda i: (jnp.maximum(i - first_c, 0), 0))
@@ -2308,7 +2333,7 @@
         scratch_shapes=scratch,
         compiler_params=params(collective_id),
         name="tail",
-    )(x, h, gx1, up, down, table, *others, *grads)
+    )(x, h, gx1, up, up2, down, table, *others, *grads)
 
 
 def unpack_kernel(
@@ -2321,6 +2346,10 @@
     right_ref,
     small_ref,
     last_ref,
+    result_in,
+    grad_in,
+    result_out,
+    grad_out,
     up_out,
     down_out,
     bias_out,
@@ -2334,8 +2363,17 @@
     taps_out,
     gains_out,
     shifts_out,
+    sem,
 ):
     mine = place_ref[0]
+    copies = []
+    for at, (source, target) in enumerate(((result_in, result_out), (grad_in, grad_out))):
+        rows = source.shape[0] // 4
+        for k in range(4):
+            part = pl.ds(k * rows, rows)
+            copies.append(pltpu.make_async_copy(source.at[part], target.at[part], sem.at[at, k]))
+    for copy in copies:
+        copy.start()
     for k in range(4):
         cols = slice(k * WIDTH, k * WIDTH + WIDTH)
         rows = slice(k * PIECE, k * PIECE + PIECE)
@@ -2369,18 +2407,22 @@
     rate_out[...] = small[:, RATE:MAP_IN]
     map_out[0] = small[:, MAP_IN:MAP_OUT]
     map_out[1] = small[:, MAP_OUT:TABLE]
-
-
-def unpack(mine, arrays, hidden):
+    for copy in copies:
+        copy.wait()
+
+
+def unpack(mine, arrays, passed, hidden):
     channels = arrays[-1].shape[1]
     devices = channels // PIECE
     f32 = lambda *shape: jax.ShapeDtypeStruct(shape, F32)
     vmem = pl.BlockSpec(memory_space=pltpu.VMEM)
     return pl.pallas_call(
         unpack_kernel,
-        in_specs=[SMEM_SPEC] + [vmem] * len(arrays),
-        out_specs=[vmem] * 13,
-        out_shape=[
+        in_specs=[SMEM_SPEC] + [vmem] * len(arrays) + [HBM_SPEC] * 2,
+        out_specs=[HBM_SPEC] * 2 + [vmem] * 13,
+        scratch_shapes=[pltpu.SemaphoreType.DMA((2, 4))],
+        out_shape=[jax.ShapeDtypeStruct(a.shape, a.dtype) for a in passed]
+        + [
             f32(2, PIECE, hidden),
             f32(2, hidden // devices, channels),
             f32(2, hidden // devices),
@@ -2396,7 +2438,7 @@
             f32(12, PIECE),
         ],
         name="unpack",
-    )(mine, *arrays)
+    )(mine, *arrays, *passed)
 
 
 def pack_table(gains, shifts, conv_bias, taps, rate, maps):
@@ -2469,7 +2511,7 @@
         h0, x1, v, y, gated, x2, p, u, w, stat, table, bias, *mixing = made[:17]
         groups = lambda g: g.reshape((devices,) + g.shape[-3:])
         places = lambda g: g.reshape(block_layout(n_dp, n_fs) + g.shape[1:])
-        first, second, third, fourth = [groups(g) for g in made[17:]]
+        first, extra, second, third, fourth = [groups(g) for g in made[17:]]
         result, gx3, gnb, grads, gbias1, gvec1, stat = middle(
             size, x2, w, cotangent, fourth, bias, table, stat, hidden, 2
         )
@@ -2484,14 +2526,14 @@
         )
         others = (gvec1, gvec2, gtaps, gmap, gdecay, gbias1)
         gx, last, *late = tail(
-            size, frames, h0, gx1, first, second, table, others, (places(grads2),), 4
+            size, frames, h0, gx1, first, extra, second, table, others, (places(grads2),), 4
         )
-        made = unpack(mine.reshape((1,)), [reduced, reduced2] + late + [last], hidden)
+        made = unpack(mine.reshape((1,)), [reduced, reduced2] + late + [last], (result, gx), hidden)
         made = list(made)
-        made[7] = made[7].reshape((-1,))
-        made[8] = made[8].T
-        made[9] = made[9].transpose((0, 2, 1))
-        return (result, gx) + tuple(made)
+        made[9] = made[9].reshape((-1,))
+        made[10] = made[10].T
+        made[11] = made[11].transpose((0, 2, 1))
+        return tuple(made)
 
     small = pack_table(gains, shifts, conv_out_bias, conv_kernel, ssm_rate, ssm_map)
     got = gather_all(
@@ -2518,11 +2560,12 @@
     tall = lambda g: g.reshape((group_count, -1, PIECE, WIDTH))
     join = lambda g: g.transpose((0, 2, 1, 3)).reshape((channels, -1))
     blank = jnp.pad(matrix(got[0]), ((0, 0), (0, WIDTH - 256))).reshape((group_count, 1, PIECE, WIDTH))
-    first = jnp.concatenate([blank, cut(up0)], axis=1)
+    extra = cut(up0)
+    first, extra = jnp.concatenate([blank, extra[:, :2]], axis=1), extra[:, 2:]
     third = jnp.concatenate([cut(mixin), cut(mixout), cut(convin)], axis=1)
     fourth = jnp.concatenate([cut(convout), cut(up1), tall(down1)], axis=1)
     made = front(
-        None, seq_offsets, seq_counts, frames, [table, bias], [first, tall(down0), third], hidden
+        None, seq_offsets, seq_counts, frames, [table, bias], [first, extra, tall(down0), third], hidden
     )
     h0, x1, v, y, gated, x2, p, u, w, stat, table, bias, *mixing = made
     pool = exchange(n_dp, n_fs, stat, frames_dev, 2, pool_kernel)
@@ -2541,7 +2584,7 @@
         [w, gnb, p, x2, gx3, gated, y, v, x1],
         [u] + mixing + [third, table, stat],
     )
-    gx, gvec3, gbias0, gup0, gdown0 = tail(None, frames, h0, gx1, first, tall(down0), table)
+    gx, gvec3, gbias0, gup0, gdown0 = tail(None, frames, h0, gx1, first, extra, tall(down0), table)
 
     def weights_of(log_rate, maps):
         log_decay = -jnp.exp(log_rate)

time: 346 us -> 483 us (1.40)
  Pallas kernels: 340 us -> 481 us
    pallas_call x1, Pallas kernels: 2.16 us -> 146 us  [unpack(): pl.pallas_call(unpack_kernel, in_specs=[SMEM_SPEC] + [vmem] * len(arrays)...]
where the time goes in v5:
time: 483 us
  Pallas kernels  481 us (100%)
    pallas_call x1, Pallas kernels, unpack(): pl.pallas_call(unpack_kernel, in_specs=[SMEM_SPEC] + [vmem] * len(arrays)...  146 us
    pallas_call x1, Pallas kernels, front(): pl.pallas_call(partial(front_kernel, mesh_size), grid=(4 * tiles + 2,), i...  121 us
    pallas_call x1, Pallas kernels, back(): pl.pallas_call(partial(back_kernel, mesh_size), grid=(3 * tiles + 2,), in...  91.7 us
    pallas_call x1, Pallas kernels, middle(): pl.pallas_call(partial(middle_kernel, mesh_size), grid=(tiles,), in_specs...  62.1 us
    pallas_call x1, Pallas kernels, tail(): pl.pallas_call(partial(tail_kernel, mesh_size), grid=(first_c + tiles,),...  60.4 us

profile of v5, /device:TPU:0, one launch (start us, length us, event | category | flops | bytes accessed | tf_op | source)
XLA Modules:
  0.0 482.8 jit_solution(13992847340093128118)
XLA Ops:
  1.3 120.9 %front.1 = (bf16[1536,2048]{1,0:T(8,128)(2,1)}, f32[1536,512]{1,0:T(8,128)}, bf16[1536,512]{1,0:T(8,128)(2,1)}, bf16[1536,512]{1,0:T(8,128)(2,1)}, bf16[1536,512...) custom-call(s32[1,3]{1,0:T(1,128)} %refs_0_.4, ...), custom_call_target="tpu_custom_call" | custom-call | tf_op jit(solution)/shard_map/front/pallas_call | solution.py:1567
  122.2 62.1 %middle.1 = (bf16[1536,512]{1,0:T(8,128)(2,1)}, f32[1536,512]{1,0:T(8,128)}, f32[1536,512]{1,0:T(8,128)}, bf16[32,9,16,512]{3,2,1,0:T(8,128)(2,1)}, f32[8,2048]{...) custom-call(f32[1536,512]{1,0:T(8,128)} %get-tuple-element.75.x2_ref.refs_5_, ...), custom_call_target="tpu_custom_call" | custom-call | tf_op jit(solution)/shard_map/middle/pallas_call | solution.py:1754
  184.3 91.7 %back.1 = (f32[1536,512]{1,0:T(8,128)}, bf16[32,2,16,512]{3,2,1,0:T(8,128)(2,1)}, f32[8,512]{1,0:T(8,128)}, f32[16,512]{1,0:T(8,128)}, f32[32,512]{1,0:T(8,128)}...) custom-call(s32[1,3]{1,0:T(1,128)} %refs_0_.4, s32[1]{0:T(128)S(6)} %copy.32.refs_1_, ...), custom_call_target="tpu_custom_call" | custom-call | tf_op jit(solution)/shard_map/back/pallas_call | solution.py:2068
  276.0 60.4 %tail.1 = (f32[1536,512]{1,0:T(8,128)}, f32[8,512]{1,0:T(8,128)}, f32[2,16,512]{2,1,0:T(8,128)}, f32[4,16,512]{2,1,0:T(8,128)}, f32[2,16,512]{2,1,0:T(8,128)}, /...) custom-call(bf16[1536,512]{1,0:T(8,128)(2,1)} %refs_0_.5, bf16[1536,2048]{1,0:T(8,128)(2,1)} %get-tuple-element.98.refs_1_, ...), custom_call_target="tpu_custom_call" | custom-call | tf_op jit(solution)/shard_map/tail/pallas_call | solution.py:2322
  336.4 146.1 %unpack.1 = (bf16[1536,512]{1,0:T(8,128)(2,1)}, f32[1536,512]{1,0:T(8,128)}, f32[2,16,2048]{2,1,0:T(8,128)}, f32[2,64,512]{2,1,0:T(8,128)}, f32[2,64]{1,0:T(2,12...) custom-call(s32[1]{0:T(128)} %bitcast.place_ref, ...), custom_call_target="tpu_custom_call" | custom-call | tf_op jit(solution)/shard_map/unpack/pallas_call | solution.py:2419
